TPU v7x, 32 devices: a whole 2x2x4 slice. The times are simulated.
32 devices in a mesh: section: 4 (over y, x), dp: 8 (over z, core).
Axes of the slice: x: 2, y: 2, z: 4, core: 2. Of those that a mesh axis runs over, the one named last changes fastest.
Arguments:
- visible: bfloat16 [32, 49, 768], P(('section', 'dp')), may hold values from -6 to 6
- cotangent: bfloat16 [32, 196, 512], P(('section', 'dp')), may hold values from -6 to 6
- keep_index: int32 [32, 49], P(('section', 'dp')), may hold values from 0 to 195, as said below
- positions: float32 [196, 512], replicated, may hold values from -1 to 1
- enc_qkv: float32 [768, 2304], P('dp', 'section'), may hold values from -0.21875 to 0.21875
- enc_out: float32 [768, 768], P('dp', 'section'), may hold values from -0.4375 to 0.4375
- enc_up: float32 [768, 3072], P('dp', 'section'), may hold values from -0.21875 to 0.21875
- enc_down: float32 [3072, 768], P('dp', 'section'), may hold values from -0.109375 to 0.109375
- dec_embed: float32 [768, 512], P('dp', 'section'), may hold values from -0.21875 to 0.21875
- dec_qkv: float32 [512, 1536], P('dp', 'section'), may hold values from -0.25 to 0.25
- dec_out: float32 [512, 512], P('dp', 'section'), may hold values from -0.75 to 0.75
- dec_up: float32 [512, 2048], P('dp', 'section'), may hold values from -0.25 to 0.25
- dec_down: float32 [2048, 512], P('dp', 'section'), may hold values from -0.125 to 0.125
- enc_gains: float32 [2, 768], P(None, ('section', 'dp')), may hold values from 0.5 to 1.5
- enc_biases: float32 [6, 768], P(None, ('section', 'dp')), may hold values from -1.2 to 1.2
- enc_up_bias: float32 [3072], P(('section', 'dp')), may hold values from -1.2 to 1.2
- dec_gains: float32 [2, 512], P(None, ('section', 'dp')), may hold values from 0.5 to 1.5
- dec_biases: float32 [8, 512], P(None, ('section', 'dp')), may hold values from -1.2 to 1.2
- dec_up_bias: float32 [2048], P(('section', 'dp')), may hold values from -1.2 to 1.2
Outputs:
- block_out: float32 [32, 196, 512], P(('section', 'dp'))
- input_grad: float32 [32, 49, 768], P(('section', 'dp'))
- grad_enc_qkv: float32 [768, 2304], P('dp', 'section')
- grad_enc_out: float32 [768, 768], P('dp', 'section')
- grad_enc_up: float32 [768, 3072], P('dp', 'section')
- grad_enc_down: float32 [3072, 768], P('dp', 'section')
- grad_dec_embed: float32 [768, 512], P('dp', 'section')
- grad_dec_qkv: float32 [512, 1536], P('dp', 'section')
- grad_dec_out: float32 [512, 512], P('dp', 'section')
- grad_dec_up: float32 [512, 2048], P('dp', 'section')
- grad_dec_down: float32 [2048, 512], P('dp', 'section')
- grad_enc_gains: float32 [2, 768], P(None, ('section', 'dp'))
- grad_enc_biases: float32 [6, 768], P(None, ('section', 'dp'))
- grad_enc_up_bias: float32 [3072], P(('section', 'dp'))
- grad_dec_gains: float32 [2, 512], P(None, ('section', 'dp'))
- grad_dec_biases: float32 [8, 512], P(None, ('section', 'dp'))
- grad_dec_up_bias: float32 [2048], P(('section', 'dp'))
Inputs may be any that keep to these rules, and one draw needn't show every extreme that they name: Each row of keep_index holds 49 different patch positions of the 196 of an image.
All inputs are finite; a program needn't handle non-finite values.
Results may differ from a plain program's by a relative error of at most 0.02.
Values may be sent and summed in bfloat16 or wider, within the bound.
No kernel may reach another device: no remote copies, remote signals or barrier semaphores. Data moves between devices by JAX's collectives and lax.ppermute only.
A program may use at most 576 MiB of HBM per device.

v0:
```python
from functools import partial

import jax
import jax.numpy as jnp
from jax import lax
from jax.experimental import pallas as pl
from jax.experimental.pallas import tpu as pltpu
from jax.sharding import PartitionSpec as P

HE = 12
HD = 16
EPS = 1e-06
SEC = 4
ROWB = 8
BLOCKS = SEC * ROWB
ENC_ROWS = 64
DEC_ROWS = 208
BF = jnp.bfloat16
F32 = jnp.float32
IN_PATH, IN_PLAIN, OUT_PATH, OUT_Z, SECTION = 0, BLOCKS, 2 * BLOCKS, 3 * BLOCKS, 3 * BLOCKS + ROWB
VMEM_BYTES = 60 * 1024 * 1024


def dot(left, right):
    return jnp.dot(left, right, preferred_element_type=F32)


def dot_nt(left, right):
    return lax.dot_general(left, right, (((1,), (1,)), ((), ())), preferred_element_type=F32)


def dot_tn(left, right):
    return lax.dot_general(left, right, (((0,), (0,)), ((), ())), preferred_element_type=F32)


def norm_stats(values):
    centred = values - jnp.mean(values, axis=-1, keepdims=True)
    scale = lax.rsqrt(jnp.mean(centred * centred, axis=-1, keepdims=True) + EPS)
    return centred * scale, scale


def norm_back(grad, normed, scale, gain):
    inner = grad * gain
    mean_inner = jnp.mean(inner, axis=-1, keepdims=True)
    mean_cross = jnp.mean(inner * normed, axis=-1, keepdims=True)
    return scale * (inner - mean_inner - normed * mean_cross)


def column_sum(values):
    return jnp.sum(values, axis=0, keepdims=True)


def gelu_parts(values):
    share = 0.5 * (1.0 + lax.erf(values * (0.5**0.5)))
    return values * share, share


def gelu_slope(values, share):
    return share + values * (jnp.exp(-0.5 * values * values) * 0.3989422804014327)


def head_masks(width, size, dtype):
    lane = lax.broadcasted_iota(jnp.int32, (1, width), 1)
    return [
        jnp.where((lane >= h * size) & (lane < (h + 1) * size), 1.0, 0.0).astype(dtype)
        for h in range(width // size)
    ]


def stack_heads(window, size):
    return jnp.concatenate([window * m for m in head_masks(window.shape[1], size, window.dtype)], axis=0)


def unstack_heads(stacked, size):
    masks = head_masks(stacked.shape[1], size, stacked.dtype)
    rows = stacked.shape[0] // len(masks)
    total = stacked[:rows] * masks[0]
    for h in range(1, len(masks)):
        total = total + stacked[h * rows : (h + 1) * rows] * masks[h]
    return total


def softmax_rows(queries, keys, valid, size):
    scores = dot_nt(queries, keys) * size**-0.5
    lane = lax.broadcasted_iota(jnp.int32, (1, scores.shape[1]), 1)
    scores = jnp.where(lane < valid, scores, -1e30)
    powers = jnp.exp(scores - jnp.max(scores, axis=-1, keepdims=True))
    return powers / jnp.sum(powers, axis=-1, keepdims=True)


def attention_fwd(packed, width, size, valid, keep_probs):
    parts = []
    for w in range(width // 256):
        lanes = slice(256 * w, 256 * w + 256)
        queries = stack_heads(packed[:, lanes], size)
        keys = packed[:, width + 256 * w : width + 256 * w + 256]
        values = packed[:, 2 * width + 256 * w : 2 * width + 256 * w + 256]
        probs = softmax_rows(queries, keys, valid, size)
        if keep_probs is not None:
            keep_probs[w] = probs
        parts.append(unstack_heads(dot(probs.astype(BF), values), size))
    return jnp.concatenate(parts, axis=1).astype(BF)


def attention_bwd(packed, grad_mixed, width, size, valid, kept_probs):
    grad_q, grad_k, grad_v = [], [], []
    for w in range(width // 256):
        queries = stack_heads(packed[:, 256 * w : 256 * w + 256], size)
        keys = packed[:, width + 256 * w : width + 256 * w + 256]
        values = packed[:, 2 * width + 256 * w : 2 * width + 256 * w + 256]
        grads = stack_heads(grad_mixed[:, 256 * w : 256 * w + 256], size)
        probs = softmax_rows(queries, keys, valid, size) if kept_probs is None else kept_probs[w]
        grad_probs = dot_nt(grads, values)
        centre = jnp.sum(probs * grad_probs, axis=-1, keepdims=True)
        grad_scores = (probs * (grad_probs - centre)).astype(BF)
        grad_q.append(unstack_heads(dot(grad_scores, keys), size) * size**-0.5)
        grad_k.append(dot_tn(grad_scores, queries) * size**-0.5)
        grad_v.append(dot_tn(probs.astype(BF), grads))
    return jnp.concatenate(grad_q + grad_k + grad_v, axis=1).astype(BF)


def block_copies(pieces, table, first, rows, lanes, place, sem, store=False):
    copies = []
    number = first
    for piece in pieces:
        for i in range(piece.shape[0]):
            outer = piece.at[i, pl.ds(*rows), pl.ds(*lanes)]
            inner = place(table[number])
            source, target = (inner, outer) if store else (outer, inner)
            copies.append(pltpu.make_async_copy(source, target, sem))
            number += 1
    for copy in copies:
        copy.start()
    return copies


def wait_all(copies):
    for copy in copies:
        copy.wait()


def rows_place(scratch, rows):
    def place(block):
        return scratch.at[block // ROWB, pl.ds(pl.multiple_of((block % ROWB) * rows, rows), rows), :]

    return place


def turned_place(scratch, rows, columns, first, count):
    def place(block):
        top = pl.multiple_of((block // ROWB) * rows + first, count)
        return scratch.at[pl.ds(top, count), pl.ds(pl.multiple_of((block % ROWB) * columns, columns), columns)]

    return place


def part_place(scratch, first, count):
    def place(block):
        top = pl.multiple_of((block % ROWB) * 96 + first, 32)
        return scratch.at[block // ROWB, pl.ds(top, count), :]

    return place


def take(refs, sizes):
    groups = []
    for count, _ in sizes:
        groups.append(refs[:count])
        refs = refs[count:]
    return groups, refs


def padded(values, rows):
    short = rows - values.shape[0]
    return jnp.concatenate([values, jnp.zeros((short, values.shape[1]), values.dtype)], axis=0)


def row_mask(rows, valid):
    return lax.broadcasted_iota(jnp.int32, (rows, 1), 0) < valid


def unpack_vectors(rows_ref, enc_ref, upe_ref, dec_ref, upd_ref):
    def joined(first, count, width):
        parts = [rows_ref[b, :count, first : first + width].astype(F32) for b in range(BLOCKS)]
        return jnp.concatenate(parts, axis=1)

    enc_ref[...] = joined(0, 8, 24)
    upe_ref[...] = joined(128, 1, 96)
    upd_ref[...] = joined(128, 2, 64)[1:]
    dec_ref[...] = jnp.concatenate([joined(256, 8, 16), joined(384, 2, 16)], axis=0)


def enc_att_fwd(inn, table, x_ref, *refs):
    (pieces,), (h_ref, a_ref, k_ref, z_ref, *rest) = take(refs, inn)
    if len(rest) == 3:
        vec_ref, w_ref, sem = rest
        copies = block_copies(pieces, table, inn[0][1], (0, 96), (0, 768), rows_place(w_ref, 96), sem)
    else:
        vec_ref, upe_ref, dec_ref, upd_ref, w_ref, rows_ref, sem, sem_v = rest
        first = block_copies(pieces, table, inn[0][1], (96, 16), (0, 512), lambda block: rows_ref.at[block], sem_v)
        copies = block_copies(pieces, table, inn[0][1], (0, 96), (0, 768), rows_place(w_ref, 96), sem)
        wait_all(first)
        unpack_vectors(rows_ref, vec_ref, upe_ref, dec_ref, upd_ref)
    inputs = padded(x_ref[0].astype(F32), ENC_ROWS)
    normed, _ = norm_stats(inputs)
    low = (normed * vec_ref[0:1] + vec_ref[2:3]).astype(BF)
    a_ref[...] = low
    wait_all(copies)
    packed = jnp.concatenate([dot(low, w_ref[s, :, 0:640])[:, :576] for s in range(SEC)], axis=1)
    zero = jnp.zeros((1, 768), F32)
    packed = (packed + jnp.concatenate([vec_ref[3:4], zero, vec_ref[4:5]], axis=1)).astype(BF)
    k_ref[...] = packed
    mixed = attention_fwd(packed, 768, 64, 49, None)
    z_ref[...] = mixed
    result = jnp.concatenate([dot(mixed, w_ref[s, :, 512:768])[:, 64:] for s in range(SEC)], axis=1)
    h_ref[...] = (inputs + result + vec_ref[5:6]).astype(BF)


def enc_ffn_fwd(inn, table, h_ref, vec_ref, upb_ref, *refs):
    (ups, downs), (o_ref, a_ref, r_ref, u_ref, v_ref, sem_u, sem_v) = take(refs, inn)
    copies_u = block_copies(ups, table, inn[0][1], (0, 96), (0, 768), rows_place(u_ref, 96), sem_u)
    copies_v = []
    for half in range(2):
        copies_v += block_copies(
            downs, table, inn[1][1], (0, 96), (384 * half, 384), turned_place(v_ref, 192, 384, 96 * half, 96), sem_v
        )
    inputs = h_ref[...].astype(F32)
    normed, _ = norm_stats(inputs)
    low = (normed * vec_ref[1:2] + vec_ref[6:7]).astype(BF)
    a_ref[...] = low
    wait_all(copies_u)
    active = []
    for s in range(SEC):
        lanes = slice(768 * s, 768 * s + 768)
        hidden = dot(low, u_ref[s]) + upb_ref[:, lanes]
        r_ref[:, lanes] = hidden
        active.append(gelu_parts(hidden)[0].astype(BF))
    wait_all(copies_v)
    result = dot_nt(jnp.concatenate(active, axis=1), v_ref[...])
    o_ref[...] = (inputs + result + vec_ref[7:8]).astype(BF)


def placing(keep_ref):
    keep = jnp.concatenate([keep_ref[...], jnp.full((1, ENC_ROWS - 49), -1, jnp.int32)], axis=1)
    place = lax.broadcasted_iota(jnp.int32, (DEC_ROWS, ENC_ROWS), 0)
    return jnp.where(place == keep, 1.0, 0.0).astype(F32)


def dec_both(inn, outs, table, h_ref, keep_ref, pos_ref, ct_ref, vec_ref, upb_ref, *refs):
    (pieces,), (y_ref, dx_ref, gvec_ref, gupb_ref, *rest) = take(refs, inn)
    (grads,), rest = take(rest, (outs,))
    e_ref, w_ref, u_ref, v_ref, ge_ref, gw_ref, gu_ref, gv_ref, p_ref, sem_e, sem_w, sem_u, sem_v, sem_o = rest
    start = inn[0][1]
    copies_e = block_copies(pieces, table, start, (0, 64), (1536, 128), part_place(e_ref, 0, 64), sem_e)
    copies_e += block_copies(pieces, table, start, (0, 32), (1664, 128), part_place(e_ref, 64, 32), sem_e)
    copies_w = block_copies(pieces, table, start, (0, 64), (0, 512), rows_place(w_ref, 64), sem_w)
    copies_u = block_copies(pieces, table, start, (0, 64), (512, 512), rows_place(u_ref, 64), sem_u)
    copies_v = []
    for half in range(2):
        copies_v += block_copies(
            pieces, table, start, (0, 64), (1024 + 256 * half, 256), turned_place(v_ref, 128, 256, 64 * half, 64), sem_v
        )
    copies = []

    def give(lanes, place, rows=64):
        copies.extend(block_copies(grads, table, outs[1], (0, rows), lanes, place, sem_o, True))

    before = h_ref[...]
    onehot = placing(keep_ref)
    uncovered = 1.0 - jnp.sum(onehot, axis=1, keepdims=True)
    wait_all(copies_e)
    embedded = dot(before, jnp.concatenate([e_ref[s] for s in range(SEC)], axis=1)) + vec_ref[2:3]
    placed = jnp.dot(onehot, embedded, precision=lax.Precision.HIGHEST, preferred_element_type=F32)
    placed = placed + uncovered * vec_ref[3:4] + padded(pos_ref[...], DEC_ROWS)
    normed_a, scale_a = norm_stats(placed)
    low_a = (normed_a * vec_ref[0:1] + vec_ref[4:5]).astype(BF)
    wait_all(copies_w)
    packed = jnp.concatenate([dot(low_a, w_ref[s, :, 0:384]) for s in range(SEC)], axis=1)
    zero = jnp.zeros((1, 512), F32)
    packed = (packed + jnp.concatenate([vec_ref[5:6], zero, vec_ref[6:7]], axis=1)).astype(BF)
    mixed = attention_fwd(packed, 512, 32, 196, p_ref)
    w_out = jnp.concatenate([w_ref[s, :, 384:512] for s in range(SEC)], axis=1)
    inputs = (placed + dot(mixed, w_out) + vec_ref[7:8]).astype(BF).astype(F32)

    normed, scale = norm_stats(inputs)
    low = (normed * vec_ref[1:2] + vec_ref[8:9]).astype(BF)
    wait_all(copies_u)
    hidden, active = [], []
    for s in range(SEC):
        hidden.append(dot(low, u_ref[s]) + upb_ref[:, 512 * s : 512 * s + 512])
        active.append(gelu_parts(hidden[s])[0].astype(BF))
    active = jnp.concatenate(active, axis=1)
    wait_all(copies_v)
    result = inputs + dot_nt(active, v_ref[...]) + vec_ref[9:10]
    y_ref[0] = result[:196]

    grad_low = padded(ct_ref[0].astype(F32), DEC_ROWS).astype(BF)
    gv_ref[...] = dot_tn(grad_low, active).astype(BF)
    for half in range(2):
        give((512 + 256 * half, 256), turned_place(gv_ref, 128, 256, 64 * half, 64))
    grad_normed = jnp.zeros((DEC_ROWS, 512), F32)
    for s in range(SEC):
        lanes = slice(512 * s, 512 * s + 512)
        share = gelu_parts(hidden[s])[1]
        grad_hidden = (dot(grad_low, v_ref[:, lanes]) * gelu_slope(hidden[s], share)).astype(BF)
        gupb_ref[:, lanes] = column_sum(grad_hidden.astype(F32))
        gu_ref[s] = dot_tn(low, grad_hidden).astype(BF)
        grad_normed = grad_normed + dot_nt(grad_hidden, u_ref[s])
    give((0, 512), rows_place(gu_ref, 64))
    grad_out = grad_low.astype(F32)
    sums_f = [column_sum(grad_normed * normed), column_sum(grad_normed), column_sum(grad_out)]
    grad = (grad_out + norm_back(grad_normed, normed, scale, vec_ref[1:2])).astype(BF)

    grad_out = grad.astype(F32)
    for s in range(SEC):
        gw_ref[s, :, 384:512] = dot_tn(mixed, grad[:, 128 * s : 128 * s + 128]).astype(BF)
    grad_mixed = dot_nt(grad, w_out).astype(BF)
    grad_packed = attention_bwd(packed, grad_mixed, 512, 32, 196, p_ref)
    grad_normed = jnp.zeros((DEC_ROWS, 512), F32)
    for s in range(SEC):
        part = grad_packed[:, 384 * s : 384 * s + 384]
        gw_ref[s, :, 0:384] = dot_tn(low_a, part).astype(BF)
        grad_normed = grad_normed + dot_nt(part, w_ref[s, :, 0:384])
    give((1024, 512), rows_place(gw_ref, 64))
    grad_placed = grad_out + norm_back(grad_normed, normed_a, scale_a, vec_ref[0:1])
    grad_token = column_sum(uncovered * grad_placed)
    grad_embedded = lax.dot_general(
        onehot, grad_placed, (((0,), (0,)), ((), ())), precision=lax.Precision.HIGHEST, preferred_element_type=F32
    ).astype(BF)
    for s in range(SEC):
        ge_ref[s] = dot_tn(before, grad_embedded[:, 128 * s : 128 * s + 128]).astype(BF)
    give((1536, 128), part_place(ge_ref, 0, 64))
    give((1664, 128), part_place(ge_ref, 64, 32), 32)
    dx_ref[...] = dot_nt(grad_embedded, jnp.concatenate([e_ref[s] for s in range(SEC)], axis=1)).astype(BF)
    totals = column_sum(grad_packed.astype(F32))
    gvec_ref[...] = jnp.concatenate(
        [
            column_sum(grad_normed * normed_a),
            sums_f[0],
            column_sum(grad_embedded.astype(F32)),
            grad_token,
            column_sum(grad_normed),
            totals[:, :512],
            totals[:, 1024:],
            column_sum(grad_out),
            *sums_f[1:],
        ],
        axis=0,
    )
    wait_all(copies)


def enc_ffn_bwd(inn, table, dh_ref, h_ref, a_ref, r_ref, vec_ref, *refs):
    (ups, downs), rest = take(refs, inn)
    dx_ref, gvec_ref, gupb_ref, *rest = rest
    (sends,), (u_ref, v_ref, dr_ref, df_ref, sem_u, sem_v) = take(rest, ((SEC, 0),))
    copies_v = []
    for half in range(2):
        copies_v += block_copies(
            downs, table, inn[1][1], (0, 96), (384 * half, 384), turned_place(v_ref, 192, 384, 96 * half, 96), sem_v
        )
    copies_u = block_copies(ups, table, inn[0][1], (0, 96), (0, 768), rows_place(u_ref, 96), sem_u)
    grad = dh_ref[...]
    grad_out = grad.astype(F32)
    low = a_ref[...]
    for s in range(SEC):
        df_ref[s] = grad[:, 192 * s : 192 * s + 192]
        sends[s][:, 0:768] = low
    wait_all(copies_v)
    wait_all(copies_u)
    grad_normed = jnp.zeros((ENC_ROWS, 768), F32)
    for s in range(SEC):
        lanes = slice(768 * s, 768 * s + 768)
        hidden = r_ref[:, lanes]
        active, share = gelu_parts(hidden)
        active = active.astype(BF)
        for r in range(SEC):
            sends[r][:, 768 + 768 * s : 1536 + 768 * s] = active
        grad_hidden = (dot(grad, v_ref[:, lanes]) * gelu_slope(hidden, share)).astype(BF)
        gupb_ref[:, lanes] = column_sum(grad_hidden.astype(F32))
        dr_ref[s] = grad_hidden
        grad_normed = grad_normed + dot_nt(grad_hidden, u_ref[s])
    here = table[SECTION]
    for r in range(SEC):
        sends[r][:, 3840:4608] = dr_ref[here ^ r]
        sends[r][:, 4608:4800] = df_ref[here ^ r]
    normed, scale = norm_stats(h_ref[...].astype(F32))
    gvec_ref[...] = jnp.concatenate(
        [column_sum(grad_normed * normed), column_sum(grad_normed), column_sum(grad_out)], axis=0
    )
    dx_ref[...] = (grad_out + norm_back(grad_normed, normed, scale, vec_ref[1:2])).astype(BF)


def enc_att_bwd(inn, table, dh_ref, x_ref, a_ref, k_ref, z_ref, vec_ref, ge_ref, gue_ref, gd_ref, gud_ref, *refs):
    (pieces,), (dx_ref, *rest) = take(refs, inn)
    (sends,), (w_ref, d_ref, v_ref, sem_w) = take(rest, ((SEC, 0),))
    copies_w = block_copies(pieces, table, inn[0][1], (0, 96), (0, 768), rows_place(w_ref, 96), sem_w)
    grad = dh_ref[...]
    grad_out = grad.astype(F32)
    low, packed, mixed = a_ref[...], k_ref[...], z_ref[...]
    gap = jnp.zeros((ENC_ROWS, 64), BF)
    parts = [grad[:, 192 * s : 192 * s + 192] for s in range(SEC)]
    wait_all(copies_w)
    grad_mixed = jnp.zeros((ENC_ROWS, 768), F32)
    for s in range(SEC):
        grad_mixed = grad_mixed + dot_nt(jnp.concatenate([gap, parts[s]], axis=1), w_ref[s, :, 512:768])
    grad_packed = attention_bwd(packed, grad_mixed.astype(BF), 768, 64, 49, None)
    grad_normed = jnp.zeros((ENC_ROWS, 768), F32)
    for s in range(SEC):
        part = grad_packed[:, 576 * s : 576 * s + 576]
        d_ref[s] = jnp.concatenate([part, parts[s]], axis=1)
        grad_normed = grad_normed + dot_nt(jnp.concatenate([part, gap], axis=1), w_ref[s, :, 0:640])
    normed, scale = norm_stats(padded(x_ref[0].astype(F32), ENC_ROWS))
    grad_in = grad_out + norm_back(grad_normed, normed, scale, vec_ref[0:1])
    dx_ref[0] = grad_in[:49]
    totals = column_sum(grad_packed.astype(F32))
    others, dec = ge_ref[...], gd_ref[...]
    enc = jnp.concatenate(
        [
            column_sum(grad_normed * normed), others[:1], column_sum(grad_normed), totals[:, :768],
            totals[:, 1536:], column_sum(grad_out), others[1:],
        ],
        axis=0,
    )
    tail = jnp.concatenate([dec[8:], jnp.zeros((6, 512), F32)], axis=0)
    dec = dec[:8]
    up_e = jnp.concatenate([gue_ref[...], jnp.zeros((7, 3072), F32)], axis=0)
    up_d = jnp.concatenate([gud_ref[...], jnp.zeros((7, 2048), F32)], axis=0)
    v_ref[...] = jnp.zeros_like(v_ref)
    for s in range(SEC):
        v_ref[s, :, 0:192] = enc[:, 192 * s : 192 * s + 192]
        v_ref[s, :, 256:384] = dec[:, 128 * s : 128 * s + 128]
        v_ref[s, :, 384:512] = tail[:, 128 * s : 128 * s + 128]
        v_ref[s, :, 512:1280] = up_e[:, 768 * s : 768 * s + 768]
        v_ref[s, :, 1280:1792] = up_d[:, 512 * s : 512 * s + 512]
    here = table[SECTION]
    for r in range(SEC):
        sends[r][:48, 0:768] = low[:48]
        sends[r][:48, 768:1536] = mixed[:48]
        sends[r][:48, 1536:2304] = d_ref[here ^ r, :48]
        last = jnp.concatenate([low[48:56], mixed[48:56], d_ref[here ^ r, 48:56]], axis=1).astype(F32)
        sends[r][48:, :] = jnp.concatenate([last, v_ref[here ^ r]], axis=0).astype(BF)


def enc_ffn_weights(outs, table, own_ref, *refs):
    (others, grads), (gu_ref, gv_ref, sem) = take(refs, ((SEC - 1, 0), outs))

    def gathered(first, count):
        return jnp.concatenate([own_ref[:, first : first + count]] + [o[:, first : first + count] for o in others], axis=0)

    turned = gathered(4608, 192)
    whole = dot_tn(gathered(0, 768), gathered(3840, 768)).astype(BF)
    for d in range(ROWB):
        gu_ref[d] = whole[96 * d : 96 * d + 96]
    copies = block_copies(grads, table, outs[1], (0, 96), (0, 768), lambda block: gu_ref.at[block], sem, True)
    for d in range(ROWB):
        gv_ref[d] = dot_tn(turned, gathered(768 + 384 * d, 384)).astype(BF)
    for half in range(2):
        copies += block_copies(
            grads, table, outs[1], (0, 96), (768 + 384 * half, 384),
            lambda block: gv_ref.at[block, pl.ds(96 * half, 96), :], sem, True,
        )
    wait_all(copies)


def enc_att_weights(outs, table, own_ref, *refs):
    (others, grads), (g_ref, v_ref, sem) = take(refs, ((SEC - 1, 0), outs))

    valid = row_mask(ENC_ROWS, 49)

    def gathered(first, count):
        return jnp.concatenate([o[:, first : first + count] for o in (own_ref, *others)], axis=0)

    def left(first):
        parts = [o[:, first : first + 768].astype(F32) for o in (own_ref, *others)]
        return jnp.concatenate([jnp.where(valid, part, 0.0).astype(BF) for part in parts], axis=0)

    right = gathered(1536, 768)
    lane = lax.broadcasted_iota(jnp.int32, (1, 768), 1)
    whole = jnp.where(lane < 576, dot_tn(left(0), right), dot_tn(left(768), right)).astype(BF)
    vectors = own_ref[48:, :1792].astype(F32)
    for other in others:
        vectors = vectors + other[48:, :1792].astype(F32)
    vectors = jnp.concatenate([vectors[8:], jnp.zeros((8, 1792), F32)], axis=0)
    below = jnp.zeros((16, 768), F32)
    for d in range(ROWB):
        g_ref[d, :96] = whole[96 * d : 96 * d + 96]
        v_ref[...] = below
        v_ref[:, 0:24] = vectors[:, 24 * d : 24 * d + 24]
        v_ref[:, 128:144] = vectors[:, 256 + 16 * d : 272 + 16 * d]
        v_ref[:, 256:272] = vectors[:, 384 + 16 * d : 400 + 16 * d]
        v_ref[:, 384:480] = vectors[:, 512 + 96 * d : 608 + 96 * d]
        v_ref[:, 512:576] = vectors[:, 1280 + 64 * d : 1344 + 64 * d]
        g_ref[d, 96:112] = v_ref[...].astype(BF)
    wait_all(block_copies(grads, table, outs[1], (0, 112), (0, 768), lambda block: g_ref.at[block], sem, True))


def pack_first(qkv_ref, out_ref, eg_ref, eb_ref, eu_ref, dg_ref, db_ref, du_ref, o_ref):
    o_ref[:96] = jnp.concatenate([qkv_ref[...], out_ref[...]], axis=1).astype(BF)
    def wide(values):
        return jnp.concatenate([values, jnp.zeros((values.shape[0], 128 - values.shape[1]), F32)], axis=1)

    def tall(values):
        return jnp.concatenate([values, jnp.zeros((8 - values.shape[0], 128), F32)], axis=0)

    db = db_ref[...]
    parts = [
        jnp.concatenate([wide(eg_ref[...]), wide(eb_ref[...])], axis=0),
        tall(jnp.concatenate([wide(eu_ref[...]), wide(du_ref[...])], axis=0)),
        jnp.concatenate([wide(dg_ref[...]), wide(db[:6])], axis=0),
        tall(wide(db[6:])),
    ]
    below = jnp.concatenate(parts + [jnp.zeros((8, 256), F32)], axis=1)
    o_ref[96:112] = jnp.concatenate([below, jnp.zeros((8, 768), F32)], axis=0).astype(BF)


def pack_rest(up_ref, down_ref, embed_ref, qkv_ref, out_ref, upd_ref, downd_ref, up_o, down_o, dec_o):
    up_o[...] = up_ref[...].astype(BF)
    turned = jnp.transpose(down_ref[...])
    down_o[...] = jnp.concatenate([turned[:96], turned[96:]], axis=1).astype(BF)
    turned = jnp.transpose(downd_ref[...])
    dec_o[...] = jnp.concatenate(
        [qkv_ref[...], out_ref[...], upd_ref[...], turned[:64], turned[64:], embed_ref[:64], padded(embed_ref[64:], 64)],
        axis=1,
    ).astype(BF)


def call(body, outs, scratch, *operands, memory, micros=8):
    spaces = {"v": pltpu.VMEM, "s": pltpu.SMEM, "h": pl.ANY}
    return pl.pallas_call(
        body,
        out_shape=[jax.ShapeDtypeStruct(shape, dtype) for shape, dtype, _ in outs],
        in_specs=[pl.BlockSpec(memory_space=spaces[m]) for m in memory],
        out_specs=[pl.BlockSpec(memory_space=spaces[m]) for _, _, m in outs],
        scratch_shapes=scratch,
        compiler_params=pltpu.CompilerParams(vmem_limit_bytes=VMEM_BYTES),
        cost_estimate=pl.CostEstimate(flops=micros * 10**9, bytes_accessed=micros * 10**6, transcendentals=0),
    )(*operands)


def fold_rows(matrix):
    half = matrix.shape[-2] // 2
    return jnp.concatenate([matrix[..., :half, :], matrix[..., half:, :]], axis=-1)


def unfold_rows(matrix):
    half = matrix.shape[-1] // 2
    return jnp.concatenate([matrix[..., :half], matrix[..., half:]], axis=-2)


def turn(matrix):
    return jnp.swapaxes(matrix, -1, -2)


def pack_weights(qkv_e, out_e, up_e, down_e, embed, qkv_d, out_d, up_d, down_d):
    return (
        jnp.concatenate([qkv_e, out_e], axis=-1),
        up_e,
        fold_rows(turn(down_e)),
        jnp.concatenate(
            [
                *(member[..., :64, :] for member in (qkv_d, out_d, up_d, fold_rows(turn(down_d)), embed)),
                jnp.pad(embed[..., 64:, :], ((0, 0), (0, 32), (0, 0))),
            ],
            axis=-1,
        ),
    )


def unpack_grads(dec, ffn_e, att_e):
    embed = jnp.concatenate([dec[..., 1536:1664], dec[..., :32, 1664:]], axis=-2)
    return (
        att_e[..., :96, :576],
        att_e[..., :96, 576:],
        ffn_e[..., :768],
        turn(unfold_rows(ffn_e[..., 768:])),
        embed,
        dec[..., 1024:1408],
        dec[..., 1408:1536],
        dec[..., :512],
        turn(unfold_rows(dec[..., 512:1024])),
    )


def spread(rows):
    return rows.transpose(1, 0, 2).reshape(rows.shape[1], -1)


def exchange(value, flip):
    flips = flip if isinstance(flip, tuple) else (flip, flip)
    pairs = [(device, device ^ flips[device & 1]) for device in range(BLOCKS)]
    return lax.ppermute(value, ("section", "dp"), pairs)


CORE, NEAR, FAR, FIRST, SECOND = 1, 2, 4, (8, 16), (16, 8)


def block_at(device, core, relative):
    first = jnp.where(core == 1, FIRST[1], FIRST[0])
    flips = NEAR * (relative & 3) + first * ((relative >> 2) & 1) + (24 - first) * ((relative >> 3) & 1)
    return ((device & 30) | core) ^ flips


EVENTS = """
aZ1 aZ2 aZ3 aC aP aQ bZ1 bZ2 bZ3 bC a1 aR bP bQ cZ1 cZ2 cZ3 a2 a3 cC b1 bR cP cQ a4 F1 b2 b3 cR b4 c1 c2 c3 c4
"""


class Order:
    def __init__(self):
        self.token = None

    def after(self, value):
        if self.token is None:
            return value
        return lax.optimization_barrier((value, self.token))[0]

    def came(self, value):
        value = self.after(value)
        self.token = value
        return value


def add(*members):
    total = members[0].astype(F32)
    for member in members[1:]:
        total = total + member.astype(F32)
    return total


def line_add(*members):
    return add(*(member[:2] for member in members)), add(*(member[2:] for member in members)).astype(BF)


def move(value, pairs):
    return lax.ppermute(value, ("section", "dp"), pairs)


MIDDLE = [(d, d ^ 6) for d in range(BLOCKS) if (d >> 1) & 3 in (1, 2)]
INWARD = [(d, d ^ 2) for d in range(BLOCKS) if (d >> 1) & 3 in (0, 3)]


def together(*members):
    return lax.optimization_barrier(members)


def shards(visible, cotangent, keep_index, positions, *parameters):
    both = ("section", "dp")
    fast = lax.axis_size("dp") == ROWB
    section = lax.axis_index("section")
    enc_g, enc_b, enc_u, dec_g, dec_b, dec_u = parameters[9:]
    enc_u, dec_u = enc_u[None], dec_u[None]
    order = jnp.arange(BLOCKS, dtype=jnp.int32)
    dma = pltpu.SemaphoreType.DMA
    enc_shape, dec_shape = (ENC_ROWS, 768), (DEC_ROWS, 512)
    enc_sq, enc_wide, dec_sq, dec_wide = (
        pltpu.VMEM(shape, BF) for shape in ((SEC, 768, 768), (768, 3072), (SEC, 512, 512), (512, 2048))
    )
    path, plain, here = order, order, section[None]
    out_path, out_z = order, order[:ROWB]
    if fast:
        device = lax.axis_index(both)
        core = device & 1
        near = jnp.where(order < 16, core, 1 - core)
        path = block_at(device, near, order & 15)
        z = (device >> 1) & 3
        line = order & 3
        line = z ^ jnp.where(line < 2, line, jnp.where((z == 0) | (z == 3), line, 5 - line))
        out_path = (block_at(device, 1 - near, 12 - (order & 12)) & 25) | (2 * line)
        out_z = (2 * line | jnp.where(order < 4, 1 - core, core))[:ROWB]
    table = jnp.concatenate([path, plain, out_path, out_z, here])
    step = Order()

    def start(member, flip):
        return exchange(step.after(member), flip)

    def spaces(*sets):
        return "h" * sum(len(member) for member, _ in sets)

    def used(*sets):
        return tuple((len(member), first) for member, first in sets)

    def operands(*sets):
        return [piece for member, _ in sets for piece in member]

    def run_f1(att_e, inputs, enc_vec=None):
        outs = [(enc_shape, BF, "v"), (enc_shape, BF, "v"), ((ENC_ROWS, 2304), BF, "v"), (enc_shape, BF, "v")]
        vectors = [((r, c), F32, "v") for r, c in ((8, 768), (1, 3072), (10, 512), (1, 2048))]
        if enc_vec is None:
            return call(
                partial(enc_att_fwd, used(att_e)),
                outs + vectors,
                [enc_sq, pltpu.VMEM((BLOCKS, 16, 512), BF), dma, dma],
                table, inputs, *operands(att_e),
                memory="sv" + spaces(att_e),
            )

        def body(table, x_ref, vec_ref, *refs):
            count = len(operands(att_e))
            enc_att_fwd(used(att_e), table, x_ref, *refs[: count + 4], vec_ref, *refs[count + 4 :])

        return call(
            body, outs, [enc_sq, dma], table, inputs, enc_vec, *operands(att_e), memory="svv" + spaces(att_e)
        )

    def run_f2(h1, up_e, down_e, enc_vec, enc_upb):
        return call(
            partial(enc_ffn_fwd, used(up_e, down_e)),
            [(enc_shape, BF, "v"), (enc_shape, BF, "v"), ((ENC_ROWS, 3072), F32, "v")],
            [enc_sq, enc_wide, dma, dma],
            table, h1, enc_vec, enc_upb, *operands(up_e, down_e),
            memory="svvv" + spaces(up_e, down_e),
        )

    if fast:
        qkv_e, out_e, mat_up, mat_down, embed, qkv_d, out_d, up_d, down_d = parameters[:9]
        (first,) = call(
            pack_first, [((112, 768), BF, "v")], [],
            qkv_e, out_e, enc_g, enc_b, enc_u, dec_g, dec_b, dec_u, memory="v" * 8,
        )
        rest = call(
            pack_rest, [((96, 768), BF, "v"), ((96, 768), BF, "v"), ((64, 1792), BF, "v")], [],
            mat_up, mat_down, embed, qkv_d, out_d, up_d, down_d, memory="v" * 7,
        )
        dec = ([lax.all_gather(rest[2], both, axis=0, tiled=False)], IN_PLAIN)
        own = {"a": first[None], "b": rest[0][None], "c": rest[1][None]}
        got = {}

        def pieces(name):
            return ([got[name + part] for part in ("C", "P", "Q", "R", "1", "2", "3", "4")], IN_PATH)

        for event in EVENTS.split():
            name, part = event[0], event[1:]
            if event == "F1":
                got[event] = list(run_f1(pieces("a"), step.after(visible)))
                got[event][0] = step.came(got[event][0])
            elif part[0] == "Z":
                got[event] = start(own[name], NEAR * int(part[1]))
            elif part == "C":
                got[event] = step.came(jnp.concatenate([own[name]] + [got[name + "Z" + i] for i in "123"], axis=0))
            elif part == "P":
                got[event] = start(got[name + "C"], FIRST)
            elif part == "Q":
                got[event] = start(got[name + "C"], SECOND)
            elif part == "R":
                got[event] = exchange(step.came(got[name + "P"]), SECOND)
            elif part in "1234":
                held = name + "CPQR"[int(part) - 1]
                got[event] = exchange(step.came(got[held]), CORE)
        att_e, up_e, down_e = pieces("a"), pieces("b"), pieces("c")
        h1, a1, k1, z1, enc_vec, enc_upb, dec_vec, dec_upb = got["F1"]
    else:
        full = []
        for member in parameters[:9]:
            member = lax.all_gather(member.astype(BF), "dp", axis=0, tiled=True)
            member = lax.all_gather(member, "section", axis=0, tiled=False)
            full.append(member.reshape(BLOCKS, member.shape[1] // ROWB, member.shape[2]))
        att_e, up_e, down_e, dec = (([member], IN_PLAIN) for member in pack_weights(*full))
        enc_vec, enc_upb, dec_vec, dec_upb = (
            lax.all_gather(member.astype(BF), both, axis=1, tiled=True).astype(F32)
            for member in (jnp.concatenate([enc_g, enc_b]), enc_u, jnp.concatenate([dec_g, dec_b]), dec_u)
        )
        h1, a1, k1, z1 = run_f1(att_e, visible, enc_vec)
    h2, a2, r2 = run_f2(h1, up_e, down_e, enc_vec, enc_upb)
    many = 2 if fast else 1

    def grad_blocks(blocks, rows, columns):
        return [((blocks // many, rows, columns), BF, "h")] * many

    embed_sq, probs = pltpu.VMEM((SEC, 768, 128), BF), pltpu.VMEM((2, 8 * DEC_ROWS, DEC_ROWS), F32)
    block_out, dh2, gvec_d, gupb_d, *g_dec = call(
        partial(dec_both, used(dec), (many, OUT_PATH)),
        [((1, 196, 512), F32, "v"), (enc_shape, BF, "v"), ((10, 512), F32, "v"), ((1, 2048), F32, "v")]
        + grad_blocks(BLOCKS, 64, 1792),
        [embed_sq, dec_sq, dec_sq, dec_wide] * 2 + [probs] + [dma] * 5,
        table, h2, keep_index, positions, cotangent, dec_vec, dec_upb, *operands(dec),
        memory="svvvvvv" + spaces(dec),
    )
    if fast:
        swap_d = exchange(g_dec[0], CORE)
    dh1, gv_ffn_e, gupb_e, *sends_f = call(
        partial(enc_ffn_bwd, used(up_e, down_e)),
        [(enc_shape, BF, "v"), ((3, 768), F32, "v"), ((1, 3072), F32, "v")] + [((ENC_ROWS, 4800), BF, "v")] * SEC,
        [enc_sq, enc_wide, pltpu.VMEM((SEC, ENC_ROWS, 768), BF), pltpu.VMEM((SEC, ENC_ROWS, 192), BF), dma, dma],
        table, dh2, h1, a2, r2, enc_vec, *operands(up_e, down_e),
        memory="s" + "v" * 5 + spaces(up_e, down_e),
    )

    def to_section(members):
        return [
            lax.ppermute(members[i], "section", [(s, s ^ i) for s in range(SEC)]) for i in range(1, SEC)
        ]

    if fast:
        dh1, swap_d, *sends_f = together(dh1, swap_d, *sends_f)
        came_f = to_section(sends_f)
        pair_d = add(g_dec[1][:8], swap_d[:8]).astype(BF)
        dh1, pair_d = together(dh1, pair_d)
        second_d = exchange(pair_d, SECOND)
    else:
        came_f = to_section(sends_f)
    input_grad, *sends_a = call(
        partial(enc_att_bwd, used(att_e)),
        [((1, 49, 768), F32, "v")] + [((ENC_ROWS, 2304), BF, "v")] * SEC,
        [enc_sq, pltpu.VMEM((SEC, ENC_ROWS, 768), BF), pltpu.VMEM((SEC, 8, 2304), F32), dma],
        table, dh1, visible, a1, k1, z1, enc_vec, gv_ffn_e, gupb_e, gvec_d, gupb_d, *operands(att_e),
        memory="s" + "v" * 10 + spaces(att_e),
    )
    step = Order()
    if fast:
        step.came(input_grad)
        second_d = step.came(second_d)
        first_d = exchange(add(g_dec[1][8:12], swap_d[8:12], second_d[:4]).astype(BF), FIRST)
        came_f = [step.came(member) for member in came_f]
        sends_a = [step.after(member) for member in sends_a]
    came_a = to_section(sends_a)
    g_ffn_e = call(
        partial(enc_ffn_weights, (many, OUT_Z)),
        grad_blocks(ROWB, 96, 1536),
        [pltpu.VMEM((ROWB, 96, 768), BF), pltpu.VMEM((ROWB, 192, 384), BF), dma],
        table, sends_f[0], *came_f,
        memory="svvvv",
    )
    if fast:
        swap_f = exchange(g_ffn_e[0], CORE)
        step.came(g_ffn_e[1])
        first_d = step.came(first_d)
        pair_d, far_d = line_add(g_dec[1][12:], swap_d[12:], second_d[4:], first_d)
        in_d = move(far_d, INWARD)
        swap_f = step.came(swap_f)
        pair_f, far_f = line_add(g_ffn_e[1], swap_f)
        in_f = move(far_f, INWARD)
        far_d = add(far_d, step.came(in_d)).astype(BF)
        mid_d = move(far_d, MIDDLE)
        came_a = [step.came(member) for member in came_a]
    g_att_e = call(
        partial(enc_att_weights, (many, OUT_Z)),
        grad_blocks(ROWB, 112, 768),
        [pltpu.VMEM((ROWB, 112, 768), BF), pltpu.VMEM((16, 768), F32), dma],
        table, sends_a[0], *came_a,
        memory="svvvv",
    )
    if fast:
        swap_x = exchange(g_att_e[0], CORE)
        step.came(g_att_e[1])
        far_f = add(far_f, step.came(in_f)).astype(BF)
        mid_f = move(far_f, MIDDLE)
        pair_d = add(pair_d, step.came(mid_d))
        near_d = exchange(pair_d[1].astype(BF), NEAR)
        swap_x = step.came(swap_x)
        pair_x, far_x = line_add(g_att_e[1], swap_x)
        in_x = move(far_x, INWARD)
        pair_f = add(pair_f, step.came(mid_f))
        near_f = exchange(pair_f[1].astype(BF), NEAR)
        far_x = add(far_x, step.came(in_x)).astype(BF)
        mid_x = move(far_x, MIDDLE)
        sum_d = add(pair_d[0], step.came(near_d))
        pair_x = add(pair_x, step.came(mid_x))
        near_x = exchange(pair_x[1].astype(BF), NEAR)
        sum_f = add(pair_f[0], step.came(near_f))
        sums = [sum_d, sum_f, add(pair_x[0], near_x)]
        matrix_outs = unpack_grads(*sums)
        below = sums[2][None, 96:104]
    else:
        matrix_outs = []
        for number, member in enumerate(unpack_grads(g_dec[0], g_ffn_e[0], g_att_e[0])):
            if number >= 4:
                member = member.reshape(SEC, ROWB * member.shape[1], member.shape[2])
                member = lax.psum_scatter(member, "section", scatter_dimension=0, tiled=False)
            else:
                member = member.reshape(ROWB * member.shape[1], member.shape[2])
            matrix_outs.append(lax.psum_scatter(member, "dp", scatter_dimension=0, tiled=True).astype(F32))
        below = g_att_e[0][:, 96:104].astype(F32)
    vector_outs = [
        spread(member)
        for member in (
            below[:, :, :24], below[:, :, 128:144], below[:, :2, 256:272], below[:, :1, 384:480], below[:, :1, 512:576]
        )
    ]
    if not fast:
        vector_outs = [lax.psum_scatter(member, "dp", scatter_dimension=1, tiled=True) for member in vector_outs]
    enc, dec_first, dec_last, enc_u, dec_u = vector_outs
    dec_all = jnp.concatenate([dec_first, dec_last], axis=0)
    return (block_out, input_grad, *matrix_outs, enc[:2], enc[2:], enc_u[0], dec_all[:2], dec_all[2:], dec_u[0])


def solution(mesh):
    matrix, wide, line = P("dp", "section"), P(None, ("section", "dp")), P(("section", "dp"))
    image = P(("section", "dp"), None, None)
    vectors = (wide, wide, line, wide, wide, line)
    return jax.shard_map(
        shards,
        mesh=mesh,
        in_specs=(image, image, P(("section", "dp"), None), P()) + (matrix,) * 9 + vectors,
        out_specs=(image, image) + (matrix,) * 9 + vectors,
        check_vma=False,
    )
```

profile of v0, /device:TPU:0, one launch (start us, length us, event | category | flops | bytes accessed | tf_op | source)
XLA Modules:
  0.0 313.8 jit_solution(10914436612012815084)
XLA Ops:
  7.2 1.9 copy.36.down_ref
  9.1 2.1 shard_map.315
  11.3 1.8 shard_map.314
  13.1 5.0 %collective-permute-start.2 = (bf16[1,112,768]{2,1,0:T(8,128)(2,1)}, bf16[1,112,768]{2,1,0:T(8,128)(2,1)S(1)}, u32[]{:S(2)}, u32[]{:S(2)}) collective-permute-start(bf16[1,112,768]{2,1,0:T(8,128)(2,1)} %bitcast.46), channel_id=1, source_target_pairs={{0,6},{1,7},{2,4},{3,5},{4,2},{5,3},{6,0},{7,1},{8,14},{9,15},{10,... | collective-permute-start | bytes 516104 | tf_op jit(solution)/shard_map/ppermute | solution.py:592
  18.8 4.9 %collective-permute-done.2 = bf16[1,112,768]{2,1,0:T(8,128)(2,1)S(1)} collective-permute-done((bf16[1,112,768]{2,1,0:T(8,128)(2,1)}, bf16[1,112,768]{2,1,0:T(8,128)(2,1)S(1)}, u32[]{:S(2)}, u32[]{:S(2)}) %collective-permute-start.2) | collective-permute-done | bytes 172064 | tf_op jit(solution)/shard_map/ppermute | solution.py:592
  23.7 14.2 %collective-permute-done.1 = bf16[1,112,768]{2,1,0:T(8,128)(2,1)S(1)} collective-permute-done((bf16[1,112,768]{2,1,0:T(8,128)(2,1)}, bf16[1,112,768]{2,1,0:T(8,128)(2,1)S(1)}, u32[]{:S(2)}, u32[]{:S(2)}) %collective-permute-start.1) | collective-permute-done | bytes 172064 | tf_op jit(solution)/shard_map/ppermute | solution.py:592
  37.8 1.0 pad_maximum_fusion.refs_0_
  38.9 1.6 collective-permute-start.3
  40.4 1.5 collective-permute-start.12
  41.9 2.5 collective-permute-start.6
  44.4 1.9 collective-permute-start.4
  46.3 6.7 %collective-permute-done.6 = bf16[1,96,768]{2,1,0:T(8,128)(2,1)S(1)} collective-permute-done((bf16[1,96,768]{2,1,0:T(8,128)(2,1)S(1)}, bf16[1,96,768]{2,1,0:T(8,128)(2,1)S(1)}, u32[]{:S(2)}, u32[]{:S(2)}) %collective-permute-start.6) | collective-permute-done | bytes 147488 | tf_op jit(solution)/shard_map/ppermute | solution.py:592
  53.0 12.1 %collective-permute-done.5 = bf16[1,96,768]{2,1,0:T(8,128)(2,1)S(1)} collective-permute-done((bf16[1,96,768]{2,1,0:T(8,128)(2,1)S(1)}, bf16[1,96,768]{2,1,0:T(8,128)(2,1)S(1)}, u32[]{:S(2)}, u32[]{:S(2)}) %collective-permute-start.5) | collective-permute-done | bytes 147488 | tf_op jit(solution)/shard_map/ppermute | solution.py:592
  65.4 1.9 collective-permute-start.11
  67.3 2.6 collective-permute-start.9
  69.9 2.8 collective-permute-done.11
  72.6 15.0 %collective-permute-done.10 = bf16[1,96,768]{2,1,0:T(8,128)(2,1)S(1)} collective-permute-done((bf16[1,96,768]{2,1,0:T(8,128)(2,1)S(1)}, bf16[1,96,768]{2,1,0:T(8,128)(2,1)S(1)}, u32[]{:S(2)}, u32[]{:S(2)}) %collective-permute-start.10) | collective-permute-done | bytes 147488 | tf_op jit(solution)/shard_map/ppermute | solution.py:592
  88.2 0.9 copy-done.17
  91.0 1.0 collective-permute-start.24
  92.5 1.6 collective-permute-start.18
  94.1 6.2 %shard_map.316 = (bf16[64,768]{1,0:T(8,128)(2,1)}, bf16[64,768]{1,0:T(8,128)(2,1)}, bf16[64,2304]{1,0:T(8,128)(2,1)}, bf16[64,768]{1,0:T(8,128)(2,1)}, f32[8,768...) custom-call(s32[105]{0:T(128)} %concatenate.24.table, bf16[1,49,768]{2,1,0:T(8,128)(2,1)} %x_ref.2, ...), custom_call_target="tpu_custom_call" | custom-call | flops 8000000000 | bytes 8000000 | tf_op jit(solution)/shard_map/pallas_call | solution.py:530
  100.3 4.7 %collective-permute-done.17.refs_2_ = bf16[4,96,768]{2,1,0:T(8,128)(2,1)} collective-permute-done((bf16[4,96,768]{2,1,0:T(8,128)(2,1)S(1)}, bf16[4,96,768]{2,1,0:T(8,128)(2,1)}, u32[]{:S(2)}, u32[]{:S(2)}) %collective-permute-start.17) | collective-permute-done | bytes 589856 | tf_op jit(solution)/shard_map/ppermute | solution.py:592
  105.0 3.3 %collective-permute-done.22.refs_9_ = bf16[4,96,768]{2,1,0:T(8,128)(2,1)} collective-permute-done((bf16[4,96,768]{2,1,0:T(8,128)(2,1)S(1)}, bf16[4,96,768]{2,1,0:T(8,128)(2,1)}, u32[]{:S(2)}, u32[]{:S(2)}) %collective-permute-start.22) | collective-permute-done | bytes 589856 | tf_op jit(solution)/shard_map/ppermute | solution.py:592
  108.3 1.1 collective-permute-start.25
  109.4 9.4 %collective-permute-done.18.refs_3_ = bf16[4,96,768]{2,1,0:T(8,128)(2,1)} collective-permute-done((bf16[4,96,768]{2,1,0:T(8,128)(2,1)}, bf16[4,96,768]{2,1,0:T(8,128)(2,1)}, u32[]{:S(2)}, u32[]{:S(2)}) %collective-permute-start.18) | collective-permute-done | bytes 589856 | tf_op jit(solution)/shard_map/ppermute | solution.py:592
  119.3 5.7 %collective-permute-done.25.refs_11_ = bf16[4,96,768]{2,1,0:T(8,128)(2,1)S(1)} collective-permute-done((bf16[4,96,768]{2,1,0:T(8,128)(2,1)}, bf16[4,96,768]{2,1,0:T(8,128)(2,1)S(1)}, u32[]{:S(2)}, u32[]{:S(2)}) %collective-permute-start.25) | collective-permute-done | bytes 589856 | tf_op jit(solution)/shard_map/ppermute | solution.py:592
  126.0 1.2 collective-permute-done.23.refs_7_
  127.2 1.7 collective-permute-done.21.refs_6_
  128.9 0.8 collective-permute-done.20.refs_5_
  130.8 8.0 %shard_map.317 = (bf16[64,768]{1,0:T(8,128)(2,1)}, bf16[64,768]{1,0:T(8,128)(2,1)}, f32[64,3072]{1,0:T(8,128)}) custom-call(s32[105]{0:T(128)} %concatenate.24.table, bf16[64,768]{1,0:T(8,128)(2,1)} %get-tuple-element.122.h_ref, f32[8,768]{1,0:T(8,128)} %get-tuple-element.123.vec_ref, f32[1,3072]{1,0:T(1,128)} %get-tuple-element.124.upb_ref, ...), custom_call_target="tpu_custom_call" | custom-call | flops 8000000000 | bytes 8000000 | tf_op jit(solution)/shard_map/pallas_call | solution.py:530
  138.8 19.2 %shard_map.318 = (f32[1,196,512]{2,1,0:T(8,128)}, bf16[64,768]{1,0:T(8,128)(2,1)}, f32[10,512]{1,0:T(8,128)}, f32[1,2048]{1,0:T(1,128)}, bf16[16,64,1792]{2,1,0:T(8,128)(2,1)}, /*index=5*/bf16[16,64,1792]{2,1,0:T(8,128)(2,1)}) custom-call(s32[105]{0:T(128)} %concatenate.24.table, bf16[64,768]{1,0:T(8,128)(2,1)} %get-tuple-element.134.h_ref, ...), custom_call_target="tpu_custom_call" | custom-call | flops 8000000000 | bytes 8000000 | tf_op jit(solution)/shard_map/pallas_call | solution.py:530
  158.2 9.1 %shard_map.319 = (bf16[64,768]{1,0:T(8,128)(2,1)}, f32[3,768]{1,0:T(4,128)}, f32[1,3072]{1,0:T(1,128)}, bf16[64,4800]{1,0:T(8,128)(2,1)}, bf16[64,4800]{1,0:T(8,...) custom-call(s32[105]{0:T(128)} %concatenate.24.table, bf16[64,768]{1,0:T(8,128)(2,1)} %get-tuple-element.139.dh_ref, ...), custom_call_target="tpu_custom_call" | custom-call | flops 8000000000 | bytes 8000000 | tf_op jit(solution)/shard_map/pallas_call | solution.py:530
  167.4 3.2 %add_convert_fusion = bf16[8,64,1792]{2,1,0:T(8,128)(2,1)} fusion(bf16[16,64,1792]{2,1,0:T(8,128)(2,1)} %collective-permute-done.30, bf16[16,64,1792]{2,1,0:T(8,128)(2,1)S(1)} %copy-done), kind=kLoop, calls=%fused_computation | loop fusion | flops 3670016 | bytes 5505024 | tf_op jit(solution)/shard_map/convert_element_type | solution.py:797
  171.1 1.3 collective-permute-start.31
  172.4 1.1 collective-permute-start.32
  173.5 1.1 collective-permute-start.33
  174.6 8.9 %shard_map.320 = (f32[1,49,768]{2,1,0:T(8,128)}, bf16[64,2304]{1,0:T(8,128)(2,1)}, bf16[64,2304]{1,0:T(8,128)(2,1)}, bf16[64,2304]{1,0:T(8,128)(2,1)}, bf16[64,2304]{1,0:T(8,128)(2,1)}) custom-call(s32[105]{0:T(128)} %concatenate.24.table, bf16[64,768]{1,0:T(8,128)(2,1)} %get-tuple-element.151.dh_ref, bf16[1,49,768]{2,1,0:T(8,128)(2,1)} %x_ref.2, ...), custom_call_target="tpu_custom_call" | custom-call | flops 8000000000 | bytes 8000000 | tf_op jit(solution)/shard_map/pallas_call | solution.py:530
  183.5 30.7 %collective-permute-done.34 = bf16[8,64,1792]{2,1,0:T(8,128)(2,1)} collective-permute-done((bf16[8,64,1792]{2,1,0:T(8,128)(2,1)}, bf16[8,64,1792]{2,1,0:T(8,128)(2,1)}, u32[]{:S(2)}, u32[]{:S(2)}) %collective-permute-start.34) | collective-permute-done | bytes 1835040 | tf_op jit(solution)/shard_map/ppermute | solution.py:592
  214.2 6.7 %collective-permute-done.32.refs_1_ = bf16[64,4800]{1,0:T(8,128)(2,1)} collective-permute-done((bf16[64,4800]{1,0:T(8,128)(2,1)}, bf16[64,4800]{1,0:T(8,128)(2,1)}, u32[]{:S(2)}, u32[]{:S(2)}) %collective-permute-start.32) | collective-permute-done | bytes 614432 | tf_op jit(solution)/shard_map/ppermute | solution.py:791
  220.8 2.7 add_convert_fusion.1
  223.9 3.7 %shard_map.321 = (bf16[4,96,1536]{2,1,0:T(8,128)(2,1)}, bf16[4,96,1536]{2,1,0:T(8,128)(2,1)}) custom-call(s32[105]{0:T(128)} %concatenate.24.table, bf16[64,4800]{1,0:T(8,128)(2,1)} %get-tuple-element.172.own_ref, bf16[64,4800]{1,0:T(8,128)(2,1)} %collective-permute-done.33.refs_0_, bf16[64,4800]{1,0:T(8,128)(2,1)} %collective-permute-done.32.refs_1_, ...), custom_call_target="tpu_custom_call" | custom-call | flops 8000000000 | bytes 8000000 | tf_op jit(solution)/shard_map/pallas_call | solution.py:530
  227.7 1.2 copy.37
  228.8 1.7 copy.38
  230.6 1.7 collective-permute-start.35
  232.7 1.3 collective-permute-start.40
  234.1 6.5 %collective-permute-done.36 = bf16[4,64,1792]{2,1,0:T(8,128)(2,1)} collective-permute-done((bf16[4,64,1792]{2,1,0:T(8,128)(2,1)}, bf16[4,64,1792]{2,1,0:T(8,128)(2,1)}, u32[]{:S(2)}, u32[]{:S(2)}) %collective-permute-start.36) | collective-permute-done | bytes 917536 | tf_op jit(solution)/shard_map/ppermute | solution.py:592
  240.5 1.5 add_convert_fusion.5
  242.0 1.3 collective-permute-start.37
  243.4 1.1 add_convert_fusion.3
  244.5 2.1 collective-permute-start.43
  246.6 7.7 %collective-permute-done.37 = bf16[2,64,1792]{2,1,0:T(8,128)(2,1)S(1)} collective-permute-done((bf16[2,64,1792]{2,1,0:T(8,128)(2,1)S(1)}, bf16[2,64,1792]{2,1,0:T(8,128)(2,1)S(1)}, u32[]{:S(2)}, u32[]{:S(2)}) %collective-permute-start.37) | collective-permute-done | bytes 458784 | tf_op jit(solution)/shard_map/ppermute | solution.py:636
  254.3 1.0 add_convert_fusion.4
  256.7 3.2 %shard_map.322 = (bf16[4,112,768]{2,1,0:T(8,128)(2,1)}, bf16[4,112,768]{2,1,0:T(8,128)(2,1)}) custom-call(s32[105]{0:T(128)} %concatenate.24.table, bf16[64,2304]{1,0:T(8,128)(2,1)} %get-tuple-element.169.own_ref, bf16[64,2304]{1,0:T(8,128)(2,1)} %copy-done.26, bf16[64,2304]{1,0:T(8,128)(2,1)} %copy-done.27, bf16[64,2304]{1,0:T(8,128)(2,1)} %copy-done.28), custom_call_target="tpu_custom_call" | custom-call | flops 8000000000 | bytes 8000000 | tf_op jit(solution)/shard_map/pallas_call | solution.py:530
  260.0 1.7 collective-permute-done.43
  261.7 1.4 add_convert_fusion.2
  263.2 0.8 collective-permute-start.45
  264.0 1.6 convert_add_fusion.1
  265.6 5.4 %collective-permute-start.47 = (bf16[64,1792]{1,0:T(8,128)(2,1)S(1)}, bf16[64,1792]{1,0:T(8,128)(2,1)S(1)}, u32[]{:S(2)}, u32[]{:S(2)}) collective-permute-start(bf16[64,1792]{1,0:T(8,128)(2,1)S(1)} %fusion.4), channel_id=1, source_target_pairs={{0,2},{1,3},{2,0},{3,1},{4,6},{5,7},{6,4},{7,5},{8,10},{9,11},{10,... | collective-permute-start | bytes 688136 | tf_op jit(solution)/shard_map/ppermute | solution.py:592
  271.2 2.0 collective-permute-start.44
  274.1 10.8 %collective-permute-start.49 = (bf16[96,1536]{1,0:T(8,128)(2,1)}, bf16[96,1536]{1,0:T(8,128)(2,1)}, u32[]{:S(2)}, u32[]{:S(2)}) collective-permute-start(bf16[96,1536]{1,0:T(8,128)(2,1)} %fusion.3), channel_id=1, source_target_pairs={{0,2},{1,3},{2,0},{3,1},{4,6},{5,7},{6,4},{7,5},{8,10},{9,11},{10,... | collective-permute-start | bytes 884744 | tf_op jit(solution)/shard_map/ppermute | solution.py:592
  289.3 2.9 collective-permute-done.49
  292.1 1.0 fusion
  293.2 5.6 %collective-permute-start.48 = (bf16[112,768]{1,0:T(8,128)(2,1)S(1)}, bf16[112,768]{1,0:T(8,128)(2,1)S(1)}, u32[]{:S(2)}, u32[]{:S(2)}) collective-permute-start(bf16[112,768]{1,0:T(8,128)(2,1)S(1)} %fusion.5), channel_id=1, source_target_pairs={{0,2},{1,3},{2,0},{3,1},{4,6},{5,7},{6,4},{7,5},{8,10},{9,11},{10,... | collective-permute-start | bytes 516104 | tf_op jit(solution)/shard_map/ppermute | solution.py:592
  300.2 1.9 collective-permute-done.48
  (154 shorter events, 21.3 us)
Async XLA Ops:
  7.2 131.6 %all-gather.3.cloned.1.call-start = ((), (), s32[]{:S(2)}) async-start(), calls=%async_computation | async-start | bytes 7569408 | tf_op jit(solution)/shard_map/all_gather | solution.py:725
  11.3 30.7 %copy-start.14 = (bf16[96,768]{1,0:T(8,128)(2,1)S(1)}, bf16[96,768]{1,0:T(8,128)(2,1)}, u32[]{:S(2)}) copy-start(bf16[96,768]{1,0:T(8,128)(2,1)} %get-tuple-element.106) | copy-start | bytes 442372
  13.1 52.3 %copy-start.13 = (bf16[96,768]{1,0:T(8,128)(2,1)S(1)}, bf16[96,768]{1,0:T(8,128)(2,1)}, u32[]{:S(2)}) copy-start(bf16[96,768]{1,0:T(8,128)(2,1)} %get-tuple-element.112) | copy-start | bytes 442372
  13.1 10.6 %collective-permute-start.2 = (bf16[1,112,768]{2,1,0:T(8,128)(2,1)}, bf16[1,112,768]{2,1,0:T(8,128)(2,1)S(1)}, u32[]{:S(2)}, u32[]{:S(2)}) collective-permute-start(bf16[1,112,768]{2,1,0:T(8,128)(2,1)} %bitcast.46), channel_id=1, source_target_pairs={{0,6},{1,7},{2,4},{3,5},{4,2},{5,3},{6,0},{7,1},{8,14},{9,15},{10,... | collective-permute-start | bytes 516104 | tf_op jit(solution)/shard_map/ppermute | solution.py:592
  18.2 19.7 %collective-permute-start.1 = (bf16[1,112,768]{2,1,0:T(8,128)(2,1)}, bf16[1,112,768]{2,1,0:T(8,128)(2,1)S(1)}, u32[]{:S(2)}, u32[]{:S(2)}) collective-permute-start(bf16[1,112,768]{2,1,0:T(8,128)(2,1)} %bitcast.47), channel_id=1, source_target_pairs={{0,4},{1,5},{2,6},{3,7},{4,0},{5,1},{6,2},{7,3},{8,12},{9,13},{10,... | collective-permute-start | bytes 516104 | tf_op jit(solution)/shard_map/ppermute | solution.py:592
  18.2 19.7 %collective-permute-start = (bf16[1,112,768]{2,1,0:T(8,128)(2,1)}, bf16[1,112,768]{2,1,0:T(8,128)(2,1)S(1)}, u32[]{:S(2)}, u32[]{:S(2)}) collective-permute-start(bf16[1,112,768]{2,1,0:T(8,128)(2,1)} %bitcast.48), channel_id=1, source_target_pairs={{0,2},{1,3},{2,0},{3,1},{4,6},{5,7},{6,4},{7,5},{8,10},{9,11},{10,... | collective-permute-start | bytes 516104 | tf_op jit(solution)/shard_map/ppermute | solution.py:592
  38.9 55.2 %copy-start.5 = (bf16[4,112,768]{2,1,0:T(8,128)(2,1)}, bf16[4,112,768]{2,1,0:T(8,128)(2,1)S(1)}, u32[]{:S(2)}) copy-start(bf16[4,112,768]{2,1,0:T(8,128)(2,1)S(1)} %pad_maximum_fusion.refs_0_) | copy-start | bytes 2064388
  38.9 26.4 %collective-permute-start.3 = (bf16[4,112,768]{2,1,0:T(8,128)(2,1)S(1)}, bf16[4,112,768]{2,1,0:T(8,128)(2,1)S(1)}, u32[]{:S(2)}, u32[]{:S(2)}) collective-permute-start(bf16[4,112,768]{2,1,0:T(8,128)(2,1)S(1)} %pad_maximum_fusion.refs_0_), channel_id=1, source_target_pairs={{0,8},{1,17},{2,10},{3,19},{4,12},{5,21},{6,14},{7,23},{8,0},{9,25... | collective-permute-start | bytes 2064392 | tf_op jit(solution)/shard_map/ppermute | solution.py:592
  40.4 26.9 %collective-permute-start.12 = (bf16[4,112,768]{2,1,0:T(8,128)(2,1)S(1)}, bf16[4,112,768]{2,1,0:T(8,128)(2,1)S(1)}, u32[]{:S(2)}, u32[]{:S(2)}) collective-permute-start(bf16[4,112,768]{2,1,0:T(8,128)(2,1)S(1)} %pad_maximum_fusion.refs_0_), channel_id=1, source_target_pairs={{0,16},{1,9},{2,18},{3,11},{4,20},{5,13},{6,22},{7,15},{8,24},{9,1... | collective-permute-start | bytes 2064392 | tf_op jit(solution)/shard_map/ppermute | solution.py:592
  41.9 11.1 %collective-permute-start.6 = (bf16[1,96,768]{2,1,0:T(8,128)(2,1)S(1)}, bf16[1,96,768]{2,1,0:T(8,128)(2,1)S(1)}, u32[]{:S(2)}, u32[]{:S(2)}) collective-permute-start(bf16[1,96,768]{2,1,0:T(8,128)(2,1)S(1)} %bitcast.54), channel_id=1, source_target_pairs={{0,6},{1,7},{2,4},{3,5},{4,2},{5,3},{6,0},{7,1},{8,14},{9,15},{10,... | collective-permute-start | bytes 442376 | tf_op jit(solution)/shard_map/ppermute | solution.py:592
  44.4 20.7 %collective-permute-start.5 = (bf16[1,96,768]{2,1,0:T(8,128)(2,1)S(1)}, bf16[1,96,768]{2,1,0:T(8,128)(2,1)S(1)}, u32[]{:S(2)}, u32[]{:S(2)}) collective-permute-start(bf16[1,96,768]{2,1,0:T(8,128)(2,1)S(1)} %bitcast.55), channel_id=1, source_target_pairs={{0,4},{1,5},{2,6},{3,7},{4,0},{5,1},{6,2},{7,3},{8,12},{9,13},{10,... | collective-permute-start | bytes 442376 | tf_op jit(solution)/shard_map/ppermute | solution.py:592
  44.4 20.7 %collective-permute-start.4 = (bf16[1,96,768]{2,1,0:T(8,128)(2,1)S(1)}, bf16[1,96,768]{2,1,0:T(8,128)(2,1)S(1)}, u32[]{:S(2)}, u32[]{:S(2)}) collective-permute-start(bf16[1,96,768]{2,1,0:T(8,128)(2,1)S(1)} %bitcast.56), channel_id=1, source_target_pairs={{0,2},{1,3},{2,0},{3,1},{4,6},{5,7},{6,4},{7,5},{8,10},{9,11},{10,... | collective-permute-start | bytes 442376 | tf_op jit(solution)/shard_map/ppermute | solution.py:592
  65.2 35.1 %copy-start.10 = (bf16[4,96,768]{2,1,0:T(8,128)(2,1)}, bf16[4,96,768]{2,1,0:T(8,128)(2,1)S(1)}, u32[]{:S(2)}) copy-start(bf16[4,96,768]{2,1,0:T(8,128)(2,1)S(1)} %pad_maximum_fusion.1.refs_0_) | copy-start | bytes 1769476
  65.2 28.9 %copy-start.15 = (bf16[4,112,768]{2,1,0:T(8,128)(2,1)}, bf16[4,112,768]{2,1,0:T(8,128)(2,1)S(1)}, u32[]{:S(2)}) copy-start(bf16[4,112,768]{2,1,0:T(8,128)(2,1)S(1)} %collective-permute-done.3.refs_1_) | copy-start | bytes 2064388
  65.2 23.0 %collective-permute-start.7 = (bf16[4,112,768]{2,1,0:T(8,128)(2,1)S(1)}, bf16[4,112,768]{2,1,0:T(8,128)(2,1)}, u32[]{:S(2)}, u32[]{:S(2)}) collective-permute-start(bf16[4,112,768]{2,1,0:T(8,128)(2,1)S(1)} %collective-permute-done.3.refs_1_), channel_id=1, source_target_pairs={{0,16},{1,9},{2,18},{3,11},{4,20},{5,13},{6,22},{7,15},{8,24},{9,1... | collective-permute-start | bytes 2064392 | tf_op jit(solution)/shard_map/ppermute | solution.py:592
  65.3 22.9 %collective-permute-start.8 = (bf16[4,96,768]{2,1,0:T(8,128)(2,1)S(1)}, bf16[4,96,768]{2,1,0:T(8,128)(2,1)S(1)}, u32[]{:S(2)}, u32[]{:S(2)}) collective-permute-start(bf16[4,96,768]{2,1,0:T(8,128)(2,1)S(1)} %pad_maximum_fusion.1.refs_0_), channel_id=1, source_target_pairs={{0,8},{1,17},{2,10},{3,19},{4,12},{5,21},{6,14},{7,23},{8,0},{9,25... | collective-permute-start | bytes 1769480 | tf_op jit(solution)/shard_map/ppermute | solution.py:592
  65.4 7.2 %collective-permute-start.11 = (bf16[1,96,768]{2,1,0:T(8,128)(2,1)S(1)}, bf16[1,96,768]{2,1,0:T(8,128)(2,1)S(1)}, u32[]{:S(2)}, u32[]{:S(2)}) collective-permute-start(bf16[1,96,768]{2,1,0:T(8,128)(2,1)S(1)} %bitcast.50), channel_id=1, source_target_pairs={{0,6},{1,7},{2,4},{3,5},{4,2},{5,3},{6,0},{7,1},{8,14},{9,15},{10,... | collective-permute-start | bytes 442376 | tf_op jit(solution)/shard_map/ppermute | solution.py:592
  67.3 20.3 %collective-permute-start.10 = (bf16[1,96,768]{2,1,0:T(8,128)(2,1)S(1)}, bf16[1,96,768]{2,1,0:T(8,128)(2,1)S(1)}, u32[]{:S(2)}, u32[]{:S(2)}) collective-permute-start(bf16[1,96,768]{2,1,0:T(8,128)(2,1)S(1)} %bitcast.51), channel_id=1, source_target_pairs={{0,4},{1,5},{2,6},{3,7},{4,0},{5,1},{6,2},{7,3},{8,12},{9,13},{10,... | collective-permute-start | bytes 442376 | tf_op jit(solution)/shard_map/ppermute | solution.py:592
  67.3 26.8 %copy-start.16 = (bf16[4,112,768]{2,1,0:T(8,128)(2,1)}, bf16[4,112,768]{2,1,0:T(8,128)(2,1)S(1)}, u32[]{:S(2)}) copy-start(bf16[4,112,768]{2,1,0:T(8,128)(2,1)S(1)} %collective-permute-done.12.refs_2_) | copy-start | bytes 2064388
  67.3 20.3 %collective-permute-start.9 = (bf16[1,96,768]{2,1,0:T(8,128)(2,1)S(1)}, bf16[1,96,768]{2,1,0:T(8,128)(2,1)S(1)}, u32[]{:S(2)}, u32[]{:S(2)}) collective-permute-start(bf16[1,96,768]{2,1,0:T(8,128)(2,1)S(1)} %bitcast.52), channel_id=1, source_target_pairs={{0,2},{1,3},{2,0},{3,1},{4,6},{5,7},{6,4},{7,5},{8,10},{9,11},{10,... | collective-permute-start | bytes 442376 | tf_op jit(solution)/shard_map/ppermute | solution.py:592
  72.6 17.7 %collective-permute-start.13 = (bf16[4,112,768]{2,1,0:T(8,128)(2,1)S(1)}, bf16[4,112,768]{2,1,0:T(8,128)(2,1)}, u32[]{:S(2)}, u32[]{:S(2)}) collective-permute-start(bf16[4,112,768]{2,1,0:T(8,128)(2,1)S(1)} %pad_maximum_fusion.refs_0_), channel_id=1, source_target_pairs={{0,1},{1,0},{2,3},{3,2},{4,5},{5,4},{6,7},{7,6},{8,9},{9,8},{10,11... | collective-permute-start | bytes 2064392 | tf_op jit(solution)/shard_map/ppermute | solution.py:592
  87.6 4.3 %collective-permute-start.14 = (bf16[4,112,768]{2,1,0:T(8,128)(2,1)S(1)}, bf16[4,112,768]{2,1,0:T(8,128)(2,1)}, u32[]{:S(2)}, u32[]{:S(2)}) collective-permute-start(bf16[4,112,768]{2,1,0:T(8,128)(2,1)S(1)} %collective-permute-done.3.refs_1_), channel_id=1, source_target_pairs={{0,1},{1,0},{2,3},{3,2},{4,5},{5,4},{6,7},{7,6},{8,9},{9,8},{10,11... | collective-permute-start | bytes 2064392 | tf_op jit(solution)/shard_map/ppermute | solution.py:592
  87.6 3.4 %collective-permute-start.15 = (bf16[4,112,768]{2,1,0:T(8,128)(2,1)S(1)}, bf16[4,112,768]{2,1,0:T(8,128)(2,1)}, u32[]{:S(2)}, u32[]{:S(2)}) collective-permute-start(bf16[4,112,768]{2,1,0:T(8,128)(2,1)S(1)} %collective-permute-done.12.refs_2_), channel_id=1, source_target_pairs={{0,1},{1,0},{2,3},{3,2},{4,5},{5,4},{6,7},{7,6},{8,9},{9,8},{10,11... | collective-permute-start | bytes 2064392 | tf_op jit(solution)/shard_map/ppermute | solution.py:592
  88.2 31.1 %copy-start.11 = (bf16[4,96,768]{2,1,0:T(8,128)(2,1)}, bf16[4,96,768]{2,1,0:T(8,128)(2,1)S(1)}, u32[]{:S(2)}) copy-start(bf16[4,96,768]{2,1,0:T(8,128)(2,1)S(1)} %pad_maximum_fusion.2.refs_8_) | copy-start | bytes 1769476
  89.2 3.4 %collective-permute-start.16 = (bf16[4,112,768]{2,1,0:T(8,128)(2,1)}, bf16[4,112,768]{2,1,0:T(8,128)(2,1)}, u32[]{:S(2)}, u32[]{:S(2)}) collective-permute-start(bf16[4,112,768]{2,1,0:T(8,128)(2,1)} %collective-permute-done.7.refs_3_), channel_id=1, source_target_pairs={{0,1},{1,0},{2,3},{3,2},{4,5},{5,4},{6,7},{7,6},{8,9},{9,8},{10,11... | collective-permute-start | bytes 2064392 | tf_op jit(solution)/shard_map/ppermute | solution.py:592
  89.8 15.2 %collective-permute-start.17 = (bf16[4,96,768]{2,1,0:T(8,128)(2,1)S(1)}, bf16[4,96,768]{2,1,0:T(8,128)(2,1)}, u32[]{:S(2)}, u32[]{:S(2)}) collective-permute-start(bf16[4,96,768]{2,1,0:T(8,128)(2,1)S(1)} %pad_maximum_fusion.1.refs_0_), channel_id=1, source_target_pairs={{0,16},{1,9},{2,18},{3,11},{4,20},{5,13},{6,22},{7,15},{8,24},{9,1... | collective-permute-start | bytes 1769480 | tf_op jit(solution)/shard_map/ppermute | solution.py:592
  90.3 34.7 %collective-permute-start.19 = (bf16[4,96,768]{2,1,0:T(8,128)(2,1)S(1)}, bf16[4,96,768]{2,1,0:T(8,128)(2,1)}, u32[]{:S(2)}, u32[]{:S(2)}) collective-permute-start(bf16[4,96,768]{2,1,0:T(8,128)(2,1)S(1)} %pad_maximum_fusion.1.refs_0_), channel_id=1, source_target_pairs={{0,1},{1,0},{2,3},{3,2},{4,5},{5,4},{6,7},{7,6},{8,9},{9,8},{10,11... | collective-permute-start | bytes 1769480 | tf_op jit(solution)/shard_map/ppermute | solution.py:592
  91.0 27.8 %collective-permute-start.24 = (bf16[4,96,768]{2,1,0:T(8,128)(2,1)S(1)}, bf16[4,96,768]{2,1,0:T(8,128)(2,1)}, u32[]{:S(2)}, u32[]{:S(2)}) collective-permute-start(bf16[4,96,768]{2,1,0:T(8,128)(2,1)S(1)} %pad_maximum_fusion.2.refs_8_), channel_id=1, source_target_pairs={{0,16},{1,9},{2,18},{3,11},{4,20},{5,13},{6,22},{7,15},{8,24},{9,1... | collective-permute-start | bytes 1769480 | tf_op jit(solution)/shard_map/ppermute | solution.py:592
  91.9 16.4 %collective-permute-start.22 = (bf16[4,96,768]{2,1,0:T(8,128)(2,1)S(1)}, bf16[4,96,768]{2,1,0:T(8,128)(2,1)}, u32[]{:S(2)}, u32[]{:S(2)}) collective-permute-start(bf16[4,96,768]{2,1,0:T(8,128)(2,1)S(1)} %pad_maximum_fusion.2.refs_8_), channel_id=1, source_target_pairs={{0,8},{1,17},{2,10},{3,19},{4,12},{5,21},{6,14},{7,23},{8,0},{9,25... | collective-permute-start | bytes 1769480 | tf_op jit(solution)/shard_map/ppermute | solution.py:592
  92.5 26.2 %collective-permute-start.18 = (bf16[4,96,768]{2,1,0:T(8,128)(2,1)}, bf16[4,96,768]{2,1,0:T(8,128)(2,1)}, u32[]{:S(2)}, u32[]{:S(2)}) collective-permute-start(bf16[4,96,768]{2,1,0:T(8,128)(2,1)} %copy-done.17), channel_id=1, source_target_pairs={{0,16},{1,9},{2,18},{3,11},{4,20},{5,13},{6,22},{7,15},{8,24},{9,1... | collective-permute-start | bytes 1769480 | tf_op jit(solution)/shard_map/ppermute | solution.py:592
  108.3 16.7 %collective-permute-start.25 = (bf16[4,96,768]{2,1,0:T(8,128)(2,1)}, bf16[4,96,768]{2,1,0:T(8,128)(2,1)S(1)}, u32[]{:S(2)}, u32[]{:S(2)}) collective-permute-start(bf16[4,96,768]{2,1,0:T(8,128)(2,1)} %collective-permute-done.22.refs_9_), channel_id=1, source_target_pairs={{0,16},{1,9},{2,18},{3,11},{4,20},{5,13},{6,22},{7,15},{8,24},{9,1... | collective-permute-start | bytes 1769480 | tf_op jit(solution)/shard_map/ppermute | solution.py:592
  118.8 6.7 %collective-permute-start.28 = (bf16[4,96,768]{2,1,0:T(8,128)(2,1)}, bf16[4,96,768]{2,1,0:T(8,128)(2,1)S(1)}, u32[]{:S(2)}, u32[]{:S(2)}) collective-permute-start(bf16[4,96,768]{2,1,0:T(8,128)(2,1)} %collective-permute-done.24.refs_10_), channel_id=1, source_target_pairs={{0,1},{1,0},{2,3},{3,2},{4,5},{5,4},{6,7},{7,6},{8,9},{9,8},{10,11... | collective-permute-start | bytes 1769480 | tf_op jit(solution)/shard_map/ppermute | solution.py:592
  118.8 6.8 %collective-permute-start.27 = (bf16[4,96,768]{2,1,0:T(8,128)(2,1)}, bf16[4,96,768]{2,1,0:T(8,128)(2,1)S(1)}, u32[]{:S(2)}, u32[]{:S(2)}) collective-permute-start(bf16[4,96,768]{2,1,0:T(8,128)(2,1)} %collective-permute-done.22.refs_9_), channel_id=1, source_target_pairs={{0,1},{1,0},{2,3},{3,2},{4,5},{5,4},{6,7},{7,6},{8,9},{9,8},{10,11... | collective-permute-start | bytes 1769480 | tf_op jit(solution)/shard_map/ppermute | solution.py:592
  119.3 6.7 %collective-permute-start.26 = (bf16[4,96,768]{2,1,0:T(8,128)(2,1)S(1)}, bf16[4,96,768]{2,1,0:T(8,128)(2,1)S(1)}, u32[]{:S(2)}, u32[]{:S(2)}) collective-permute-start(bf16[4,96,768]{2,1,0:T(8,128)(2,1)S(1)} %pad_maximum_fusion.2.refs_8_), channel_id=1, source_target_pairs={{0,1},{1,0},{2,3},{3,2},{4,5},{5,4},{6,7},{7,6},{8,9},{9,8},{10,11... | collective-permute-start | bytes 1769480 | tf_op jit(solution)/shard_map/ppermute | solution.py:592
  125.0 2.2 collective-permute-start.23
  125.0 3.9 %collective-permute-start.21 = (bf16[4,96,768]{2,1,0:T(8,128)(2,1)}, bf16[4,96,768]{2,1,0:T(8,128)(2,1)S(1)}, u32[]{:S(2)}, u32[]{:S(2)}) collective-permute-start(bf16[4,96,768]{2,1,0:T(8,128)(2,1)} %collective-permute-done.17.refs_2_), channel_id=1, source_target_pairs={{0,1},{1,0},{2,3},{3,2},{4,5},{5,4},{6,7},{7,6},{8,9},{9,8},{10,11... | collective-permute-start | bytes 1769480 | tf_op jit(solution)/shard_map/ppermute | solution.py:592
  125.5 4.2 %collective-permute-start.20 = (bf16[4,96,768]{2,1,0:T(8,128)(2,1)}, bf16[4,96,768]{2,1,0:T(8,128)(2,1)S(1)}, u32[]{:S(2)}, u32[]{:S(2)}) collective-permute-start(bf16[4,96,768]{2,1,0:T(8,128)(2,1)} %copy-done.17), channel_id=1, source_target_pairs={{0,1},{1,0},{2,3},{3,2},{4,5},{5,4},{6,7},{7,6},{8,9},{9,8},{10,11... | collective-permute-start | bytes 1769480 | tf_op jit(solution)/shard_map/ppermute | solution.py:592
  125.6 4.1 %collective-permute-start.29 = (bf16[4,96,768]{2,1,0:T(8,128)(2,1)S(1)}, bf16[4,96,768]{2,1,0:T(8,128)(2,1)S(1)}, u32[]{:S(2)}, u32[]{:S(2)}) collective-permute-start(bf16[4,96,768]{2,1,0:T(8,128)(2,1)S(1)} %collective-permute-done.25.refs_11_), channel_id=1, source_target_pairs={{0,1},{1,0},{2,3},{3,2},{4,5},{5,4},{6,7},{7,6},{8,9},{9,8},{10,11... | collective-permute-start | bytes 1769480 | tf_op jit(solution)/shard_map/ppermute | solution.py:592
  158.0 9.4 %collective-permute-start.30 = (bf16[16,64,1792]{2,1,0:T(8,128)(2,1)}, bf16[16,64,1792]{2,1,0:T(8,128)(2,1)}, u32[]{:S(2)}, u32[]{:S(2)}) collective-permute-start(bf16[16,64,1792]{2,1,0:T(8,128)(2,1)} %get-tuple-element.143), channel_id=1, source_target_pairs={{0,1},{1,0},{2,3},{3,2},{4,5},{5,4},{6,7},{7,6},{8,9},{9,8},{10,11... | collective-permute-start | bytes 11010056 | tf_op jit(solution)/shard_map/ppermute | solution.py:592
  170.6 43.6 %collective-permute-start.34 = (bf16[8,64,1792]{2,1,0:T(8,128)(2,1)}, bf16[8,64,1792]{2,1,0:T(8,128)(2,1)}, u32[]{:S(2)}, u32[]{:S(2)}) collective-permute-start(bf16[8,64,1792]{2,1,0:T(8,128)(2,1)} %add_convert_fusion), channel_id=1, source_target_pairs={{0,16},{1,9},{2,18},{3,11},{4,20},{5,13},{6,22},{7,15},{8,24},{9,1... | collective-permute-start | bytes 5505032 | tf_op jit(solution)/shard_map/ppermute | solution.py:592
  171.1 52.5 %collective-permute-start.31 = (bf16[64,4800]{1,0:T(8,128)(2,1)}, bf16[64,4800]{1,0:T(8,128)(2,1)}, u32[]{:S(2)}, u32[]{:S(2)}) collective-permute-start(bf16[64,4800]{1,0:T(8,128)(2,1)} %get-tuple-element.161), channel_id=1, source_target_pairs={{0,24},{8,16},{16,8},{24,0},{1,25},{9,17},{17,9},{25,1},{2,26},{10... | collective-permute-start | bytes 1843208 | tf_op jit(solution)/shard_map/ppermute | solution.py:791
  172.4 48.4 %collective-permute-start.32 = (bf16[64,4800]{1,0:T(8,128)(2,1)}, bf16[64,4800]{1,0:T(8,128)(2,1)}, u32[]{:S(2)}, u32[]{:S(2)}) collective-permute-start(bf16[64,4800]{1,0:T(8,128)(2,1)} %get-tuple-element.162), channel_id=1, source_target_pairs={{0,16},{8,24},{16,0},{24,8},{1,17},{9,25},{17,1},{25,9},{2,18},{10... | collective-permute-start | bytes 1843208 | tf_op jit(solution)/shard_map/ppermute | solution.py:791
  173.5 40.7 %collective-permute-start.33 = (bf16[64,4800]{1,0:T(8,128)(2,1)}, bf16[64,4800]{1,0:T(8,128)(2,1)}, u32[]{:S(2)}, u32[]{:S(2)}) collective-permute-start(bf16[64,4800]{1,0:T(8,128)(2,1)} %get-tuple-element.163), channel_id=1, source_target_pairs={{0,8},{8,0},{16,24},{24,16},{1,9},{9,1},{17,25},{25,17},{2,10},{10... | collective-permute-start | bytes 1843208 | tf_op jit(solution)/shard_map/ppermute | solution.py:791
  223.6 16.9 %collective-permute-start.36 = (bf16[4,64,1792]{2,1,0:T(8,128)(2,1)}, bf16[4,64,1792]{2,1,0:T(8,128)(2,1)}, u32[]{:S(2)}, u32[]{:S(2)}) collective-permute-start(bf16[4,64,1792]{2,1,0:T(8,128)(2,1)} %add_convert_fusion.1), channel_id=1, source_target_pairs={{0,8},{1,17},{2,10},{3,19},{4,12},{5,21},{6,14},{7,23},{8,0},{9,25... | collective-permute-start | bytes 2752520 | tf_op jit(solution)/shard_map/ppermute | solution.py:592
  227.6 15.8 %copy-start.1 = (bf16[4,96,1536]{2,1,0:T(8,128)(2,1)S(1)}, bf16[4,96,1536]{2,1,0:T(8,128)(2,1)}, u32[]{:S(2)}) copy-start(bf16[4,96,1536]{2,1,0:T(8,128)(2,1)} %get-tuple-element.185) | copy-start | bytes 3538948
  227.6 15.8 %collective-permute-start.38 = (bf16[4,96,1536]{2,1,0:T(8,128)(2,1)}, bf16[4,96,1536]{2,1,0:T(8,128)(2,1)S(1)}, u32[]{:S(2)}, u32[]{:S(2)}) collective-permute-start(bf16[4,96,1536]{2,1,0:T(8,128)(2,1)} %get-tuple-element.173), channel_id=1, source_target_pairs={{0,1},{1,0},{2,3},{3,2},{4,5},{5,4},{6,7},{7,6},{8,9},{9,8},{10,11... | collective-permute-start | bytes 3538952 | tf_op jit(solution)/shard_map/ppermute | solution.py:592
  230.6 23.7 %collective-permute-start.35 = (bf16[64,2304]{1,0:T(8,128)(2,1)}, bf16[64,2304]{1,0:T(8,128)(2,1)S(1)}, u32[]{:S(2)}, u32[]{:S(2)}) collective-permute-start(bf16[64,2304]{1,0:T(8,128)(2,1)} %get-tuple-element.171), channel_id=1, source_target_pairs={{0,8},{8,0},{16,24},{24,16},{1,9},{9,1},{17,25},{25,17},{2,10},{10... | collective-permute-start | bytes 884744 | tf_op jit(solution)/shard_map/ppermute | solution.py:791
  232.3 22.0 %collective-permute-start.39 = (bf16[64,2304]{1,0:T(8,128)(2,1)}, bf16[64,2304]{1,0:T(8,128)(2,1)S(1)}, u32[]{:S(2)}, u32[]{:S(2)}) collective-permute-start(bf16[64,2304]{1,0:T(8,128)(2,1)} %get-tuple-element.178), channel_id=1, source_target_pairs={{0,16},{8,24},{16,0},{24,8},{1,17},{9,25},{17,1},{25,9},{2,18},{10... | collective-permute-start | bytes 884744 | tf_op jit(solution)/shard_map/ppermute | solution.py:791
  232.7 22.5 %collective-permute-start.40 = (bf16[64,2304]{1,0:T(8,128)(2,1)}, bf16[64,2304]{1,0:T(8,128)(2,1)S(1)}, u32[]{:S(2)}, u32[]{:S(2)}) collective-permute-start(bf16[64,2304]{1,0:T(8,128)(2,1)} %get-tuple-element.181), channel_id=1, source_target_pairs={{0,24},{8,16},{16,8},{24,0},{1,25},{9,17},{17,9},{25,1},{2,26},{10... | collective-permute-start | bytes 884744 | tf_op jit(solution)/shard_map/ppermute | solution.py:791
  242.0 12.3 %collective-permute-start.37 = (bf16[2,64,1792]{2,1,0:T(8,128)(2,1)S(1)}, bf16[2,64,1792]{2,1,0:T(8,128)(2,1)S(1)}, u32[]{:S(2)}, u32[]{:S(2)}) collective-permute-start(bf16[2,64,1792]{2,1,0:T(8,128)(2,1)S(1)} %add_convert_fusion.5), channel_id=1, source_target_pairs={{0,2},{1,3},{6,4},{7,5},{8,10},{9,11},{14,12},{15,13},{16,18},{17,... | collective-permute-start | bytes 1376264 | tf_op jit(solution)/shard_map/ppermute | solution.py:636
  243.4 11.9 %copy-start.3 = (bf16[4,96,1536]{2,1,0:T(8,128)(2,1)}, bf16[4,96,1536]{2,1,0:T(8,128)(2,1)S(1)}, u32[]{:S(2)}) copy-start(bf16[4,96,1536]{2,1,0:T(8,128)(2,1)S(1)} %collective-permute-done.38) | copy-start | bytes 3538948
  244.5 17.3 %collective-permute-start.43 = (bf16[2,96,1536]{2,1,0:T(8,128)(2,1)}, bf16[2,96,1536]{2,1,0:T(8,128)(2,1)}, u32[]{:S(2)}, u32[]{:S(2)}) collective-permute-start(bf16[2,96,1536]{2,1,0:T(8,128)(2,1)} %add_convert_fusion.3), channel_id=1, source_target_pairs={{0,2},{1,3},{6,4},{7,5},{8,10},{9,11},{14,12},{15,13},{16,18},{17,... | collective-permute-start | bytes 1769480 | tf_op jit(solution)/shard_map/ppermute | solution.py:636
  256.0 8.0 %collective-permute-start.42 = (bf16[2,64,1792]{2,1,0:T(8,128)(2,1)}, bf16[2,64,1792]{2,1,0:T(8,128)(2,1)S(1)}, u32[]{:S(2)}, u32[]{:S(2)}) collective-permute-start(bf16[2,64,1792]{2,1,0:T(8,128)(2,1)} %add_convert_fusion.4), channel_id=1, source_target_pairs={{2,4},{3,5},{4,2},{5,3},{10,12},{11,13},{12,10},{13,11},{18,20},{1... | collective-permute-start | bytes 1376264 | tf_op jit(solution)/shard_map/ppermute | solution.py:636
  259.9 11.2 %collective-permute-start.41 = (bf16[4,112,768]{2,1,0:T(8,128)(2,1)}, bf16[4,112,768]{2,1,0:T(8,128)(2,1)S(1)}, u32[]{:S(2)}, u32[]{:S(2)}) collective-permute-start(bf16[4,112,768]{2,1,0:T(8,128)(2,1)} %get-tuple-element.184), channel_id=1, source_target_pairs={{0,1},{1,0},{2,3},{3,2},{4,5},{5,4},{6,7},{7,6},{8,9},{9,8},{10,11... | collective-permute-start | bytes 2064392 | tf_op jit(solution)/shard_map/ppermute | solution.py:592
  263.1 10.0 %copy-start.2 = (bf16[4,96,1536]{2,1,0:T(8,128)(2,1)S(1)}, bf16[4,96,1536]{2,1,0:T(8,128)(2,1)}, u32[]{:S(2)}) copy-start(bf16[4,96,1536]{2,1,0:T(8,128)(2,1)} %get-tuple-element.185) | copy-start | bytes 3538948
  263.1 10.0 %copy-start.4 = (bf16[4,96,1536]{2,1,0:T(8,128)(2,1)S(1)}, bf16[4,96,1536]{2,1,0:T(8,128)(2,1)}, u32[]{:S(2)}) copy-start(bf16[4,96,1536]{2,1,0:T(8,128)(2,1)} %copy-done.3) | copy-start | bytes 3538948
  263.2 10.0 %collective-permute-start.45 = (bf16[2,96,1536]{2,1,0:T(8,128)(2,1)S(1)}, bf16[2,96,1536]{2,1,0:T(8,128)(2,1)S(1)}, u32[]{:S(2)}, u32[]{:S(2)}) collective-permute-start(bf16[2,96,1536]{2,1,0:T(8,128)(2,1)S(1)} %add_convert_fusion.2), channel_id=1, source_target_pairs={{2,4},{3,5},{4,2},{5,3},{10,12},{11,13},{12,10},{13,11},{18,20},{1... | collective-permute-start | bytes 1769480 | tf_op jit(solution)/shard_map/ppermute | solution.py:636
  265.6 19.4 %collective-permute-start.47 = (bf16[64,1792]{1,0:T(8,128)(2,1)S(1)}, bf16[64,1792]{1,0:T(8,128)(2,1)S(1)}, u32[]{:S(2)}, u32[]{:S(2)}) collective-permute-start(bf16[64,1792]{1,0:T(8,128)(2,1)S(1)} %fusion.4), channel_id=1, source_target_pairs={{0,2},{1,3},{2,0},{3,1},{4,6},{5,7},{6,4},{7,5},{8,10},{9,11},{10,... | collective-permute-start | bytes 688136 | tf_op jit(solution)/shard_map/ppermute | solution.py:592
  271.2 13.7 %collective-permute-start.44 = (bf16[2,112,768]{2,1,0:T(8,128)(2,1)S(1)}, bf16[2,112,768]{2,1,0:T(8,128)(2,1)S(1)}, u32[]{:S(2)}, u32[]{:S(2)}) collective-permute-start(bf16[2,112,768]{2,1,0:T(8,128)(2,1)S(1)} %add_convert_fusion.7), channel_id=1, source_target_pairs={{0,2},{1,3},{6,4},{7,5},{8,10},{9,11},{14,12},{15,13},{16,18},{17,... | collective-permute-start | bytes 1032200 | tf_op jit(solution)/shard_map/ppermute | solution.py:636
  274.1 15.0 %copy-start.7 = (bf16[4,112,768]{2,1,0:T(8,128)(2,1)S(1)}, bf16[4,112,768]{2,1,0:T(8,128)(2,1)}, u32[]{:S(2)}) copy-start(bf16[4,112,768]{2,1,0:T(8,128)(2,1)} %get-tuple-element.183) | copy-start | bytes 2064388
  274.1 15.0 %copy-start.9 = (bf16[4,112,768]{2,1,0:T(8,128)(2,1)S(1)}, bf16[4,112,768]{2,1,0:T(8,128)(2,1)}, u32[]{:S(2)}) copy-start(bf16[4,112,768]{2,1,0:T(8,128)(2,1)} %copy-done.8) | copy-start | bytes 2064388
  274.1 18.0 %collective-permute-start.49 = (bf16[96,1536]{1,0:T(8,128)(2,1)}, bf16[96,1536]{1,0:T(8,128)(2,1)}, u32[]{:S(2)}, u32[]{:S(2)}) collective-permute-start(bf16[96,1536]{1,0:T(8,128)(2,1)} %fusion.3), channel_id=1, source_target_pairs={{0,2},{1,3},{2,0},{3,1},{4,6},{5,7},{6,4},{7,5},{8,10},{9,11},{10,... | collective-permute-start | bytes 884744 | tf_op jit(solution)/shard_map/ppermute | solution.py:592
  285.1 4.0 %collective-permute-start.46 = (bf16[2,112,768]{2,1,0:T(8,128)(2,1)S(1)}, bf16[2,112,768]{2,1,0:T(8,128)(2,1)S(1)}, u32[]{:S(2)}, u32[]{:S(2)}) collective-permute-start(bf16[2,112,768]{2,1,0:T(8,128)(2,1)S(1)} %add_convert_fusion.6), channel_id=1, source_target_pairs={{2,4},{3,5},{4,2},{5,3},{10,12},{11,13},{12,10},{13,11},{18,20},{1... | collective-permute-start | bytes 1032200 | tf_op jit(solution)/shard_map/ppermute | solution.py:636
  293.2 8.9 %collective-permute-start.48 = (bf16[112,768]{1,0:T(8,128)(2,1)S(1)}, bf16[112,768]{1,0:T(8,128)(2,1)S(1)}, u32[]{:S(2)}, u32[]{:S(2)}) collective-permute-start(bf16[112,768]{1,0:T(8,128)(2,1)S(1)} %fusion.5), channel_id=1, source_target_pairs={{0,2},{1,3},{2,0},{3,1},{4,6},{5,7},{6,4},{7,5},{8,10},{9,11},{10,... | collective-permute-start | bytes 516104 | tf_op jit(solution)/shard_map/ppermute | solution.py:592
  (16 other events, 53.5 us)
Sparse Core Ops, SparseCore 0:
  11.5 88.5 all-gather.2
where the time goes:
time: 315 us; the launch traced here: 314 us
  waiting for transfers between devices  141 us (45%)
  Pallas kernels  62.3 us (20%)
  starting transfers between devices  62.1 us (20%)
  other arithmetic  17.3 us (5%)
  local copies, waits for them, and re-layouts  16.6 us (5%)
  between operations  14.6 us (5%)
    ppermute x38, waiting for transfers between devices, exchange(): return lax.ppermute(value, ('section', 'dp'), pairs)  125 us
    pallas_call x9, Pallas kernels, call(): pl.pallas_call(body, out_shape=[jax.ShapeDtypeStruct(shape, dtype) for sh...  62.3 us
    ppermute x38, starting transfers between devices, exchange(): return lax.ppermute(value, ('section', 'dp'), pairs)  47.4 us
    ppermute x6, waiting for transfers between devices, move(): return lax.ppermute(value, ('section', 'dp'), pairs)  9.44 us
    unnamed x62, local copies, waits for them, and re-layouts  8.29 us
    ppermute x6, starting transfers between devices, move(): return lax.ppermute(value, ('section', 'dp'), pairs)  7.59 us
    ppermute x6, starting transfers between devices, to_section(): lax.ppermute(members[i], 'section', [(s, s ^ i) for s in range(SEC)])  6.98 us
    ppermute x6, waiting for transfers between devices, to_section(): lax.ppermute(members[i], 'section', [(s, s ^ i) for s in range(SEC)])  6.68 us
  transfers between devices with their start and end apart: 51, of which 21 were waited for; matrix products, arithmetic and copies ran while one was open for 6% of the time, Pallas kernels for 13%

commit v1 on v0

--- a/solution.py
+++ b/solution.py
@@ -216,41 +216,25 @@
     h_ref[...] = (inputs + result + vec_ref[5:6]).astype(BF)
 
 
-def enc_ffn_fwd(inn, table, h_ref, vec_ref, upb_ref, *refs):
-    (ups, downs), (o_ref, a_ref, r_ref, u_ref, v_ref, sem_u, sem_v) = take(refs, inn)
-    copies_u = block_copies(ups, table, inn[0][1], (0, 96), (0, 768), rows_place(u_ref, 96), sem_u)
-    copies_v = []
-    for half in range(2):
-        copies_v += block_copies(
-            downs, table, inn[1][1], (0, 96), (384 * half, 384), turned_place(v_ref, 192, 384, 96 * half, 96), sem_v
-        )
-    inputs = h_ref[...].astype(F32)
-    normed, _ = norm_stats(inputs)
-    low = (normed * vec_ref[1:2] + vec_ref[6:7]).astype(BF)
-    a_ref[...] = low
-    wait_all(copies_u)
-    active = []
-    for s in range(SEC):
-        lanes = slice(768 * s, 768 * s + 768)
-        hidden = dot(low, u_ref[s]) + upb_ref[:, lanes]
-        r_ref[:, lanes] = hidden
-        active.append(gelu_parts(hidden)[0].astype(BF))
-    wait_all(copies_v)
-    result = dot_nt(jnp.concatenate(active, axis=1), v_ref[...])
-    o_ref[...] = (inputs + result + vec_ref[7:8]).astype(BF)
-
-
 def placing(keep_ref):
     keep = jnp.concatenate([keep_ref[...], jnp.full((1, ENC_ROWS - 49), -1, jnp.int32)], axis=1)
     place = lax.broadcasted_iota(jnp.int32, (DEC_ROWS, ENC_ROWS), 0)
     return jnp.where(place == keep, 1.0, 0.0).astype(F32)
 
 
-def dec_both(inn, outs, table, h_ref, keep_ref, pos_ref, ct_ref, vec_ref, upb_ref, *refs):
-    (pieces,), (y_ref, dx_ref, gvec_ref, gupb_ref, *rest) = take(refs, inn)
-    (grads,), rest = take(rest, (outs,))
-    e_ref, w_ref, u_ref, v_ref, ge_ref, gw_ref, gu_ref, gv_ref, p_ref, sem_e, sem_w, sem_u, sem_v, sem_o = rest
-    start = inn[0][1]
+def middle(inn, outs, table, h_ref, keep_ref, pos_ref, ct_ref, enc_ref, upe_ref, dec_ref, upd_ref, *refs):
+    (ups, downs, pieces), rest = take(refs, inn)
+    y_ref, dx_ref, genc_ref, gupe_ref, gdec_ref, gupd_ref, *rest = rest
+    (sends, grads), rest = take(rest, ((SEC, 0), outs))
+    eu_ref, ev_ref, r_ref, dr_ref, df_ref, e_ref, w_ref, u_ref, v_ref, ge_ref, gw_ref, gu_ref, gv_ref, p_ref = rest[:14]
+    sem_eu, sem_ev, sem_e, sem_w, sem_u, sem_v, sem_o = rest[14:]
+    copies_eu = block_copies(ups, table, inn[0][1], (0, 96), (0, 768), rows_place(eu_ref, 96), sem_eu)
+    copies_ev = []
+    for half in range(2):
+        copies_ev += block_copies(
+            downs, table, inn[1][1], (0, 96), (384 * half, 384), turned_place(ev_ref, 192, 384, 96 * half, 96), sem_ev
+        )
+    start = inn[2][1]
     copies_e = block_copies(pieces, table, start, (0, 64), (1536, 128), part_place(e_ref, 0, 64), sem_e)
     copies_e += block_copies(pieces, table, start, (0, 32), (1664, 128), part_place(e_ref, 64, 32), sem_e)
     copies_w = block_copies(pieces, table, start, (0, 64), (0, 512), rows_place(w_ref, 64), sem_w)
@@ -260,38 +244,56 @@
         copies_v += block_copies(
             pieces, table, start, (0, 64), (1024 + 256 * half, 256), turned_place(v_ref, 128, 256, 64 * half, 64), sem_v
         )
+    inputs_e = h_ref[...].astype(F32)
+    normed_e, scale_e = norm_stats(inputs_e)
+    low_e = (normed_e * enc_ref[1:2] + enc_ref[6:7]).astype(BF)
+    wait_all(copies_eu)
+    active = []
+    for s in range(SEC):
+        lanes = slice(768 * s, 768 * s + 768)
+        hidden = dot(low_e, eu_ref[s]) + upe_ref[:, lanes]
+        r_ref[:, lanes] = hidden
+        active.append(gelu_parts(hidden)[0].astype(BF))
+        for r in range(SEC):
+            sends[r][:, 768 + 768 * s : 1536 + 768 * s] = active[s]
+    for r in range(SEC):
+        sends[r][:, 0:768] = low_e
+    wait_all(copies_ev)
+    result = dot_nt(jnp.concatenate(active, axis=1), ev_ref[...])
+    after_e = (inputs_e + result + enc_ref[7:8]).astype(BF)
+
     copies = []
 
     def give(lanes, place, rows=64):
         copies.extend(block_copies(grads, table, outs[1], (0, rows), lanes, place, sem_o, True))
 
-    before = h_ref[...]
+    before = after_e
     onehot = placing(keep_ref)
     uncovered = 1.0 - jnp.sum(onehot, axis=1, keepdims=True)
     wait_all(copies_e)
-    embedded = dot(before, jnp.concatenate([e_ref[s] for s in range(SEC)], axis=1)) + vec_ref[2:3]
+    embedded = dot(before, jnp.concatenate([e_ref[s] for s in range(SEC)], axis=1)) + dec_ref[2:3]
     placed = jnp.dot(onehot, embedded, precision=lax.Precision.HIGHEST, preferred_element_type=F32)
-    placed = placed + uncovered * vec_ref[3:4] + padded(pos_ref[...], DEC_ROWS)
+    placed = placed + uncovered * dec_ref[3:4] + padded(pos_ref[...], DEC_ROWS)
     normed_a, scale_a = norm_stats(placed)
-    low_a = (normed_a * vec_ref[0:1] + vec_ref[4:5]).astype(BF)
+    low_a = (normed_a * dec_ref[0:1] + dec_ref[4:5]).astype(BF)
     wait_all(copies_w)
     packed = jnp.concatenate([dot(low_a, w_ref[s, :, 0:384]) for s in range(SEC)], axis=1)
     zero = jnp.zeros((1, 512), F32)
-    packed = (packed + jnp.concatenate([vec_ref[5:6], zero, vec_ref[6:7]], axis=1)).astype(BF)
+    packed = (packed + jnp.concatenate([dec_ref[5:6], zero, dec_ref[6:7]], axis=1)).astype(BF)
     mixed = attention_fwd(packed, 512, 32, 196, p_ref)
     w_out = jnp.concatenate([w_ref[s, :, 384:512] for s in range(SEC)], axis=1)
-    inputs = (placed + dot(mixed, w_out) + vec_ref[7:8]).astype(BF).astype(F32)
+    inputs = (placed + dot(mixed, w_out) + dec_ref[7:8]).astype(BF).astype(F32)
 
     normed, scale = norm_stats(inputs)
-    low = (normed * vec_ref[1:2] + vec_ref[8:9]).astype(BF)
+    low = (normed * dec_ref[1:2] + dec_ref[8:9]).astype(BF)
     wait_all(copies_u)
     hidden, active = [], []
     for s in range(SEC):
-        hidden.append(dot(low, u_ref[s]) + upb_ref[:, 512 * s : 512 * s + 512])
+        hidden.append(dot(low, u_ref[s]) + upd_ref[:, 512 * s : 512 * s + 512])
         active.append(gelu_parts(hidden[s])[0].astype(BF))
     active = jnp.concatenate(active, axis=1)
     wait_all(copies_v)
-    result = inputs + dot_nt(active, v_ref[...]) + vec_ref[9:10]
+    result = inputs + dot_nt(active, v_ref[...]) + dec_ref[9:10]
     y_ref[0] = result[:196]
 
     grad_low = padded(ct_ref[0].astype(F32), DEC_ROWS).astype(BF)
@@ -303,13 +305,13 @@
         lanes = slice(512 * s, 512 * s + 512)
         share = gelu_parts(hidden[s])[1]
         grad_hidden = (dot(grad_low, v_ref[:, lanes]) * gelu_slope(hidden[s], share)).astype(BF)
-        gupb_ref[:, lanes] = column_sum(grad_hidden.astype(F32))
+        gupd_ref[:, lanes] = column_sum(grad_hidden.astype(F32))
         gu_ref[s] = dot_tn(low, grad_hidden).astype(BF)
         grad_normed = grad_normed + dot_nt(grad_hidden, u_ref[s])
     give((0, 512), rows_place(gu_ref, 64))
     grad_out = grad_low.astype(F32)
     sums_f = [column_sum(grad_normed * normed), column_sum(grad_normed), column_sum(grad_out)]
-    grad = (grad_out + norm_back(grad_normed, normed, scale, vec_ref[1:2])).astype(BF)
+    grad = (grad_out + norm_back(grad_normed, normed, scale, dec_ref[1:2])).astype(BF)
 
     grad_out = grad.astype(F32)
     for s in range(SEC):
@@ -322,7 +324,7 @@
         gw_ref[s, :, 0:384] = dot_tn(low_a, part).astype(BF)
         grad_normed = grad_normed + dot_nt(part, w_ref[s, :, 0:384])
     give((1024, 512), rows_place(gw_ref, 64))
-    grad_placed = grad_out + norm_back(grad_normed, normed_a, scale_a, vec_ref[0:1])
+    grad_placed = grad_out + norm_back(grad_normed, normed_a, scale_a, dec_ref[0:1])
     grad_token = column_sum(uncovered * grad_placed)
     grad_embedded = lax.dot_general(
         onehot, grad_placed, (((0,), (0,)), ((), ())), precision=lax.Precision.HIGHEST, preferred_element_type=F32
@@ -331,9 +333,9 @@
         ge_ref[s] = dot_tn(before, grad_embedded[:, 128 * s : 128 * s + 128]).astype(BF)
     give((1536, 128), part_place(ge_ref, 0, 64))
     give((1664, 128), part_place(ge_ref, 64, 32), 32)
-    dx_ref[...] = dot_nt(grad_embedded, jnp.concatenate([e_ref[s] for s in range(SEC)], axis=1)).astype(BF)
+    grad_e = dot_nt(grad_embedded, jnp.concatenate([e_ref[s] for s in range(SEC)], axis=1)).astype(BF)
     totals = column_sum(grad_packed.astype(F32))
-    gvec_ref[...] = jnp.concatenate(
+    gdec_ref[...] = jnp.concatenate(
         [
             column_sum(grad_normed * normed_a),
             sums_f[0],
@@ -347,48 +349,28 @@
         ],
         axis=0,
     )
-    wait_all(copies)
-
-
-def enc_ffn_bwd(inn, table, dh_ref, h_ref, a_ref, r_ref, vec_ref, *refs):
-    (ups, downs), rest = take(refs, inn)
-    dx_ref, gvec_ref, gupb_ref, *rest = rest
-    (sends,), (u_ref, v_ref, dr_ref, df_ref, sem_u, sem_v) = take(rest, ((SEC, 0),))
-    copies_v = []
-    for half in range(2):
-        copies_v += block_copies(
-            downs, table, inn[1][1], (0, 96), (384 * half, 384), turned_place(v_ref, 192, 384, 96 * half, 96), sem_v
-        )
-    copies_u = block_copies(ups, table, inn[0][1], (0, 96), (0, 768), rows_place(u_ref, 96), sem_u)
-    grad = dh_ref[...]
-    grad_out = grad.astype(F32)
-    low = a_ref[...]
-    for s in range(SEC):
-        df_ref[s] = grad[:, 192 * s : 192 * s + 192]
-        sends[s][:, 0:768] = low
-    wait_all(copies_v)
-    wait_all(copies_u)
+
+    grad_out = grad_e.astype(F32)
+    for s in range(SEC):
+        df_ref[s] = grad_e[:, 192 * s : 192 * s + 192]
     grad_normed = jnp.zeros((ENC_ROWS, 768), F32)
     for s in range(SEC):
         lanes = slice(768 * s, 768 * s + 768)
         hidden = r_ref[:, lanes]
-        active, share = gelu_parts(hidden)
-        active = active.astype(BF)
-        for r in range(SEC):
-            sends[r][:, 768 + 768 * s : 1536 + 768 * s] = active
-        grad_hidden = (dot(grad, v_ref[:, lanes]) * gelu_slope(hidden, share)).astype(BF)
-        gupb_ref[:, lanes] = column_sum(grad_hidden.astype(F32))
+        share = gelu_parts(hidden)[1]
+        grad_hidden = (dot(grad_e, ev_ref[:, lanes]) * gelu_slope(hidden, share)).astype(BF)
+        gupe_ref[:, lanes] = column_sum(grad_hidden.astype(F32))
         dr_ref[s] = grad_hidden
-        grad_normed = grad_normed + dot_nt(grad_hidden, u_ref[s])
+        grad_normed = grad_normed + dot_nt(grad_hidden, eu_ref[s])
     here = table[SECTION]
     for r in range(SEC):
         sends[r][:, 3840:4608] = dr_ref[here ^ r]
         sends[r][:, 4608:4800] = df_ref[here ^ r]
-    normed, scale = norm_stats(h_ref[...].astype(F32))
-    gvec_ref[...] = jnp.concatenate(
-        [column_sum(grad_normed * normed), column_sum(grad_normed), column_sum(grad_out)], axis=0
-    )
-    dx_ref[...] = (grad_out + norm_back(grad_normed, normed, scale, vec_ref[1:2])).astype(BF)
+    genc_ref[...] = jnp.concatenate(
+        [column_sum(grad_normed * normed_e), column_sum(grad_normed), column_sum(grad_out)], axis=0
+    )
+    dx_ref[...] = (grad_out + norm_back(grad_normed, normed_e, scale_e, enc_ref[1:2])).astype(BF)
+    wait_all(copies)
 
 
 def enc_att_bwd(inn, table, dh_ref, x_ref, a_ref, k_ref, z_ref, vec_ref, ge_ref, gue_ref, gd_ref, gud_ref, *refs):
@@ -601,9 +583,17 @@
     return ((device & 30) | core) ^ flips
 
 
-EVENTS = """
-aZ1 aZ2 aZ3 aC aP aQ bZ1 bZ2 bZ3 bC a1 aR bP bQ cZ1 cZ2 cZ3 a2 a3 cC b1 bR cP cQ a4 F1 b2 b3 cR b4 c1 c2 c3 c4
-"""
+EVENTS = (
+    "aZ1 aZ2 aZ3 aC",
+    "aP aQ bZ1 bZ2",
+    "bZ3 bC a1 aR",
+    "bP bQ cZ1 cZ2",
+    "cZ3 a2 a3 cC",
+    "b1 bR cP cQ",
+    "a4 F1 b2 b3",
+    "cR b4 c1 c2",
+    "c3 c4",
+)
 
 
 class Order:
@@ -703,15 +693,6 @@
             body, outs, [enc_sq, dma], table, inputs, enc_vec, *operands(att_e), memory="svv" + spaces(att_e)
         )
 
-    def run_f2(h1, up_e, down_e, enc_vec, enc_upb):
-        return call(
-            partial(enc_ffn_fwd, used(up_e, down_e)),
-            [(enc_shape, BF, "v"), (enc_shape, BF, "v"), ((ENC_ROWS, 3072), F32, "v")],
-            [enc_sq, enc_wide, dma, dma],
-            table, h1, enc_vec, enc_upb, *operands(up_e, down_e),
-            memory="svvv" + spaces(up_e, down_e),
-        )
-
     if fast:
         qkv_e, out_e, mat_up, mat_down, embed, qkv_d, out_d, up_d, down_d = parameters[:9]
         (first,) = call(
@@ -729,7 +710,7 @@
         def pieces(name):
             return ([got[name + part] for part in ("C", "P", "Q", "R", "1", "2", "3", "4")], IN_PATH)
 
-        for event in EVENTS.split():
+        for event in " ".join(EVENTS).split():
             name, part = event[0], event[1:]
             if event == "F1":
                 got[event] = list(run_f1(pieces("a"), step.after(visible)))
@@ -761,44 +742,34 @@
             for member in (jnp.concatenate([enc_g, enc_b]), enc_u, jnp.concatenate([dec_g, dec_b]), dec_u)
         )
         h1, a1, k1, z1 = run_f1(att_e, visible, enc_vec)
-    h2, a2, r2 = run_f2(h1, up_e, down_e, enc_vec, enc_upb)
     many = 2 if fast else 1
 
     def grad_blocks(blocks, rows, columns):
         return [((blocks // many, rows, columns), BF, "h")] * many
 
     embed_sq, probs = pltpu.VMEM((SEC, 768, 128), BF), pltpu.VMEM((2, 8 * DEC_ROWS, DEC_ROWS), F32)
-    block_out, dh2, gvec_d, gupb_d, *g_dec = call(
-        partial(dec_both, used(dec), (many, OUT_PATH)),
-        [((1, 196, 512), F32, "v"), (enc_shape, BF, "v"), ((10, 512), F32, "v"), ((1, 2048), F32, "v")]
+    half_sq = pltpu.VMEM((SEC, ENC_ROWS, 768), BF)
+    block_out, dh1, gv_ffn_e, gupb_e, gvec_d, gupb_d, *rest = call(
+        partial(middle, used(up_e, down_e, dec), (many, OUT_PATH)),
+        [((1, 196, 512), F32, "v"), (enc_shape, BF, "v"), ((3, 768), F32, "v"), ((1, 3072), F32, "v")]
+        + [((10, 512), F32, "v"), ((1, 2048), F32, "v")]
+        + [((ENC_ROWS, 4800), BF, "v")] * SEC
         + grad_blocks(BLOCKS, 64, 1792),
-        [embed_sq, dec_sq, dec_sq, dec_wide] * 2 + [probs] + [dma] * 5,
-        table, h2, keep_index, positions, cotangent, dec_vec, dec_upb, *operands(dec),
-        memory="svvvvvv" + spaces(dec),
-    )
-    if fast:
-        swap_d = exchange(g_dec[0], CORE)
-    dh1, gv_ffn_e, gupb_e, *sends_f = call(
-        partial(enc_ffn_bwd, used(up_e, down_e)),
-        [(enc_shape, BF, "v"), ((3, 768), F32, "v"), ((1, 3072), F32, "v")] + [((ENC_ROWS, 4800), BF, "v")] * SEC,
-        [enc_sq, enc_wide, pltpu.VMEM((SEC, ENC_ROWS, 768), BF), pltpu.VMEM((SEC, ENC_ROWS, 192), BF), dma, dma],
-        table, dh2, h1, a2, r2, enc_vec, *operands(up_e, down_e),
-        memory="s" + "v" * 5 + spaces(up_e, down_e),
-    )
+        [enc_sq, enc_wide, pltpu.VMEM((ENC_ROWS, 3072), F32), half_sq, pltpu.VMEM((SEC, ENC_ROWS, 192), BF)]
+        + [embed_sq, dec_sq, dec_sq, dec_wide] * 2 + [probs] + [dma] * 7,
+        table, h1, keep_index, positions, cotangent, enc_vec, enc_upb, dec_vec, dec_upb, *operands(up_e, down_e, dec),
+        memory="s" + "v" * 8 + spaces(up_e, down_e, dec),
+    )
+    sends_f, g_dec = rest[:SEC], rest[SEC:]
 
     def to_section(members):
         return [
             lax.ppermute(members[i], "section", [(s, s ^ i) for s in range(SEC)]) for i in range(1, SEC)
         ]
 
+    came_f = to_section(sends_f)
     if fast:
-        dh1, swap_d, *sends_f = together(dh1, swap_d, *sends_f)
-        came_f = to_section(sends_f)
-        pair_d = add(g_dec[1][:8], swap_d[:8]).astype(BF)
-        dh1, pair_d = together(dh1, pair_d)
-        second_d = exchange(pair_d, SECOND)
-    else:
-        came_f = to_section(sends_f)
+        swap_d = exchange(g_dec[0], CORE)
     input_grad, *sends_a = call(
         partial(enc_att_bwd, used(att_e)),
         [((1, 49, 768), F32, "v")] + [((ENC_ROWS, 2304), BF, "v")] * SEC,
@@ -809,8 +780,8 @@
     step = Order()
     if fast:
         step.came(input_grad)
-        second_d = step.came(second_d)
-        first_d = exchange(add(g_dec[1][8:12], swap_d[8:12], second_d[:4]).astype(BF), FIRST)
+        swap_d = step.came(swap_d)
+        second_d = exchange(add(g_dec[1][:8], swap_d[:8]).astype(BF), SECOND)
         came_f = [step.came(member) for member in came_f]
         sends_a = [step.after(member) for member in sends_a]
     came_a = to_section(sends_a)
@@ -824,14 +795,9 @@
     if fast:
         swap_f = exchange(g_ffn_e[0], CORE)
         step.came(g_ffn_e[1])
-        first_d = step.came(first_d)
-        pair_d, far_d = line_add(g_dec[1][12:], swap_d[12:], second_d[4:], first_d)
-        in_d = move(far_d, INWARD)
         swap_f = step.came(swap_f)
         pair_f, far_f = line_add(g_ffn_e[1], swap_f)
         in_f = move(far_f, INWARD)
-        far_d = add(far_d, step.came(in_d)).astype(BF)
-        mid_d = move(far_d, MIDDLE)
         came_a = [step.came(member) for member in came_a]
     g_att_e = call(
         partial(enc_att_weights, (many, OUT_Z)),
@@ -845,8 +811,8 @@
         step.came(g_att_e[1])
         far_f = add(far_f, step.came(in_f)).astype(BF)
         mid_f = move(far_f, MIDDLE)
-        pair_d = add(pair_d, step.came(mid_d))
-        near_d = exchange(pair_d[1].astype(BF), NEAR)
+        second_d = step.came(second_d)
+        first_d = exchange(add(g_dec[1][8:12], swap_d[8:12], second_d[:4]).astype(BF), FIRST)
         swap_x = step.came(swap_x)
         pair_x, far_x = line_add(g_att_e[1], swap_x)
         in_x = move(far_x, INWARD)
@@ -854,11 +820,19 @@
         near_f = exchange(pair_f[1].astype(BF), NEAR)
         far_x = add(far_x, step.came(in_x)).astype(BF)
         mid_x = move(far_x, MIDDLE)
-        sum_d = add(pair_d[0], step.came(near_d))
+        first_d = step.came(first_d)
+        pair_d, far_d = line_add(g_dec[1][12:], swap_d[12:], second_d[4:], first_d)
+        in_d = move(far_d, INWARD)
         pair_x = add(pair_x, step.came(mid_x))
         near_x = exchange(pair_x[1].astype(BF), NEAR)
         sum_f = add(pair_f[0], step.came(near_f))
-        sums = [sum_d, sum_f, add(pair_x[0], near_x)]
+        far_d = add(far_d, step.came(in_d)).astype(BF)
+        mid_d = move(far_d, MIDDLE)
+        sum_x = add(pair_x[0], step.came(near_x))
+        pair_d = add(pair_d, step.came(mid_d))
+        near_d = exchange(pair_d[1].astype(BF), NEAR)
+        sum_d = add(pair_d[0], near_d)
+        sums = [sum_d, sum_f, sum_x]
         matrix_outs = unpack_grads(*sums)
         below = sums[2][None, 96:104]
     else:

time: 315 us -> 300 us (0.952)
  waiting for transfers between devices: 141 us -> 129 us
  starting transfers between devices: 62.1 us -> 69.7 us
  Pallas kernels: 62.3 us -> 56.2 us
    ppermute x38, waiting for transfers between devices: 125 us -> 89.4 us  [exchange(): return lax.ppermute(value, ('section', 'dp'), pairs)]
    ppermute x6, waiting for transfers between devices: 6.68 us -> 25 us  [to_section(): lax.ppermute(members[i], 'section', [(s, s ^ i) for s in range(SEC)])]
    ppermute x6, starting transfers between devices: 7.59 us -> 16.7 us  [move(): return lax.ppermute(value, ('section', 'dp'), pairs)]
    pallas_call x9 -> x7, Pallas kernels: 62.3 us -> 56.2 us  [call(): pl.pallas_call(body, out_shape=[jax.ShapeDtypeStruct(shape, dtype) for sh...]
    ppermute x6, waiting for transfers between devices: 9.44 us -> 14.9 us  [move(): return lax.ppermute(value, ('section', 'dp'), pairs)]
    unnamed x62 -> x58, local copies, waits for them, and re-layouts: 8.29 us -> 7.9 us
  transfers between devices with their start and end apart: 51 -> 51, of which waited for: 21 -> 25; matrix products, arithmetic and copies ran while one was open for 6% -> 6% of each run, Pallas kernels for 13% -> 7%
where the time goes in v1:
time: 300 us
  waiting for transfers between devices  129 us (43%)
  starting transfers between devices  69.7 us (23%)
  Pallas kernels  56.2 us (19%)
  local copies, waits for them, and re-layouts  15.5 us (5%)
  between operations  14.6 us (5%)
  other arithmetic  14.3 us (5%)
    ppermute x38, waiting for transfers between devices, exchange(): return lax.ppermute(value, ('section', 'dp'), pairs)  89.4 us
    pallas_call x7, Pallas kernels, call(): pl.pallas_call(body, out_shape=[jax.ShapeDtypeStruct(shape, dtype) for sh...  56.2 us
    ppermute x38, starting transfers between devices, exchange(): return lax.ppermute(value, ('section', 'dp'), pairs)  45.9 us
    ppermute x6, waiting for transfers between devices, to_section(): lax.ppermute(members[i], 'section', [(s, s ^ i) for s in range(SEC)])  25 us
    ppermute x6, starting transfers between devices, move(): return lax.ppermute(value, ('section', 'dp'), pairs)  16.7 us
    ppermute x6, waiting for transfers between devices, move(): return lax.ppermute(value, ('section', 'dp'), pairs)  14.9 us
    unnamed x58, local copies, waits for them, and re-layouts  7.9 us
    ppermute x6, starting transfers between devices, to_section(): lax.ppermute(members[i], 'section', [(s, s ^ i) for s in range(SEC)])  7.06 us
  transfers between devices with their start and end apart: 51, of which 25 were waited for; matrix products, arithmetic and copies ran while one was open for 6% of the time, Pallas kernels for 7%

profile of v1, /device:TPU:0, one launch (start us, length us, event | category | flops | bytes accessed | tf_op | source)
XLA Modules:
  0.0 299.6 jit_solution(3870383267672350099)
XLA Ops:
  7.2 1.9 copy.36.down_ref
  9.1 2.1 shard_map.315
  11.3 1.8 shard_map.314
  13.1 5.0 %collective-permute-start.2 = (bf16[1,112,768]{2,1,0:T(8,128)(2,1)}, bf16[1,112,768]{2,1,0:T(8,128)(2,1)S(1)}, u32[]{:S(2)}, u32[]{:S(2)}) collective-permute-start(bf16[1,112,768]{2,1,0:T(8,128)(2,1)} %bitcast.46), channel_id=1, source_target_pairs={{0,6},{1,7},{2,4},{3,5},{4,2},{5,3},{6,0},{7,1},{8,14},{9,15},{10,... | collective-permute-start | bytes 516104 | tf_op jit(solution)/shard_map/ppermute | solution.py:574
  18.8 4.9 %collective-permute-done.2 = bf16[1,112,768]{2,1,0:T(8,128)(2,1)S(1)} collective-permute-done((bf16[1,112,768]{2,1,0:T(8,128)(2,1)}, bf16[1,112,768]{2,1,0:T(8,128)(2,1)S(1)}, u32[]{:S(2)}, u32[]{:S(2)}) %collective-permute-start.2) | collective-permute-done | bytes 172064 | tf_op jit(solution)/shard_map/ppermute | solution.py:574
  23.7 14.2 %collective-permute-done.1 = bf16[1,112,768]{2,1,0:T(8,128)(2,1)S(1)} collective-permute-done((bf16[1,112,768]{2,1,0:T(8,128)(2,1)}, bf16[1,112,768]{2,1,0:T(8,128)(2,1)S(1)}, u32[]{:S(2)}, u32[]{:S(2)}) %collective-permute-start.1) | collective-permute-done | bytes 172064 | tf_op jit(solution)/shard_map/ppermute | solution.py:574
  37.8 1.0 pad_maximum_fusion.refs_0_
  38.9 1.6 collective-permute-start.3
  40.4 1.5 collective-permute-start.12
  41.9 2.5 collective-permute-start.6
  44.4 1.9 collective-permute-start.4
  46.3 6.7 %collective-permute-done.6 = bf16[1,96,768]{2,1,0:T(8,128)(2,1)S(1)} collective-permute-done((bf16[1,96,768]{2,1,0:T(8,128)(2,1)S(1)}, bf16[1,96,768]{2,1,0:T(8,128)(2,1)S(1)}, u32[]{:S(2)}, u32[]{:S(2)}) %collective-permute-start.6) | collective-permute-done | bytes 147488 | tf_op jit(solution)/shard_map/ppermute | solution.py:574
  53.0 12.1 %collective-permute-done.5 = bf16[1,96,768]{2,1,0:T(8,128)(2,1)S(1)} collective-permute-done((bf16[1,96,768]{2,1,0:T(8,128)(2,1)S(1)}, bf16[1,96,768]{2,1,0:T(8,128)(2,1)S(1)}, u32[]{:S(2)}, u32[]{:S(2)}) %collective-permute-start.5) | collective-permute-done | bytes 147488 | tf_op jit(solution)/shard_map/ppermute | solution.py:574
  65.4 1.9 collective-permute-start.11
  67.3 2.6 collective-permute-start.9
  69.9 2.8 collective-permute-done.11
  72.6 15.0 %collective-permute-done.10 = bf16[1,96,768]{2,1,0:T(8,128)(2,1)S(1)} collective-permute-done((bf16[1,96,768]{2,1,0:T(8,128)(2,1)S(1)}, bf16[1,96,768]{2,1,0:T(8,128)(2,1)S(1)}, u32[]{:S(2)}, u32[]{:S(2)}) %collective-permute-start.10) | collective-permute-done | bytes 147488 | tf_op jit(solution)/shard_map/ppermute | solution.py:574
  88.2 0.9 copy-done.16
  91.0 0.9 collective-permute-start.24
  92.5 1.6 collective-permute-start.18
  94.1 6.2 %shard_map.316 = (bf16[64,768]{1,0:T(8,128)(2,1)}, bf16[64,768]{1,0:T(8,128)(2,1)}, bf16[64,2304]{1,0:T(8,128)(2,1)}, bf16[64,768]{1,0:T(8,128)(2,1)}, f32[8,768...) custom-call(s32[105]{0:T(128)} %concatenate.24.table, bf16[1,49,768]{2,1,0:T(8,128)(2,1)} %x_ref.2, ...), custom_call_target="tpu_custom_call" | custom-call | flops 8000000000 | bytes 8000000 | tf_op jit(solution)/shard_map/pallas_call | solution.py:512
  100.3 4.7 %collective-permute-done.17.refs_2_ = bf16[4,96,768]{2,1,0:T(8,128)(2,1)} collective-permute-done((bf16[4,96,768]{2,1,0:T(8,128)(2,1)S(1)}, bf16[4,96,768]{2,1,0:T(8,128)(2,1)}, u32[]{:S(2)}, u32[]{:S(2)}) %collective-permute-start.17) | collective-permute-done | bytes 589856 | tf_op jit(solution)/shard_map/ppermute | solution.py:574
  105.0 3.3 %collective-permute-done.22.refs_9_ = bf16[4,96,768]{2,1,0:T(8,128)(2,1)} collective-permute-done((bf16[4,96,768]{2,1,0:T(8,128)(2,1)S(1)}, bf16[4,96,768]{2,1,0:T(8,128)(2,1)}, u32[]{:S(2)}, u32[]{:S(2)}) %collective-permute-start.22) | collective-permute-done | bytes 589856 | tf_op jit(solution)/shard_map/ppermute | solution.py:574
  108.2 1.1 collective-permute-start.25
  109.4 9.4 %collective-permute-done.18.refs_3_ = bf16[4,96,768]{2,1,0:T(8,128)(2,1)} collective-permute-done((bf16[4,96,768]{2,1,0:T(8,128)(2,1)}, bf16[4,96,768]{2,1,0:T(8,128)(2,1)}, u32[]{:S(2)}, u32[]{:S(2)}) %collective-permute-start.18) | collective-permute-done | bytes 589856 | tf_op jit(solution)/shard_map/ppermute | solution.py:574
  119.2 5.7 %collective-permute-done.25.refs_11_ = bf16[4,96,768]{2,1,0:T(8,128)(2,1)S(1)} collective-permute-done((bf16[4,96,768]{2,1,0:T(8,128)(2,1)}, bf16[4,96,768]{2,1,0:T(8,128)(2,1)S(1)}, u32[]{:S(2)}, u32[]{:S(2)}) %collective-permute-start.25) | collective-permute-done | bytes 589856 | tf_op jit(solution)/shard_map/ppermute | solution.py:574
  126.0 0.8 copy-done.20
  127.1 0.8 copy-done.21
  128.0 1.7 collective-permute-done.21.refs_6_
  130.5 30.1 %shard_map.317 = (f32[1,196,512]{2,1,0:T(8,128)}, bf16[64,768]{1,0:T(8,128)(2,1)}, f32[3,768]{1,0:T(4,128)}, f32[1,3072]{1,0:T(1,128)}, f32[10,512]{1,0:T(8,128)...) custom-call(s32[105]{0:T(128)} %concatenate.24.table, ...), custom_call_target="tpu_custom_call" | custom-call | flops 8000000000 | bytes 8000000 | tf_op jit(solution)/shard_map/pallas_call | solution.py:512
  160.8 0.8 collective-permute-start.30
  161.6 1.0 collective-permute-start.31
  162.6 1.7 collective-permute-start.32
  164.3 8.9 %shard_map.318 = (f32[1,49,768]{2,1,0:T(8,128)}, bf16[64,2304]{1,0:T(8,128)(2,1)}, bf16[64,2304]{1,0:T(8,128)(2,1)}, bf16[64,2304]{1,0:T(8,128)(2,1)}, bf16[64,2304]{1,0:T(8,128)(2,1)}) custom-call(s32[105]{0:T(128)} %concatenate.24.table, bf16[64,768]{1,0:T(8,128)(2,1)} %get-tuple-element.127.dh_ref, bf16[1,49,768]{2,1,0:T(8,128)(2,1)} %x_ref.2, ...), custom_call_target="tpu_custom_call" | custom-call | flops 8000000000 | bytes 8000000 | tf_op jit(solution)/shard_map/pallas_call | solution.py:512
  173.2 17.5 %collective-permute-done.32.refs_0_ = bf16[64,4800]{1,0:T(8,128)(2,1)} collective-permute-done((bf16[64,4800]{1,0:T(8,128)(2,1)}, bf16[64,4800]{1,0:T(8,128)(2,1)}, u32[]{:S(2)}, u32[]{:S(2)}) %collective-permute-start.32) | collective-permute-done | bytes 614432 | tf_op jit(solution)/shard_map/ppermute | solution.py:767
  191.3 3.9 %shard_map.319 = (bf16[4,96,1536]{2,1,0:T(8,128)(2,1)}, bf16[4,96,1536]{2,1,0:T(8,128)(2,1)}) custom-call(s32[105]{0:T(128)} %concatenate.24.table, bf16[64,4800]{1,0:T(8,128)(2,1)} %get-tuple-element.148.own_ref, bf16[64,4800]{1,0:T(8,128)(2,1)} %collective-permute-done.32.refs_0_, bf16[64,4800]{1,0:T(8,128)(2,1)} %collective-permute-done.31.refs_1_, ...), custom_call_target="tpu_custom_call" | custom-call | flops 8000000000 | bytes 8000000 | tf_op jit(solution)/shard_map/pallas_call | solution.py:512
  195.3 0.7 collective-permute-start.34
  196.0 1.1 collective-permute-start.36
  197.1 1.7 collective-permute-start.37
  198.8 3.4 %add_convert_fusion = bf16[8,64,1792]{2,1,0:T(8,128)(2,1)} fusion(bf16[16,64,1792]{2,1,0:T(8,128)(2,1)} %copy-done.1, bf16[16,64,1792]{2,1,0:T(8,128)(2,1)S(1)} %copy-done), kind=kLoop, calls=%fused_computation | loop fusion | flops 3670016 | bytes 5505024 | tf_op jit(solution)/shard_map/convert_element_type | solution.py:784
  202.2 1.0 collective-permute-start.39
  203.2 0.8 copy.38
  204.0 1.2 copy.37
  205.7 6.4 %collective-permute-done.37.refs_2_ = bf16[64,2304]{1,0:T(8,128)(2,1)S(1)} collective-permute-done((bf16[64,2304]{1,0:T(8,128)(2,1)S(1)}, bf16[64,2304]{1,0:T(8,128)(2,1)S(1)}, u32[]{:S(2)}, u32[]{:S(2)}) %collective-permute-start.37) | collective-permute-done | bytes 294944 | tf_op jit(solution)/shard_map/ppermute | solution.py:767
  212.1 1.0 add_convert_fusion.3
  213.1 2.5 collective-permute-start.40
  215.6 3.2 %shard_map.320 = (bf16[4,112,768]{2,1,0:T(8,128)(2,1)}, bf16[4,112,768]{2,1,0:T(8,128)(2,1)}) custom-call(s32[105]{0:T(128)} %concatenate.24.table, bf16[64,2304]{1,0:T(8,128)(2,1)} %get-tuple-element.145.own_ref, bf16[64,2304]{1,0:T(8,128)(2,1)} %copy-done.24, bf16[64,2304]{1,0:T(8,128)(2,1)} %copy-done.25, bf16[64,2304]{1,0:T(8,128)(2,1)} %copy-done.26), custom_call_target="tpu_custom_call" | custom-call | flops 8000000000 | bytes 8000000 | tf_op jit(solution)/shard_map/pallas_call | solution.py:512
  218.8 8.2 %collective-permute-done.40 = bf16[2,96,1536]{2,1,0:T(8,128)(2,1)} collective-permute-done((bf16[2,96,1536]{2,1,0:T(8,128)(2,1)}, bf16[2,96,1536]{2,1,0:T(8,128)(2,1)}, u32[]{:S(2)}, u32[]{:S(2)}) %collective-permute-start.40) | collective-permute-done | bytes 589856 | tf_op jit(solution)/shard_map/ppermute | solution.py:626
  227.0 1.4 add_convert_fusion.2
  228.4 0.8 collective-permute-start.42
  229.3 2.1 collective-permute-done.39
  231.4 1.8 add_convert_fusion.1
  233.2 1.4 collective-permute-start.44
  234.7 5.2 %collective-permute-start.41 = (bf16[2,112,768]{2,1,0:T(8,128)(2,1)S(1)}, bf16[2,112,768]{2,1,0:T(8,128)(2,1)S(1)}, u32[]{:S(2)}, u32[]{:S(2)}) collective-permute-start(bf16[2,112,768]{2,1,0:T(8,128)(2,1)S(1)} %add_convert_fusion.7), channel_id=1, source_target_pairs={{0,2},{1,3},{6,4},{7,5},{8,10},{9,11},{14,12},{15,13},{16,18},{17,... | collective-permute-start | bytes 1032200 | tf_op jit(solution)/shard_map/ppermute | solution.py:626
  240.2 7.4 %collective-permute-start.47 = (bf16[96,1536]{1,0:T(8,128)(2,1)S(1)}, bf16[96,1536]{1,0:T(8,128)(2,1)S(1)}, u32[]{:S(2)}, u32[]{:S(2)}) collective-permute-start(bf16[96,1536]{1,0:T(8,128)(2,1)S(1)} %fusion.3), channel_id=1, source_target_pairs={{0,2},{1,3},{2,0},{3,1},{4,6},{5,7},{6,4},{7,5},{8,10},{9,11},{10,... | collective-permute-start | bytes 884744 | tf_op jit(solution)/shard_map/ppermute | solution.py:574
  248.4 1.4 add_convert_fusion.5
  249.9 2.8 collective-permute-done.47
  252.7 6.9 %collective-permute-start.46 = (bf16[2,64,1792]{2,1,0:T(8,128)(2,1)S(1)}, bf16[2,64,1792]{2,1,0:T(8,128)(2,1)S(1)}, u32[]{:S(2)}, u32[]{:S(2)}) collective-permute-start(bf16[2,64,1792]{2,1,0:T(8,128)(2,1)S(1)} %add_convert_fusion.5), channel_id=1, source_target_pairs={{0,2},{1,3},{6,4},{7,5},{8,10},{9,11},{14,12},{15,13},{16,18},{17,... | collective-permute-start | bytes 1376264 | tf_op jit(solution)/shard_map/ppermute | solution.py:626
  261.2 6.7 %collective-permute-done.46 = bf16[2,64,1792]{2,1,0:T(8,128)(2,1)S(1)} collective-permute-done((bf16[2,64,1792]{2,1,0:T(8,128)(2,1)S(1)}, bf16[2,64,1792]{2,1,0:T(8,128)(2,1)S(1)}, u32[]{:S(2)}, u32[]{:S(2)}) %collective-permute-start.46) | collective-permute-done | bytes 458784 | tf_op jit(solution)/shard_map/ppermute | solution.py:626
  268.0 1.7 collective-permute-done.45
  272.7 1.5 convert_add_fusion.1
  274.2 11.1 %collective-permute-start.49 = (bf16[64,1792]{1,0:T(8,128)(2,1)S(1)}, bf16[64,1792]{1,0:T(8,128)(2,1)S(1)}, u32[]{:S(2)}, u32[]{:S(2)}) collective-permute-start(bf16[64,1792]{1,0:T(8,128)(2,1)S(1)} %fusion.4), channel_id=1, source_target_pairs={{0,2},{1,3},{2,0},{3,1},{4,6},{5,7},{6,4},{7,5},{8,10},{9,11},{10,... | collective-permute-start | bytes 688136 | tf_op jit(solution)/shard_map/ppermute | solution.py:574
  287.9 1.4 collective-permute-done.49
  291.3 0.8 copy.39
  (148 shorter events, 19.4 us)
Async XLA Ops:
  7.2 122.6 %all-gather.3.cloned.1.call-start = ((), (), s32[]{:S(2)}) async-start(), calls=%async_computation | async-start | bytes 7569408 | tf_op jit(solution)/shard_map/all_gather | solution.py:706
  11.3 30.7 %copy-start.13 = (bf16[96,768]{1,0:T(8,128)(2,1)S(1)}, bf16[96,768]{1,0:T(8,128)(2,1)}, u32[]{:S(2)}) copy-start(bf16[96,768]{1,0:T(8,128)(2,1)} %get-tuple-element.95) | copy-start | bytes 442372
  13.1 52.3 %copy-start.12 = (bf16[96,768]{1,0:T(8,128)(2,1)S(1)}, bf16[96,768]{1,0:T(8,128)(2,1)}, u32[]{:S(2)}) copy-start(bf16[96,768]{1,0:T(8,128)(2,1)} %get-tuple-element.101) | copy-start | bytes 442372
  13.1 10.6 %collective-permute-start.2 = (bf16[1,112,768]{2,1,0:T(8,128)(2,1)}, bf16[1,112,768]{2,1,0:T(8,128)(2,1)S(1)}, u32[]{:S(2)}, u32[]{:S(2)}) collective-permute-start(bf16[1,112,768]{2,1,0:T(8,128)(2,1)} %bitcast.46), channel_id=1, source_target_pairs={{0,6},{1,7},{2,4},{3,5},{4,2},{5,3},{6,0},{7,1},{8,14},{9,15},{10,... | collective-permute-start | bytes 516104 | tf_op jit(solution)/shard_map/ppermute | solution.py:574
  18.2 19.7 %collective-permute-start.1 = (bf16[1,112,768]{2,1,0:T(8,128)(2,1)}, bf16[1,112,768]{2,1,0:T(8,128)(2,1)S(1)}, u32[]{:S(2)}, u32[]{:S(2)}) collective-permute-start(bf16[1,112,768]{2,1,0:T(8,128)(2,1)} %bitcast.47), channel_id=1, source_target_pairs={{0,4},{1,5},{2,6},{3,7},{4,0},{5,1},{6,2},{7,3},{8,12},{9,13},{10,... | collective-permute-start | bytes 516104 | tf_op jit(solution)/shard_map/ppermute | solution.py:574
  18.2 19.7 %collective-permute-start = (bf16[1,112,768]{2,1,0:T(8,128)(2,1)}, bf16[1,112,768]{2,1,0:T(8,128)(2,1)S(1)}, u32[]{:S(2)}, u32[]{:S(2)}) collective-permute-start(bf16[1,112,768]{2,1,0:T(8,128)(2,1)} %bitcast.48), channel_id=1, source_target_pairs={{0,2},{1,3},{2,0},{3,1},{4,6},{5,7},{6,4},{7,5},{8,10},{9,11},{10,... | collective-permute-start | bytes 516104 | tf_op jit(solution)/shard_map/ppermute | solution.py:574
  38.9 55.2 %copy-start.6 = (bf16[4,112,768]{2,1,0:T(8,128)(2,1)}, bf16[4,112,768]{2,1,0:T(8,128)(2,1)S(1)}, u32[]{:S(2)}) copy-start(bf16[4,112,768]{2,1,0:T(8,128)(2,1)S(1)} %pad_maximum_fusion.refs_0_) | copy-start | bytes 2064388
  38.9 26.4 %collective-permute-start.3 = (bf16[4,112,768]{2,1,0:T(8,128)(2,1)S(1)}, bf16[4,112,768]{2,1,0:T(8,128)(2,1)S(1)}, u32[]{:S(2)}, u32[]{:S(2)}) collective-permute-start(bf16[4,112,768]{2,1,0:T(8,128)(2,1)S(1)} %pad_maximum_fusion.refs_0_), channel_id=1, source_target_pairs={{0,8},{1,17},{2,10},{3,19},{4,12},{5,21},{6,14},{7,23},{8,0},{9,25... | collective-permute-start | bytes 2064392 | tf_op jit(solution)/shard_map/ppermute | solution.py:574
  40.4 26.9 %collective-permute-start.12 = (bf16[4,112,768]{2,1,0:T(8,128)(2,1)S(1)}, bf16[4,112,768]{2,1,0:T(8,128)(2,1)S(1)}, u32[]{:S(2)}, u32[]{:S(2)}) collective-permute-start(bf16[4,112,768]{2,1,0:T(8,128)(2,1)S(1)} %pad_maximum_fusion.refs_0_), channel_id=1, source_target_pairs={{0,16},{1,9},{2,18},{3,11},{4,20},{5,13},{6,22},{7,15},{8,24},{9,1... | collective-permute-start | bytes 2064392 | tf_op jit(solution)/shard_map/ppermute | solution.py:574
  41.9 11.1 %collective-permute-start.6 = (bf16[1,96,768]{2,1,0:T(8,128)(2,1)S(1)}, bf16[1,96,768]{2,1,0:T(8,128)(2,1)S(1)}, u32[]{:S(2)}, u32[]{:S(2)}) collective-permute-start(bf16[1,96,768]{2,1,0:T(8,128)(2,1)S(1)} %bitcast.54), channel_id=1, source_target_pairs={{0,6},{1,7},{2,4},{3,5},{4,2},{5,3},{6,0},{7,1},{8,14},{9,15},{10,... | collective-permute-start | bytes 442376 | tf_op jit(solution)/shard_map/ppermute | solution.py:574
  44.4 20.7 %collective-permute-start.5 = (bf16[1,96,768]{2,1,0:T(8,128)(2,1)S(1)}, bf16[1,96,768]{2,1,0:T(8,128)(2,1)S(1)}, u32[]{:S(2)}, u32[]{:S(2)}) collective-permute-start(bf16[1,96,768]{2,1,0:T(8,128)(2,1)S(1)} %bitcast.55), channel_id=1, source_target_pairs={{0,4},{1,5},{2,6},{3,7},{4,0},{5,1},{6,2},{7,3},{8,12},{9,13},{10,... | collective-permute-start | bytes 442376 | tf_op jit(solution)/shard_map/ppermute | solution.py:574
  44.4 20.7 %collective-permute-start.4 = (bf16[1,96,768]{2,1,0:T(8,128)(2,1)S(1)}, bf16[1,96,768]{2,1,0:T(8,128)(2,1)S(1)}, u32[]{:S(2)}, u32[]{:S(2)}) collective-permute-start(bf16[1,96,768]{2,1,0:T(8,128)(2,1)S(1)} %bitcast.56), channel_id=1, source_target_pairs={{0,2},{1,3},{2,0},{3,1},{4,6},{5,7},{6,4},{7,5},{8,10},{9,11},{10,... | collective-permute-start | bytes 442376 | tf_op jit(solution)/shard_map/ppermute | solution.py:574
  65.2 35.0 %copy-start.8 = (bf16[4,96,768]{2,1,0:T(8,128)(2,1)}, bf16[4,96,768]{2,1,0:T(8,128)(2,1)S(1)}, u32[]{:S(2)}) copy-start(bf16[4,96,768]{2,1,0:T(8,128)(2,1)S(1)} %pad_maximum_fusion.1.refs_0_) | copy-start | bytes 1769476
  65.2 28.8 %copy-start.14 = (bf16[4,112,768]{2,1,0:T(8,128)(2,1)}, bf16[4,112,768]{2,1,0:T(8,128)(2,1)S(1)}, u32[]{:S(2)}) copy-start(bf16[4,112,768]{2,1,0:T(8,128)(2,1)S(1)} %collective-permute-done.3.refs_1_) | copy-start | bytes 2064388
  65.2 23.0 %collective-permute-start.7 = (bf16[4,112,768]{2,1,0:T(8,128)(2,1)S(1)}, bf16[4,112,768]{2,1,0:T(8,128)(2,1)}, u32[]{:S(2)}, u32[]{:S(2)}) collective-permute-start(bf16[4,112,768]{2,1,0:T(8,128)(2,1)S(1)} %collective-permute-done.3.refs_1_), channel_id=1, source_target_pairs={{0,16},{1,9},{2,18},{3,11},{4,20},{5,13},{6,22},{7,15},{8,24},{9,1... | collective-permute-start | bytes 2064392 | tf_op jit(solution)/shard_map/ppermute | solution.py:574
  65.3 22.9 %collective-permute-start.8 = (bf16[4,96,768]{2,1,0:T(8,128)(2,1)S(1)}, bf16[4,96,768]{2,1,0:T(8,128)(2,1)S(1)}, u32[]{:S(2)}, u32[]{:S(2)}) collective-permute-start(bf16[4,96,768]{2,1,0:T(8,128)(2,1)S(1)} %pad_maximum_fusion.1.refs_0_), channel_id=1, source_target_pairs={{0,8},{1,17},{2,10},{3,19},{4,12},{5,21},{6,14},{7,23},{8,0},{9,25... | collective-permute-start | bytes 1769480 | tf_op jit(solution)/shard_map/ppermute | solution.py:574
  65.4 7.2 %collective-permute-start.11 = (bf16[1,96,768]{2,1,0:T(8,128)(2,1)S(1)}, bf16[1,96,768]{2,1,0:T(8,128)(2,1)S(1)}, u32[]{:S(2)}, u32[]{:S(2)}) collective-permute-start(bf16[1,96,768]{2,1,0:T(8,128)(2,1)S(1)} %bitcast.50), channel_id=1, source_target_pairs={{0,6},{1,7},{2,4},{3,5},{4,2},{5,3},{6,0},{7,1},{8,14},{9,15},{10,... | collective-permute-start | bytes 442376 | tf_op jit(solution)/shard_map/ppermute | solution.py:574
  67.3 20.3 %collective-permute-start.10 = (bf16[1,96,768]{2,1,0:T(8,128)(2,1)S(1)}, bf16[1,96,768]{2,1,0:T(8,128)(2,1)S(1)}, u32[]{:S(2)}, u32[]{:S(2)}) collective-permute-start(bf16[1,96,768]{2,1,0:T(8,128)(2,1)S(1)} %bitcast.51), channel_id=1, source_target_pairs={{0,4},{1,5},{2,6},{3,7},{4,0},{5,1},{6,2},{7,3},{8,12},{9,13},{10,... | collective-permute-start | bytes 442376 | tf_op jit(solution)/shard_map/ppermute | solution.py:574
  67.3 26.8 %copy-start.15 = (bf16[4,112,768]{2,1,0:T(8,128)(2,1)}, bf16[4,112,768]{2,1,0:T(8,128)(2,1)S(1)}, u32[]{:S(2)}) copy-start(bf16[4,112,768]{2,1,0:T(8,128)(2,1)S(1)} %collective-permute-done.12.refs_2_) | copy-start | bytes 2064388
  67.3 20.3 %collective-permute-start.9 = (bf16[1,96,768]{2,1,0:T(8,128)(2,1)S(1)}, bf16[1,96,768]{2,1,0:T(8,128)(2,1)S(1)}, u32[]{:S(2)}, u32[]{:S(2)}) collective-permute-start(bf16[1,96,768]{2,1,0:T(8,128)(2,1)S(1)} %bitcast.52), channel_id=1, source_target_pairs={{0,2},{1,3},{2,0},{3,1},{4,6},{5,7},{6,4},{7,5},{8,10},{9,11},{10,... | collective-permute-start | bytes 442376 | tf_op jit(solution)/shard_map/ppermute | solution.py:574
  72.6 17.6 %collective-permute-start.13 = (bf16[4,112,768]{2,1,0:T(8,128)(2,1)S(1)}, bf16[4,112,768]{2,1,0:T(8,128)(2,1)}, u32[]{:S(2)}, u32[]{:S(2)}) collective-permute-start(bf16[4,112,768]{2,1,0:T(8,128)(2,1)S(1)} %pad_maximum_fusion.refs_0_), channel_id=1, source_target_pairs={{0,1},{1,0},{2,3},{3,2},{4,5},{5,4},{6,7},{7,6},{8,9},{9,8},{10,11... | collective-permute-start | bytes 2064392 | tf_op jit(solution)/shard_map/ppermute | solution.py:574
  87.6 4.3 %collective-permute-start.14 = (bf16[4,112,768]{2,1,0:T(8,128)(2,1)S(1)}, bf16[4,112,768]{2,1,0:T(8,128)(2,1)}, u32[]{:S(2)}, u32[]{:S(2)}) collective-permute-start(bf16[4,112,768]{2,1,0:T(8,128)(2,1)S(1)} %collective-permute-done.3.refs_1_), channel_id=1, source_target_pairs={{0,1},{1,0},{2,3},{3,2},{4,5},{5,4},{6,7},{7,6},{8,9},{9,8},{10,11... | collective-permute-start | bytes 2064392 | tf_op jit(solution)/shard_map/ppermute | solution.py:574
  87.6 3.4 %collective-permute-start.15 = (bf16[4,112,768]{2,1,0:T(8,128)(2,1)S(1)}, bf16[4,112,768]{2,1,0:T(8,128)(2,1)}, u32[]{:S(2)}, u32[]{:S(2)}) collective-permute-start(bf16[4,112,768]{2,1,0:T(8,128)(2,1)S(1)} %collective-permute-done.12.refs_2_), channel_id=1, source_target_pairs={{0,1},{1,0},{2,3},{3,2},{4,5},{5,4},{6,7},{7,6},{8,9},{9,8},{10,11... | collective-permute-start | bytes 2064392 | tf_op jit(solution)/shard_map/ppermute | solution.py:574
  88.2 31.0 %copy-start.9 = (bf16[4,96,768]{2,1,0:T(8,128)(2,1)}, bf16[4,96,768]{2,1,0:T(8,128)(2,1)S(1)}, u32[]{:S(2)}) copy-start(bf16[4,96,768]{2,1,0:T(8,128)(2,1)S(1)} %pad_maximum_fusion.2.refs_8_) | copy-start | bytes 1769476
  89.1 3.4 %collective-permute-start.16 = (bf16[4,112,768]{2,1,0:T(8,128)(2,1)}, bf16[4,112,768]{2,1,0:T(8,128)(2,1)}, u32[]{:S(2)}, u32[]{:S(2)}) collective-permute-start(bf16[4,112,768]{2,1,0:T(8,128)(2,1)} %collective-permute-done.7.refs_3_), channel_id=1, source_target_pairs={{0,1},{1,0},{2,3},{3,2},{4,5},{5,4},{6,7},{7,6},{8,9},{9,8},{10,11... | collective-permute-start | bytes 2064392 | tf_op jit(solution)/shard_map/ppermute | solution.py:574
  89.8 15.2 %collective-permute-start.17 = (bf16[4,96,768]{2,1,0:T(8,128)(2,1)S(1)}, bf16[4,96,768]{2,1,0:T(8,128)(2,1)}, u32[]{:S(2)}, u32[]{:S(2)}) collective-permute-start(bf16[4,96,768]{2,1,0:T(8,128)(2,1)S(1)} %pad_maximum_fusion.1.refs_0_), channel_id=1, source_target_pairs={{0,16},{1,9},{2,18},{3,11},{4,20},{5,13},{6,22},{7,15},{8,24},{9,1... | collective-permute-start | bytes 1769480 | tf_op jit(solution)/shard_map/ppermute | solution.py:574
  90.2 34.7 %collective-permute-start.19 = (bf16[4,96,768]{2,1,0:T(8,128)(2,1)S(1)}, bf16[4,96,768]{2,1,0:T(8,128)(2,1)}, u32[]{:S(2)}, u32[]{:S(2)}) collective-permute-start(bf16[4,96,768]{2,1,0:T(8,128)(2,1)S(1)} %pad_maximum_fusion.1.refs_0_), channel_id=1, source_target_pairs={{0,1},{1,0},{2,3},{3,2},{4,5},{5,4},{6,7},{7,6},{8,9},{9,8},{10,11... | collective-permute-start | bytes 1769480 | tf_op jit(solution)/shard_map/ppermute | solution.py:574
  91.0 27.8 %collective-permute-start.24 = (bf16[4,96,768]{2,1,0:T(8,128)(2,1)S(1)}, bf16[4,96,768]{2,1,0:T(8,128)(2,1)}, u32[]{:S(2)}, u32[]{:S(2)}) collective-permute-start(bf16[4,96,768]{2,1,0:T(8,128)(2,1)S(1)} %pad_maximum_fusion.2.refs_8_), channel_id=1, source_target_pairs={{0,16},{1,9},{2,18},{3,11},{4,20},{5,13},{6,22},{7,15},{8,24},{9,1... | collective-permute-start | bytes 1769480 | tf_op jit(solution)/shard_map/ppermute | solution.py:574
  91.9 16.4 %collective-permute-start.22 = (bf16[4,96,768]{2,1,0:T(8,128)(2,1)S(1)}, bf16[4,96,768]{2,1,0:T(8,128)(2,1)}, u32[]{:S(2)}, u32[]{:S(2)}) collective-permute-start(bf16[4,96,768]{2,1,0:T(8,128)(2,1)S(1)} %pad_maximum_fusion.2.refs_8_), channel_id=1, source_target_pairs={{0,8},{1,17},{2,10},{3,19},{4,12},{5,21},{6,14},{7,23},{8,0},{9,25... | collective-permute-start | bytes 1769480 | tf_op jit(solution)/shard_map/ppermute | solution.py:574
  92.5 26.2 %collective-permute-start.18 = (bf16[4,96,768]{2,1,0:T(8,128)(2,1)}, bf16[4,96,768]{2,1,0:T(8,128)(2,1)}, u32[]{:S(2)}, u32[]{:S(2)}) collective-permute-start(bf16[4,96,768]{2,1,0:T(8,128)(2,1)} %copy-done.16), channel_id=1, source_target_pairs={{0,16},{1,9},{2,18},{3,11},{4,20},{5,13},{6,22},{7,15},{8,24},{9,1... | collective-permute-start | bytes 1769480 | tf_op jit(solution)/shard_map/ppermute | solution.py:574
  108.2 16.7 %collective-permute-start.25 = (bf16[4,96,768]{2,1,0:T(8,128)(2,1)}, bf16[4,96,768]{2,1,0:T(8,128)(2,1)S(1)}, u32[]{:S(2)}, u32[]{:S(2)}) collective-permute-start(bf16[4,96,768]{2,1,0:T(8,128)(2,1)} %collective-permute-done.22.refs_9_), channel_id=1, source_target_pairs={{0,16},{1,9},{2,18},{3,11},{4,20},{5,13},{6,22},{7,15},{8,24},{9,1... | collective-permute-start | bytes 1769480 | tf_op jit(solution)/shard_map/ppermute | solution.py:574
  118.7 6.7 %collective-permute-start.28 = (bf16[4,96,768]{2,1,0:T(8,128)(2,1)}, bf16[4,96,768]{2,1,0:T(8,128)(2,1)S(1)}, u32[]{:S(2)}, u32[]{:S(2)}) collective-permute-start(bf16[4,96,768]{2,1,0:T(8,128)(2,1)} %collective-permute-done.24.refs_10_), channel_id=1, source_target_pairs={{0,1},{1,0},{2,3},{3,2},{4,5},{5,4},{6,7},{7,6},{8,9},{9,8},{10,11... | collective-permute-start | bytes 1769480 | tf_op jit(solution)/shard_map/ppermute | solution.py:574
  118.7 6.8 %collective-permute-start.27 = (bf16[4,96,768]{2,1,0:T(8,128)(2,1)}, bf16[4,96,768]{2,1,0:T(8,128)(2,1)S(1)}, u32[]{:S(2)}, u32[]{:S(2)}) collective-permute-start(bf16[4,96,768]{2,1,0:T(8,128)(2,1)} %collective-permute-done.22.refs_9_), channel_id=1, source_target_pairs={{0,1},{1,0},{2,3},{3,2},{4,5},{5,4},{6,7},{7,6},{8,9},{9,8},{10,11... | collective-permute-start | bytes 1769480 | tf_op jit(solution)/shard_map/ppermute | solution.py:574
  119.2 6.7 %collective-permute-start.26 = (bf16[4,96,768]{2,1,0:T(8,128)(2,1)S(1)}, bf16[4,96,768]{2,1,0:T(8,128)(2,1)S(1)}, u32[]{:S(2)}, u32[]{:S(2)}) collective-permute-start(bf16[4,96,768]{2,1,0:T(8,128)(2,1)S(1)} %pad_maximum_fusion.2.refs_8_), channel_id=1, source_target_pairs={{0,1},{1,0},{2,3},{3,2},{4,5},{5,4},{6,7},{7,6},{8,9},{9,8},{10,11... | collective-permute-start | bytes 1769480 | tf_op jit(solution)/shard_map/ppermute | solution.py:574
  124.9 2.2 collective-permute-start.23
  124.9 4.7 %collective-permute-start.21 = (bf16[4,96,768]{2,1,0:T(8,128)(2,1)}, bf16[4,96,768]{2,1,0:T(8,128)(2,1)S(1)}, u32[]{:S(2)}, u32[]{:S(2)}) collective-permute-start(bf16[4,96,768]{2,1,0:T(8,128)(2,1)} %collective-permute-done.17.refs_2_), channel_id=1, source_target_pairs={{0,1},{1,0},{2,3},{3,2},{4,5},{5,4},{6,7},{7,6},{8,9},{9,8},{10,11... | collective-permute-start | bytes 1769480 | tf_op jit(solution)/shard_map/ppermute | solution.py:574
  125.4 4.4 %collective-permute-start.20 = (bf16[4,96,768]{2,1,0:T(8,128)(2,1)}, bf16[4,96,768]{2,1,0:T(8,128)(2,1)}, u32[]{:S(2)}, u32[]{:S(2)}) collective-permute-start(bf16[4,96,768]{2,1,0:T(8,128)(2,1)} %copy-done.16), channel_id=1, source_target_pairs={{0,1},{1,0},{2,3},{3,2},{4,5},{5,4},{6,7},{7,6},{8,9},{9,8},{10,11... | collective-permute-start | bytes 1769480 | tf_op jit(solution)/shard_map/ppermute | solution.py:574
  125.5 4.3 %collective-permute-start.29 = (bf16[4,96,768]{2,1,0:T(8,128)(2,1)S(1)}, bf16[4,96,768]{2,1,0:T(8,128)(2,1)}, u32[]{:S(2)}, u32[]{:S(2)}) collective-permute-start(bf16[4,96,768]{2,1,0:T(8,128)(2,1)S(1)} %collective-permute-done.25.refs_11_), channel_id=1, source_target_pairs={{0,1},{1,0},{2,3},{3,2},{4,5},{5,4},{6,7},{7,6},{8,9},{9,8},{10,11... | collective-permute-start | bytes 1769480 | tf_op jit(solution)/shard_map/ppermute | solution.py:574
  160.6 12.6 %collective-permute-start.33 = (bf16[16,64,1792]{2,1,0:T(8,128)(2,1)}, bf16[16,64,1792]{2,1,0:T(8,128)(2,1)S(1)}, u32[]{:S(2)}, u32[]{:S(2)}) collective-permute-start(bf16[16,64,1792]{2,1,0:T(8,128)(2,1)} %get-tuple-element.140), channel_id=1, source_target_pairs={{0,1},{1,0},{2,3},{3,2},{4,5},{5,4},{6,7},{7,6},{8,9},{9,8},{10,11... | collective-permute-start | bytes 11010056 | tf_op jit(solution)/shard_map/ppermute | solution.py:574
  160.8 30.5 %collective-permute-start.30 = (bf16[64,4800]{1,0:T(8,128)(2,1)}, bf16[64,4800]{1,0:T(8,128)(2,1)}, u32[]{:S(2)}, u32[]{:S(2)}) collective-permute-start(bf16[64,4800]{1,0:T(8,128)(2,1)} %get-tuple-element.137), channel_id=1, source_target_pairs={{0,24},{8,16},{16,8},{24,0},{1,25},{9,17},{17,9},{25,1},{2,26},{10... | collective-permute-start | bytes 1843208 | tf_op jit(solution)/shard_map/ppermute | solution.py:767
  161.6 29.7 %collective-permute-start.31 = (bf16[64,4800]{1,0:T(8,128)(2,1)}, bf16[64,4800]{1,0:T(8,128)(2,1)}, u32[]{:S(2)}, u32[]{:S(2)}) collective-permute-start(bf16[64,4800]{1,0:T(8,128)(2,1)} %get-tuple-element.138), channel_id=1, source_target_pairs={{0,16},{8,24},{16,0},{24,8},{1,17},{9,25},{17,1},{25,9},{2,18},{10... | collective-permute-start | bytes 1843208 | tf_op jit(solution)/shard_map/ppermute | solution.py:767
  162.6 28.1 %collective-permute-start.32 = (bf16[64,4800]{1,0:T(8,128)(2,1)}, bf16[64,4800]{1,0:T(8,128)(2,1)}, u32[]{:S(2)}, u32[]{:S(2)}) collective-permute-start(bf16[64,4800]{1,0:T(8,128)(2,1)} %get-tuple-element.139), channel_id=1, source_target_pairs={{0,8},{8,0},{16,24},{24,16},{1,9},{9,1},{17,25},{25,17},{2,10},{10... | collective-permute-start | bytes 1843208 | tf_op jit(solution)/shard_map/ppermute | solution.py:767
  173.2 18.1 %copy-start.1 = (bf16[16,64,1792]{2,1,0:T(8,128)(2,1)}, bf16[16,64,1792]{2,1,0:T(8,128)(2,1)S(1)}, u32[]{:S(2)}) copy-start(bf16[16,64,1792]{2,1,0:T(8,128)(2,1)S(1)} %collective-permute-done.33) | copy-start | bytes 11010052
  195.2 10.0 %collective-permute-start.35 = (bf16[4,96,1536]{2,1,0:T(8,128)(2,1)}, bf16[4,96,1536]{2,1,0:T(8,128)(2,1)S(1)}, u32[]{:S(2)}, u32[]{:S(2)}) collective-permute-start(bf16[4,96,1536]{2,1,0:T(8,128)(2,1)} %get-tuple-element.149), channel_id=1, source_target_pairs={{0,1},{1,0},{2,3},{3,2},{4,5},{5,4},{6,7},{7,6},{8,9},{9,8},{10,11... | collective-permute-start | bytes 3538952 | tf_op jit(solution)/shard_map/ppermute | solution.py:574
  195.3 10.1 %collective-permute-start.34 = (bf16[64,2304]{1,0:T(8,128)(2,1)}, bf16[64,2304]{1,0:T(8,128)(2,1)S(1)}, u32[]{:S(2)}, u32[]{:S(2)}) collective-permute-start(bf16[64,2304]{1,0:T(8,128)(2,1)} %get-tuple-element.147), channel_id=1, source_target_pairs={{0,8},{8,0},{16,24},{24,16},{1,9},{9,1},{17,25},{25,17},{2,10},{10... | collective-permute-start | bytes 884744 | tf_op jit(solution)/shard_map/ppermute | solution.py:767
  196.0 9.7 %collective-permute-start.36 = (bf16[64,2304]{1,0:T(8,128)(2,1)}, bf16[64,2304]{1,0:T(8,128)(2,1)S(1)}, u32[]{:S(2)}, u32[]{:S(2)}) collective-permute-start(bf16[64,2304]{1,0:T(8,128)(2,1)} %get-tuple-element.152), channel_id=1, source_target_pairs={{0,16},{8,24},{16,0},{24,8},{1,17},{9,25},{17,1},{25,9},{2,18},{10... | collective-permute-start | bytes 884744 | tf_op jit(solution)/shard_map/ppermute | solution.py:767
  197.1 15.1 %collective-permute-start.37 = (bf16[64,2304]{1,0:T(8,128)(2,1)S(1)}, bf16[64,2304]{1,0:T(8,128)(2,1)S(1)}, u32[]{:S(2)}, u32[]{:S(2)}) collective-permute-start(bf16[64,2304]{1,0:T(8,128)(2,1)S(1)} %copy-done.23), channel_id=1, source_target_pairs={{0,24},{8,16},{16,8},{24,0},{1,25},{9,17},{17,9},{25,1},{2,26},{10... | collective-permute-start | bytes 884744 | tf_op jit(solution)/shard_map/ppermute | solution.py:767
  198.8 13.3 %copy-start.2 = (bf16[4,96,1536]{2,1,0:T(8,128)(2,1)S(1)}, bf16[4,96,1536]{2,1,0:T(8,128)(2,1)}, u32[]{:S(2)}) copy-start(bf16[4,96,1536]{2,1,0:T(8,128)(2,1)} %get-tuple-element.160) | copy-start | bytes 3538948
  202.2 29.2 %collective-permute-start.39 = (bf16[8,64,1792]{2,1,0:T(8,128)(2,1)}, bf16[8,64,1792]{2,1,0:T(8,128)(2,1)}, u32[]{:S(2)}, u32[]{:S(2)}) collective-permute-start(bf16[8,64,1792]{2,1,0:T(8,128)(2,1)} %add_convert_fusion), channel_id=1, source_target_pairs={{0,16},{1,9},{2,18},{3,11},{4,20},{5,13},{6,22},{7,15},{8,24},{9,1... | collective-permute-start | bytes 5505032 | tf_op jit(solution)/shard_map/ppermute | solution.py:574
  205.2 7.9 %copy-start.4 = (bf16[4,96,1536]{2,1,0:T(8,128)(2,1)}, bf16[4,96,1536]{2,1,0:T(8,128)(2,1)S(1)}, u32[]{:S(2)}) copy-start(bf16[4,96,1536]{2,1,0:T(8,128)(2,1)S(1)} %collective-permute-done.35) | copy-start | bytes 3538948
  205.3 7.7 %copy-start.24 = (bf16[64,2304]{1,0:T(8,128)(2,1)}, bf16[64,2304]{1,0:T(8,128)(2,1)S(1)}, u32[]{:S(2)}) copy-start(bf16[64,2304]{1,0:T(8,128)(2,1)S(1)} %collective-permute-done.34.refs_0_) | copy-start | bytes 884740
  213.1 13.9 %collective-permute-start.40 = (bf16[2,96,1536]{2,1,0:T(8,128)(2,1)}, bf16[2,96,1536]{2,1,0:T(8,128)(2,1)}, u32[]{:S(2)}, u32[]{:S(2)}) collective-permute-start(bf16[2,96,1536]{2,1,0:T(8,128)(2,1)} %add_convert_fusion.3), channel_id=1, source_target_pairs={{0,2},{1,3},{6,4},{7,5},{8,10},{9,11},{14,12},{15,13},{16,18},{17,... | collective-permute-start | bytes 1769480 | tf_op jit(solution)/shard_map/ppermute | solution.py:626
  218.7 15.8 %collective-permute-start.38 = (bf16[4,112,768]{2,1,0:T(8,128)(2,1)}, bf16[4,112,768]{2,1,0:T(8,128)(2,1)S(1)}, u32[]{:S(2)}, u32[]{:S(2)}) collective-permute-start(bf16[4,112,768]{2,1,0:T(8,128)(2,1)} %get-tuple-element.158), channel_id=1, source_target_pairs={{0,1},{1,0},{2,3},{3,2},{4,5},{5,4},{6,7},{7,6},{8,9},{9,8},{10,11... | collective-permute-start | bytes 2064392 | tf_op jit(solution)/shard_map/ppermute | solution.py:574
  228.4 11.5 %copy-start.3 = (bf16[4,96,1536]{2,1,0:T(8,128)(2,1)S(1)}, bf16[4,96,1536]{2,1,0:T(8,128)(2,1)}, u32[]{:S(2)}) copy-start(bf16[4,96,1536]{2,1,0:T(8,128)(2,1)} %get-tuple-element.160) | copy-start | bytes 3538948
  228.4 11.5 %copy-start.5 = (bf16[4,96,1536]{2,1,0:T(8,128)(2,1)S(1)}, bf16[4,96,1536]{2,1,0:T(8,128)(2,1)}, u32[]{:S(2)}) copy-start(bf16[4,96,1536]{2,1,0:T(8,128)(2,1)} %copy-done.4) | copy-start | bytes 3538948
  228.4 11.4 %collective-permute-start.42 = (bf16[2,96,1536]{2,1,0:T(8,128)(2,1)S(1)}, bf16[2,96,1536]{2,1,0:T(8,128)(2,1)S(1)}, u32[]{:S(2)}, u32[]{:S(2)}) collective-permute-start(bf16[2,96,1536]{2,1,0:T(8,128)(2,1)S(1)} %add_convert_fusion.2), channel_id=1, source_target_pairs={{2,4},{3,5},{4,2},{5,3},{10,12},{11,13},{12,10},{13,11},{18,20},{1... | collective-permute-start | bytes 1769480 | tf_op jit(solution)/shard_map/ppermute | solution.py:626
  233.2 15.2 %collective-permute-start.44 = (bf16[4,64,1792]{2,1,0:T(8,128)(2,1)S(1)}, bf16[4,64,1792]{2,1,0:T(8,128)(2,1)S(1)}, u32[]{:S(2)}, u32[]{:S(2)}) collective-permute-start(bf16[4,64,1792]{2,1,0:T(8,128)(2,1)S(1)} %add_convert_fusion.1), channel_id=1, source_target_pairs={{0,8},{1,17},{2,10},{3,19},{4,12},{5,21},{6,14},{7,23},{8,0},{9,25... | collective-permute-start | bytes 2752520 | tf_op jit(solution)/shard_map/ppermute | solution.py:574
  234.7 12.9 %collective-permute-start.41 = (bf16[2,112,768]{2,1,0:T(8,128)(2,1)S(1)}, bf16[2,112,768]{2,1,0:T(8,128)(2,1)S(1)}, u32[]{:S(2)}, u32[]{:S(2)}) collective-permute-start(bf16[2,112,768]{2,1,0:T(8,128)(2,1)S(1)} %add_convert_fusion.7), channel_id=1, source_target_pairs={{0,2},{1,3},{6,4},{7,5},{8,10},{9,11},{14,12},{15,13},{16,18},{17,... | collective-permute-start | bytes 1032200 | tf_op jit(solution)/shard_map/ppermute | solution.py:626
  240.2 12.5 %collective-permute-start.47 = (bf16[96,1536]{1,0:T(8,128)(2,1)S(1)}, bf16[96,1536]{1,0:T(8,128)(2,1)S(1)}, u32[]{:S(2)}, u32[]{:S(2)}) collective-permute-start(bf16[96,1536]{1,0:T(8,128)(2,1)S(1)} %fusion.3), channel_id=1, source_target_pairs={{0,2},{1,3},{2,0},{3,1},{4,6},{5,7},{6,4},{7,5},{8,10},{9,11},{10,... | collective-permute-start | bytes 884744 | tf_op jit(solution)/shard_map/ppermute | solution.py:574
  247.7 2.1 collective-permute-start.43
  252.7 15.2 %collective-permute-start.46 = (bf16[2,64,1792]{2,1,0:T(8,128)(2,1)S(1)}, bf16[2,64,1792]{2,1,0:T(8,128)(2,1)S(1)}, u32[]{:S(2)}, u32[]{:S(2)}) collective-permute-start(bf16[2,64,1792]{2,1,0:T(8,128)(2,1)S(1)} %add_convert_fusion.5), channel_id=1, source_target_pairs={{0,2},{1,3},{6,4},{7,5},{8,10},{9,11},{14,12},{15,13},{16,18},{17,... | collective-permute-start | bytes 1376264 | tf_op jit(solution)/shard_map/ppermute | solution.py:626
  259.6 10.1 %collective-permute-start.45 = (bf16[112,768]{1,0:T(8,128)(2,1)S(1)}, bf16[112,768]{1,0:T(8,128)(2,1)S(1)}, u32[]{:S(2)}, u32[]{:S(2)}) collective-permute-start(bf16[112,768]{1,0:T(8,128)(2,1)S(1)} %fusion.5), channel_id=1, source_target_pairs={{0,2},{1,3},{2,0},{3,1},{4,6},{5,7},{6,4},{7,5},{8,10},{9,11},{10,... | collective-permute-start | bytes 516104 | tf_op jit(solution)/shard_map/ppermute | solution.py:574
  270.9 1.8 collective-permute-start.48
  274.2 15.1 %collective-permute-start.49 = (bf16[64,1792]{1,0:T(8,128)(2,1)S(1)}, bf16[64,1792]{1,0:T(8,128)(2,1)S(1)}, u32[]{:S(2)}, u32[]{:S(2)}) collective-permute-start(bf16[64,1792]{1,0:T(8,128)(2,1)S(1)} %fusion.4), channel_id=1, source_target_pairs={{0,2},{1,3},{2,0},{3,1},{4,6},{5,7},{6,4},{7,5},{8,10},{9,11},{10,... | collective-permute-start | bytes 688136 | tf_op jit(solution)/shard_map/ppermute | solution.py:574
  (14 other events, 54.3 us)
Sparse Core Ops, SparseCore 0:
  11.5 88.5 all-gather.2

commit v2 on v1

--- a/solution.py
+++ b/solution.py
@@ -516,7 +516,7 @@
         out_specs=[pl.BlockSpec(memory_space=spaces[m]) for _, _, m in outs],
         scratch_shapes=scratch,
         compiler_params=pltpu.CompilerParams(vmem_limit_bytes=VMEM_BYTES),
-        cost_estimate=pl.CostEstimate(flops=micros * 10**9, bytes_accessed=micros * 10**6, transcendentals=0),
+        cost_estimate=pl.CostEstimate(flops=micros * 10**9 + 1, bytes_accessed=micros * 10**6 + 1, transcendentals=0),
     )(*operands)
 
 
@@ -775,7 +775,7 @@
         [((1, 49, 768), F32, "v")] + [((ENC_ROWS, 2304), BF, "v")] * SEC,
         [enc_sq, pltpu.VMEM((SEC, ENC_ROWS, 768), BF), pltpu.VMEM((SEC, 8, 2304), F32), dma],
         table, dh1, visible, a1, k1, z1, enc_vec, gv_ffn_e, gupb_e, gvec_d, gupb_d, *operands(att_e),
-        memory="s" + "v" * 10 + spaces(att_e),
+        memory="s" + "v" * 10 + spaces(att_e), micros=0,
     )
     step = Order()
     if fast:
@@ -790,7 +790,7 @@
         grad_blocks(ROWB, 96, 1536),
         [pltpu.VMEM((ROWB, 96, 768), BF), pltpu.VMEM((ROWB, 192, 384), BF), dma],
         table, sends_f[0], *came_f,
-        memory="svvvv",
+        memory="svvvv", micros=0,
     )
     if fast:
         swap_f = exchange(g_ffn_e[0], CORE)
@@ -804,7 +804,7 @@
         grad_blocks(ROWB, 112, 768),
         [pltpu.VMEM((ROWB, 112, 768), BF), pltpu.VMEM((16, 768), F32), dma],
         table, sends_a[0], *came_a,
-        memory="svvvv",
+        memory="svvvv", micros=0,
     )
     if fast:
         swap_x = exchange(g_att_e[0], CORE)

time: 300 us -> 317 us (1.057)
  waiting for transfers between devices: 129 us -> 143 us
  starting transfers between devices: 69.7 us -> 73.7 us
    ppermute x6, waiting for transfers between devices: 25 us -> 42.1 us  [to_section(): lax.ppermute(members[i], 'section', [(s, s ^ i) for s in range(SEC)])]
    ppermute x38, starting transfers between devices: 45.9 us -> 52.2 us  [exchange(): return lax.ppermute(value, ('section', 'dp'), pairs)]
    ppermute x6, waiting for transfers between devices: 14.9 us -> 8.97 us  [move(): return lax.ppermute(value, ('section', 'dp'), pairs)]
  transfers between devices with their start and end apart: 51 -> 51, of which waited for: 25 -> 21; matrix products, arithmetic and copies ran while one was open for 6% -> 6% of each run, Pallas kernels for 7% -> 6%
where the time goes in v2:
time: 317 us; the launch traced here: 316 us
  waiting for transfers between devices  143 us (45%)
  starting transfers between devices  73.7 us (23%)
  Pallas kernels  56.3 us (18%)
  other arithmetic  15.3 us (5%)
  between operations  14.6 us (5%)
  local copies, waits for them, and re-layouts  13.8 us (4%)
    ppermute x38, waiting for transfers between devices, exchange(): return lax.ppermute(value, ('section', 'dp'), pairs)  91.5 us
    pallas_call x7, Pallas kernels, call(): pl.pallas_call(body, out_shape=[jax.ShapeDtypeStruct(shape, dtype) for sh...  56.3 us
    ppermute x38, starting transfers between devices, exchange(): return lax.ppermute(value, ('section', 'dp'), pairs)  52.2 us
    ppermute x6, waiting for transfers between devices, to_section(): lax.ppermute(members[i], 'section', [(s, s ^ i) for s in range(SEC)])  42.1 us
    ppermute x6, starting transfers between devices, move(): return lax.ppermute(value, ('section', 'dp'), pairs)  14.5 us
    ppermute x6, waiting for transfers between devices, move(): return lax.ppermute(value, ('section', 'dp'), pairs)  8.97 us
    ppermute x6, starting transfers between devices, to_section(): lax.ppermute(members[i], 'section', [(s, s ^ i) for s in range(SEC)])  6.99 us
  transfers between devices with their start and end apart: 51, of which 21 were waited for; matrix products, arithmetic and copies ran while one was open for 6% of the time, Pallas kernels for 6%

profile of v2, /device:TPU:0, one launch (start us, length us, event | category | flops | bytes accessed | tf_op | source)
XLA Modules:
  0.0 316.2 jit_solution(12304002336100923677)
XLA Ops:
  7.2 1.9 copy.36.down_ref
  9.1 2.1 shard_map.315
  11.3 1.8 shard_map.314
  13.1 5.0 %collective-permute-start.2 = (bf16[1,112,768]{2,1,0:T(8,128)(2,1)}, bf16[1,112,768]{2,1,0:T(8,128)(2,1)S(1)}, u32[]{:S(2)}, u32[]{:S(2)}) collective-permute-start(bf16[1,112,768]{2,1,0:T(8,128)(2,1)} %bitcast.46), channel_id=1, source_target_pairs={{0,6},{1,7},{2,4},{3,5},{4,2},{5,3},{6,0},{7,1},{8,14},{9,15},{10,... | collective-permute-start | bytes 516104 | tf_op jit(solution)/shard_map/ppermute | solution.py:574
  18.8 4.9 %collective-permute-done.2 = bf16[1,112,768]{2,1,0:T(8,128)(2,1)S(1)} collective-permute-done((bf16[1,112,768]{2,1,0:T(8,128)(2,1)}, bf16[1,112,768]{2,1,0:T(8,128)(2,1)S(1)}, u32[]{:S(2)}, u32[]{:S(2)}) %collective-permute-start.2) | collective-permute-done | bytes 172064 | tf_op jit(solution)/shard_map/ppermute | solution.py:574
  23.7 14.2 %collective-permute-done.1 = bf16[1,112,768]{2,1,0:T(8,128)(2,1)S(1)} collective-permute-done((bf16[1,112,768]{2,1,0:T(8,128)(2,1)}, bf16[1,112,768]{2,1,0:T(8,128)(2,1)S(1)}, u32[]{:S(2)}, u32[]{:S(2)}) %collective-permute-start.1) | collective-permute-done | bytes 172064 | tf_op jit(solution)/shard_map/ppermute | solution.py:574
  37.8 1.0 pad_maximum_fusion.refs_0_
  38.9 1.6 collective-permute-start.3
  40.4 1.5 collective-permute-start.12
  41.9 2.5 collective-permute-start.6
  44.4 1.9 collective-permute-start.4
  46.3 6.7 %collective-permute-done.6 = bf16[1,96,768]{2,1,0:T(8,128)(2,1)S(1)} collective-permute-done((bf16[1,96,768]{2,1,0:T(8,128)(2,1)S(1)}, bf16[1,96,768]{2,1,0:T(8,128)(2,1)S(1)}, u32[]{:S(2)}, u32[]{:S(2)}) %collective-permute-start.6) | collective-permute-done | bytes 147488 | tf_op jit(solution)/shard_map/ppermute | solution.py:574
  53.0 12.1 %collective-permute-done.5 = bf16[1,96,768]{2,1,0:T(8,128)(2,1)S(1)} collective-permute-done((bf16[1,96,768]{2,1,0:T(8,128)(2,1)S(1)}, bf16[1,96,768]{2,1,0:T(8,128)(2,1)S(1)}, u32[]{:S(2)}, u32[]{:S(2)}) %collective-permute-start.5) | collective-permute-done | bytes 147488 | tf_op jit(solution)/shard_map/ppermute | solution.py:574
  65.4 1.9 collective-permute-start.11
  67.3 2.6 collective-permute-start.9
  69.9 2.8 collective-permute-done.11
  72.6 15.0 %collective-permute-done.10 = bf16[1,96,768]{2,1,0:T(8,128)(2,1)S(1)} collective-permute-done((bf16[1,96,768]{2,1,0:T(8,128)(2,1)S(1)}, bf16[1,96,768]{2,1,0:T(8,128)(2,1)S(1)}, u32[]{:S(2)}, u32[]{:S(2)}) %collective-permute-start.10) | collective-permute-done | bytes 147488 | tf_op jit(solution)/shard_map/ppermute | solution.py:574
  88.1 0.9 pad_maximum_fusion.2.refs_8_
  89.1 0.8 copy-done.17
  91.0 1.6 collective-permute-start.24
  93.0 1.3 collective-permute-start.18
  94.4 6.2 %shard_map.316 = (bf16[64,768]{1,0:T(8,128)(2,1)}, bf16[64,768]{1,0:T(8,128)(2,1)}, bf16[64,2304]{1,0:T(8,128)(2,1)}, bf16[64,768]{1,0:T(8,128)(2,1)}, f32[8,768...) custom-call(s32[105]{0:T(128)} %concatenate.24.table, bf16[1,49,768]{2,1,0:T(8,128)(2,1)} %x_ref.2, ...), custom_call_target="tpu_custom_call" | custom-call | flops 8000000000 | bytes 8000001 | tf_op jit(solution)/shard_map/pallas_call | solution.py:512
  100.5 5.9 %collective-permute-done.17.refs_2_ = bf16[4,96,768]{2,1,0:T(8,128)(2,1)} collective-permute-done((bf16[4,96,768]{2,1,0:T(8,128)(2,1)}, bf16[4,96,768]{2,1,0:T(8,128)(2,1)}, u32[]{:S(2)}, u32[]{:S(2)}) %collective-permute-start.17) | collective-permute-done | bytes 589856 | tf_op jit(solution)/shard_map/ppermute | solution.py:574
  106.4 2.8 collective-permute-done.22.refs_9_
  109.7 10.0 %collective-permute-done.18.refs_3_ = bf16[4,96,768]{2,1,0:T(8,128)(2,1)} collective-permute-done((bf16[4,96,768]{2,1,0:T(8,128)(2,1)}, bf16[4,96,768]{2,1,0:T(8,128)(2,1)}, u32[]{:S(2)}, u32[]{:S(2)}) %collective-permute-start.18) | collective-permute-done | bytes 589856 | tf_op jit(solution)/shard_map/ppermute | solution.py:574
  120.2 5.7 %collective-permute-done.25.refs_11_ = bf16[4,96,768]{2,1,0:T(8,128)(2,1)S(1)} collective-permute-done((bf16[4,96,768]{2,1,0:T(8,128)(2,1)}, bf16[4,96,768]{2,1,0:T(8,128)(2,1)S(1)}, u32[]{:S(2)}, u32[]{:S(2)}) %collective-permute-start.25) | collective-permute-done | bytes 589856 | tf_op jit(solution)/shard_map/ppermute | solution.py:574
  127.0 1.2 collective-permute-done.23.refs_7_
  128.1 2.5 collective-permute-done.21.refs_6_
  131.5 30.1 %shard_map.317 = (f32[1,196,512]{2,1,0:T(8,128)}, bf16[64,768]{1,0:T(8,128)(2,1)}, f32[3,768]{1,0:T(4,128)}, f32[1,3072]{1,0:T(1,128)}, f32[10,512]{1,0:T(8,128)...) custom-call(s32[105]{0:T(128)} %concatenate.24.table, ...), custom_call_target="tpu_custom_call" | custom-call | flops 8000000000 | bytes 8000001 | tf_op jit(solution)/shard_map/pallas_call | solution.py:512
  162.1 1.1 collective-permute-start.31
  163.2 2.1 collective-permute-start.30
  165.3 9.2 %shard_map.318 = (f32[1,49,768]{2,1,0:T(8,128)}, bf16[64,2304]{1,0:T(8,128)(2,1)}, bf16[64,2304]{1,0:T(8,128)(2,1)}, bf16[64,2304]{1,0:T(8,128)(2,1)}, bf16[64,2304]{1,0:T(8,128)(2,1)}) custom-call(s32[105]{0:T(128)} %concatenate.24.table, bf16[64,768]{1,0:T(8,128)(2,1)} %get-tuple-element.127.dh_ref, bf16[1,49,768]{2,1,0:T(8,128)(2,1)} %x_ref.2, ...), custom_call_target="tpu_custom_call" | custom-call | flops 1 | bytes 1 | tf_op jit(solution)/shard_map/pallas_call | solution.py:512
  174.5 4.5 %collective-permute-done.32.refs_0_ = bf16[64,4800]{1,0:T(8,128)(2,1)} collective-permute-done((bf16[64,4800]{1,0:T(8,128)(2,1)}, bf16[64,4800]{1,0:T(8,128)(2,1)}, u32[]{:S(2)}, u32[]{:S(2)}) %collective-permute-start.32) | collective-permute-done | bytes 614432 | tf_op jit(solution)/shard_map/ppermute | solution.py:767
  178.9 12.8 %collective-permute-done.31.refs_1_ = bf16[64,4800]{1,0:T(8,128)(2,1)} collective-permute-done((bf16[64,4800]{1,0:T(8,128)(2,1)}, bf16[64,4800]{1,0:T(8,128)(2,1)}, u32[]{:S(2)}, u32[]{:S(2)}) %collective-permute-start.31) | collective-permute-done | bytes 614432 | tf_op jit(solution)/shard_map/ppermute | solution.py:767
  191.8 3.7 %shard_map.319 = (bf16[4,96,1536]{2,1,0:T(8,128)(2,1)}, bf16[4,96,1536]{2,1,0:T(8,128)(2,1)}) custom-call(s32[105]{0:T(128)} %concatenate.24.table, bf16[64,4800]{1,0:T(8,128)(2,1)} %get-tuple-element.148.own_ref, bf16[64,4800]{1,0:T(8,128)(2,1)} %collective-permute-done.32.refs_0_, bf16[64,4800]{1,0:T(8,128)(2,1)} %collective-permute-done.31.refs_1_, ...), custom_call_target="tpu_custom_call" | custom-call | flops 1 | bytes 1 | tf_op jit(solution)/shard_map/pallas_call | solution.py:512
  195.6 3.4 %add_convert_fusion = bf16[8,64,1792]{2,1,0:T(8,128)(2,1)} fusion(bf16[16,64,1792]{2,1,0:T(8,128)(2,1)} %collective-permute-done.33, bf16[16,64,1792]{2,1,0:T(8,128)(2,1)S(1)} %copy-done), kind=kLoop, calls=%fused_computation | loop fusion | flops 3670016 | bytes 5505024 | tf_op jit(solution)/shard_map/convert_element_type | solution.py:784
  199.0 1.4 collective-permute-start.39
  200.4 1.1 add_convert_fusion.3
  201.7 2.1 collective-permute-start.40
  203.8 1.7 collective-permute-start.34
  206.1 1.2 collective-permute-start.37
  207.3 0.8 copy.38
  208.1 1.2 copy.37
  209.3 4.5 %collective-permute-done.34.refs_0_ = bf16[64,2304]{1,0:T(8,128)(2,1)S(1)} collective-permute-done((bf16[64,2304]{1,0:T(8,128)(2,1)S(1)}, bf16[64,2304]{1,0:T(8,128)(2,1)S(1)}, u32[]{:S(2)}, u32[]{:S(2)}) %collective-permute-start.34) | collective-permute-done | bytes 294944 | tf_op jit(solution)/shard_map/ppermute | solution.py:767
  213.8 20.3 %collective-permute-done.36.refs_1_ = bf16[64,2304]{1,0:T(8,128)(2,1)} collective-permute-done((bf16[64,2304]{1,0:T(8,128)(2,1)S(1)}, bf16[64,2304]{1,0:T(8,128)(2,1)}, u32[]{:S(2)}, u32[]{:S(2)}) %collective-permute-start.36) | collective-permute-done | bytes 294944 | tf_op jit(solution)/shard_map/ppermute | solution.py:767
  234.1 3.2 %shard_map.320 = (bf16[4,112,768]{2,1,0:T(8,128)(2,1)}, bf16[4,112,768]{2,1,0:T(8,128)(2,1)}) custom-call(s32[105]{0:T(128)} %concatenate.24.table, bf16[64,2304]{1,0:T(8,128)(2,1)} %get-tuple-element.145.own_ref, bf16[64,2304]{1,0:T(8,128)(2,1)} %copy-done.13, bf16[64,2304]{1,0:T(8,128)(2,1)} %collective-permute-done.36.refs_1_, ...), custom_call_target="tpu_custom_call" | custom-call | flops 1 | bytes 1 | tf_op jit(solution)/shard_map/pallas_call | solution.py:512
  237.2 1.4 collective-permute-start.38
  238.6 1.4 add_convert_fusion.2
  240.0 0.8 collective-permute-start.42
  240.9 1.8 add_convert_fusion.1
  242.7 1.6 collective-permute-start.44
  244.4 3.3 %collective-permute-start.41 = (bf16[2,112,768]{2,1,0:T(8,128)(2,1)S(1)}, bf16[2,112,768]{2,1,0:T(8,128)(2,1)S(1)}, u32[]{:S(2)}, u32[]{:S(2)}) collective-permute-start(bf16[2,112,768]{2,1,0:T(8,128)(2,1)S(1)} %add_convert_fusion.7), channel_id=1, source_target_pairs={{0,2},{1,3},{6,4},{7,5},{8,10},{9,11},{14,12},{15,13},{16,18},{17,... | collective-permute-start | bytes 1032200 | tf_op jit(solution)/shard_map/ppermute | solution.py:626
  248.0 10.4 %collective-permute-start.47 = (bf16[96,1536]{1,0:T(8,128)(2,1)S(1)}, bf16[96,1536]{1,0:T(8,128)(2,1)S(1)}, u32[]{:S(2)}, u32[]{:S(2)}) collective-permute-start(bf16[96,1536]{1,0:T(8,128)(2,1)S(1)} %fusion.3), channel_id=1, source_target_pairs={{0,2},{1,3},{2,0},{3,1},{4,6},{5,7},{6,4},{7,5},{8,10},{9,11},{10,... | collective-permute-start | bytes 884744 | tf_op jit(solution)/shard_map/ppermute | solution.py:574
  259.1 1.4 add_convert_fusion.5
  260.7 4.5 %collective-permute-done.47 = bf16[96,1536]{1,0:T(8,128)(2,1)S(1)} collective-permute-done((bf16[96,1536]{1,0:T(8,128)(2,1)S(1)}, bf16[96,1536]{1,0:T(8,128)(2,1)S(1)}, u32[]{:S(2)}, u32[]{:S(2)}) %collective-permute-start.47) | collective-permute-done | bytes 294944 | tf_op jit(solution)/shard_map/ppermute | solution.py:574
  265.3 6.9 %collective-permute-start.46 = (bf16[2,64,1792]{2,1,0:T(8,128)(2,1)S(1)}, bf16[2,64,1792]{2,1,0:T(8,128)(2,1)S(1)}, u32[]{:S(2)}, u32[]{:S(2)}) collective-permute-start(bf16[2,64,1792]{2,1,0:T(8,128)(2,1)S(1)} %add_convert_fusion.5), channel_id=1, source_target_pairs={{0,2},{1,3},{6,4},{7,5},{8,10},{9,11},{14,12},{15,13},{16,18},{17,... | collective-permute-start | bytes 1376264 | tf_op jit(solution)/shard_map/ppermute | solution.py:626
  272.3 0.7 slice.238
  273.0 0.7 maximum_bitcast_fusion
  273.8 9.0 %collective-permute-done.46 = bf16[2,64,1792]{2,1,0:T(8,128)(2,1)S(1)} collective-permute-done((bf16[2,64,1792]{2,1,0:T(8,128)(2,1)S(1)}, bf16[2,64,1792]{2,1,0:T(8,128)(2,1)S(1)}, u32[]{:S(2)}, u32[]{:S(2)}) %collective-permute-start.46) | collective-permute-done | bytes 458784 | tf_op jit(solution)/shard_map/ppermute | solution.py:626
  282.9 1.7 collective-permute-done.45
  287.5 1.5 convert_add_fusion.1
  289.0 13.0 %collective-permute-start.49 = (bf16[64,1792]{1,0:T(8,128)(2,1)S(1)}, bf16[64,1792]{1,0:T(8,128)(2,1)S(1)}, u32[]{:S(2)}, u32[]{:S(2)}) collective-permute-start(bf16[64,1792]{1,0:T(8,128)(2,1)S(1)} %fusion.4), channel_id=1, source_target_pairs={{0,2},{1,3},{2,0},{3,1},{4,6},{5,7},{6,4},{7,5},{8,10},{9,11},{10,... | collective-permute-start | bytes 688136 | tf_op jit(solution)/shard_map/ppermute | solution.py:574
  304.6 1.4 collective-permute-done.49
  308.0 0.8 copy.39
  (148 shorter events, 16.8 us)
Async XLA Ops:
  7.2 123.6 %all-gather.3.cloned.1.call-start = ((), (), s32[]{:S(2)}) async-start(), calls=%async_computation | async-start | bytes 7569408 | tf_op jit(solution)/shard_map/all_gather | solution.py:706
  11.3 30.7 %copy-start.16 = (bf16[96,768]{1,0:T(8,128)(2,1)S(1)}, bf16[96,768]{1,0:T(8,128)(2,1)}, u32[]{:S(2)}) copy-start(bf16[96,768]{1,0:T(8,128)(2,1)} %get-tuple-element.95) | copy-start | bytes 442372
  13.1 52.3 %copy-start.15 = (bf16[96,768]{1,0:T(8,128)(2,1)S(1)}, bf16[96,768]{1,0:T(8,128)(2,1)}, u32[]{:S(2)}) copy-start(bf16[96,768]{1,0:T(8,128)(2,1)} %get-tuple-element.101) | copy-start | bytes 442372
  13.1 10.6 %collective-permute-start.2 = (bf16[1,112,768]{2,1,0:T(8,128)(2,1)}, bf16[1,112,768]{2,1,0:T(8,128)(2,1)S(1)}, u32[]{:S(2)}, u32[]{:S(2)}) collective-permute-start(bf16[1,112,768]{2,1,0:T(8,128)(2,1)} %bitcast.46), channel_id=1, source_target_pairs={{0,6},{1,7},{2,4},{3,5},{4,2},{5,3},{6,0},{7,1},{8,14},{9,15},{10,... | collective-permute-start | bytes 516104 | tf_op jit(solution)/shard_map/ppermute | solution.py:574
  18.2 19.7 %collective-permute-start.1 = (bf16[1,112,768]{2,1,0:T(8,128)(2,1)}, bf16[1,112,768]{2,1,0:T(8,128)(2,1)S(1)}, u32[]{:S(2)}, u32[]{:S(2)}) collective-permute-start(bf16[1,112,768]{2,1,0:T(8,128)(2,1)} %bitcast.47), channel_id=1, source_target_pairs={{0,4},{1,5},{2,6},{3,7},{4,0},{5,1},{6,2},{7,3},{8,12},{9,13},{10,... | collective-permute-start | bytes 516104 | tf_op jit(solution)/shard_map/ppermute | solution.py:574
  18.2 19.7 %collective-permute-start = (bf16[1,112,768]{2,1,0:T(8,128)(2,1)}, bf16[1,112,768]{2,1,0:T(8,128)(2,1)S(1)}, u32[]{:S(2)}, u32[]{:S(2)}) collective-permute-start(bf16[1,112,768]{2,1,0:T(8,128)(2,1)} %bitcast.48), channel_id=1, source_target_pairs={{0,2},{1,3},{2,0},{3,1},{4,6},{5,7},{6,4},{7,5},{8,10},{9,11},{10,... | collective-permute-start | bytes 516104 | tf_op jit(solution)/shard_map/ppermute | solution.py:574
  38.9 55.5 %copy-start.1 = (bf16[4,112,768]{2,1,0:T(8,128)(2,1)}, bf16[4,112,768]{2,1,0:T(8,128)(2,1)S(1)}, u32[]{:S(2)}) copy-start(bf16[4,112,768]{2,1,0:T(8,128)(2,1)S(1)} %pad_maximum_fusion.refs_0_) | copy-start | bytes 2064388
  38.9 26.4 %collective-permute-start.3 = (bf16[4,112,768]{2,1,0:T(8,128)(2,1)S(1)}, bf16[4,112,768]{2,1,0:T(8,128)(2,1)S(1)}, u32[]{:S(2)}, u32[]{:S(2)}) collective-permute-start(bf16[4,112,768]{2,1,0:T(8,128)(2,1)S(1)} %pad_maximum_fusion.refs_0_), channel_id=1, source_target_pairs={{0,8},{1,17},{2,10},{3,19},{4,12},{5,21},{6,14},{7,23},{8,0},{9,25... | collective-permute-start | bytes 2064392 | tf_op jit(solution)/shard_map/ppermute | solution.py:574
  40.4 26.9 %collective-permute-start.12 = (bf16[4,112,768]{2,1,0:T(8,128)(2,1)S(1)}, bf16[4,112,768]{2,1,0:T(8,128)(2,1)S(1)}, u32[]{:S(2)}, u32[]{:S(2)}) collective-permute-start(bf16[4,112,768]{2,1,0:T(8,128)(2,1)S(1)} %pad_maximum_fusion.refs_0_), channel_id=1, source_target_pairs={{0,16},{1,9},{2,18},{3,11},{4,20},{5,13},{6,22},{7,15},{8,24},{9,1... | collective-permute-start | bytes 2064392 | tf_op jit(solution)/shard_map/ppermute | solution.py:574
  41.9 11.1 %collective-permute-start.6 = (bf16[1,96,768]{2,1,0:T(8,128)(2,1)S(1)}, bf16[1,96,768]{2,1,0:T(8,128)(2,1)S(1)}, u32[]{:S(2)}, u32[]{:S(2)}) collective-permute-start(bf16[1,96,768]{2,1,0:T(8,128)(2,1)S(1)} %bitcast.54), channel_id=1, source_target_pairs={{0,6},{1,7},{2,4},{3,5},{4,2},{5,3},{6,0},{7,1},{8,14},{9,15},{10,... | collective-permute-start | bytes 442376 | tf_op jit(solution)/shard_map/ppermute | solution.py:574
  44.4 20.7 %collective-permute-start.5 = (bf16[1,96,768]{2,1,0:T(8,128)(2,1)S(1)}, bf16[1,96,768]{2,1,0:T(8,128)(2,1)S(1)}, u32[]{:S(2)}, u32[]{:S(2)}) collective-permute-start(bf16[1,96,768]{2,1,0:T(8,128)(2,1)S(1)} %bitcast.55), channel_id=1, source_target_pairs={{0,4},{1,5},{2,6},{3,7},{4,0},{5,1},{6,2},{7,3},{8,12},{9,13},{10,... | collective-permute-start | bytes 442376 | tf_op jit(solution)/shard_map/ppermute | solution.py:574
  44.4 20.7 %collective-permute-start.4 = (bf16[1,96,768]{2,1,0:T(8,128)(2,1)S(1)}, bf16[1,96,768]{2,1,0:T(8,128)(2,1)S(1)}, u32[]{:S(2)}, u32[]{:S(2)}) collective-permute-start(bf16[1,96,768]{2,1,0:T(8,128)(2,1)S(1)} %bitcast.56), channel_id=1, source_target_pairs={{0,2},{1,3},{2,0},{3,1},{4,6},{5,7},{6,4},{7,5},{8,10},{9,11},{10,... | collective-permute-start | bytes 442376 | tf_op jit(solution)/shard_map/ppermute | solution.py:574
  65.2 23.8 %copy-start.11 = (bf16[4,96,768]{2,1,0:T(8,128)(2,1)}, bf16[4,96,768]{2,1,0:T(8,128)(2,1)S(1)}, u32[]{:S(2)}) copy-start(bf16[4,96,768]{2,1,0:T(8,128)(2,1)S(1)} %pad_maximum_fusion.1.refs_0_) | copy-start | bytes 1769476
  65.2 29.1 %copy-start.7 = (bf16[4,112,768]{2,1,0:T(8,128)(2,1)}, bf16[4,112,768]{2,1,0:T(8,128)(2,1)S(1)}, u32[]{:S(2)}) copy-start(bf16[4,112,768]{2,1,0:T(8,128)(2,1)S(1)} %collective-permute-done.3.refs_1_) | copy-start | bytes 2064388
  65.2 23.8 %collective-permute-start.7 = (bf16[4,112,768]{2,1,0:T(8,128)(2,1)S(1)}, bf16[4,112,768]{2,1,0:T(8,128)(2,1)S(1)}, u32[]{:S(2)}, u32[]{:S(2)}) collective-permute-start(bf16[4,112,768]{2,1,0:T(8,128)(2,1)S(1)} %collective-permute-done.3.refs_1_), channel_id=1, source_target_pairs={{0,16},{1,9},{2,18},{3,11},{4,20},{5,13},{6,22},{7,15},{8,24},{9,1... | collective-permute-start | bytes 2064392 | tf_op jit(solution)/shard_map/ppermute | solution.py:574
  65.3 23.7 %collective-permute-start.8 = (bf16[4,96,768]{2,1,0:T(8,128)(2,1)S(1)}, bf16[4,96,768]{2,1,0:T(8,128)(2,1)S(1)}, u32[]{:S(2)}, u32[]{:S(2)}) collective-permute-start(bf16[4,96,768]{2,1,0:T(8,128)(2,1)S(1)} %pad_maximum_fusion.1.refs_0_), channel_id=1, source_target_pairs={{0,8},{1,17},{2,10},{3,19},{4,12},{5,21},{6,14},{7,23},{8,0},{9,25... | collective-permute-start | bytes 1769480 | tf_op jit(solution)/shard_map/ppermute | solution.py:574
  65.4 7.2 %collective-permute-start.11 = (bf16[1,96,768]{2,1,0:T(8,128)(2,1)S(1)}, bf16[1,96,768]{2,1,0:T(8,128)(2,1)S(1)}, u32[]{:S(2)}, u32[]{:S(2)}) collective-permute-start(bf16[1,96,768]{2,1,0:T(8,128)(2,1)S(1)} %bitcast.50), channel_id=1, source_target_pairs={{0,6},{1,7},{2,4},{3,5},{4,2},{5,3},{6,0},{7,1},{8,14},{9,15},{10,... | collective-permute-start | bytes 442376 | tf_op jit(solution)/shard_map/ppermute | solution.py:574
  67.3 20.3 %collective-permute-start.10 = (bf16[1,96,768]{2,1,0:T(8,128)(2,1)S(1)}, bf16[1,96,768]{2,1,0:T(8,128)(2,1)S(1)}, u32[]{:S(2)}, u32[]{:S(2)}) collective-permute-start(bf16[1,96,768]{2,1,0:T(8,128)(2,1)S(1)} %bitcast.51), channel_id=1, source_target_pairs={{0,4},{1,5},{2,6},{3,7},{4,0},{5,1},{6,2},{7,3},{8,12},{9,13},{10,... | collective-permute-start | bytes 442376 | tf_op jit(solution)/shard_map/ppermute | solution.py:574
  67.3 27.1 %copy-start.8 = (bf16[4,112,768]{2,1,0:T(8,128)(2,1)}, bf16[4,112,768]{2,1,0:T(8,128)(2,1)S(1)}, u32[]{:S(2)}) copy-start(bf16[4,112,768]{2,1,0:T(8,128)(2,1)S(1)} %collective-permute-done.12.refs_2_) | copy-start | bytes 2064388
  67.3 20.3 %collective-permute-start.9 = (bf16[1,96,768]{2,1,0:T(8,128)(2,1)S(1)}, bf16[1,96,768]{2,1,0:T(8,128)(2,1)S(1)}, u32[]{:S(2)}, u32[]{:S(2)}) collective-permute-start(bf16[1,96,768]{2,1,0:T(8,128)(2,1)S(1)} %bitcast.52), channel_id=1, source_target_pairs={{0,2},{1,3},{2,0},{3,1},{4,6},{5,7},{6,4},{7,5},{8,10},{9,11},{10,... | collective-permute-start | bytes 442376 | tf_op jit(solution)/shard_map/ppermute | solution.py:574
  72.6 18.4 %collective-permute-start.13 = (bf16[4,112,768]{2,1,0:T(8,128)(2,1)S(1)}, bf16[4,112,768]{2,1,0:T(8,128)(2,1)S(1)}, u32[]{:S(2)}, u32[]{:S(2)}) collective-permute-start(bf16[4,112,768]{2,1,0:T(8,128)(2,1)S(1)} %pad_maximum_fusion.refs_0_), channel_id=1, source_target_pairs={{0,1},{1,0},{2,3},{3,2},{4,5},{5,4},{6,7},{7,6},{8,9},{9,8},{10,11... | collective-permute-start | bytes 2064392 | tf_op jit(solution)/shard_map/ppermute | solution.py:574
  87.6 5.1 %collective-permute-start.14 = (bf16[4,112,768]{2,1,0:T(8,128)(2,1)S(1)}, bf16[4,112,768]{2,1,0:T(8,128)(2,1)}, u32[]{:S(2)}, u32[]{:S(2)}) collective-permute-start(bf16[4,112,768]{2,1,0:T(8,128)(2,1)S(1)} %collective-permute-done.3.refs_1_), channel_id=1, source_target_pairs={{0,1},{1,0},{2,3},{3,2},{4,5},{5,4},{6,7},{7,6},{8,9},{9,8},{10,11... | collective-permute-start | bytes 2064392 | tf_op jit(solution)/shard_map/ppermute | solution.py:574
  87.6 3.4 %collective-permute-start.15 = (bf16[4,112,768]{2,1,0:T(8,128)(2,1)S(1)}, bf16[4,112,768]{2,1,0:T(8,128)(2,1)}, u32[]{:S(2)}, u32[]{:S(2)}) collective-permute-start(bf16[4,112,768]{2,1,0:T(8,128)(2,1)S(1)} %collective-permute-done.12.refs_2_), channel_id=1, source_target_pairs={{0,1},{1,0},{2,3},{3,2},{4,5},{5,4},{6,7},{7,6},{8,9},{9,8},{10,11... | collective-permute-start | bytes 2064392 | tf_op jit(solution)/shard_map/ppermute | solution.py:574
  89.1 3.9 %collective-permute-start.16 = (bf16[4,112,768]{2,1,0:T(8,128)(2,1)S(1)}, bf16[4,112,768]{2,1,0:T(8,128)(2,1)}, u32[]{:S(2)}, u32[]{:S(2)}) collective-permute-start(bf16[4,112,768]{2,1,0:T(8,128)(2,1)S(1)} %collective-permute-done.7.refs_3_), channel_id=1, source_target_pairs={{0,1},{1,0},{2,3},{3,2},{4,5},{5,4},{6,7},{7,6},{8,9},{9,8},{10,11... | collective-permute-start | bytes 2064392 | tf_op jit(solution)/shard_map/ppermute | solution.py:574
  90.5 15.9 %collective-permute-start.17 = (bf16[4,96,768]{2,1,0:T(8,128)(2,1)}, bf16[4,96,768]{2,1,0:T(8,128)(2,1)}, u32[]{:S(2)}, u32[]{:S(2)}) collective-permute-start(bf16[4,96,768]{2,1,0:T(8,128)(2,1)} %copy-done.11), channel_id=1, source_target_pairs={{0,16},{1,9},{2,18},{3,11},{4,20},{5,13},{6,22},{7,15},{8,24},{9,1... | collective-permute-start | bytes 1769480 | tf_op jit(solution)/shard_map/ppermute | solution.py:574
  91.0 34.9 %collective-permute-start.19 = (bf16[4,96,768]{2,1,0:T(8,128)(2,1)}, bf16[4,96,768]{2,1,0:T(8,128)(2,1)}, u32[]{:S(2)}, u32[]{:S(2)}) collective-permute-start(bf16[4,96,768]{2,1,0:T(8,128)(2,1)} %copy-done.11), channel_id=1, source_target_pairs={{0,1},{1,0},{2,3},{3,2},{4,5},{5,4},{6,7},{7,6},{8,9},{9,8},{10,11... | collective-permute-start | bytes 1769480 | tf_op jit(solution)/shard_map/ppermute | solution.py:574
  91.0 28.7 %collective-permute-start.24 = (bf16[4,96,768]{2,1,0:T(8,128)(2,1)}, bf16[4,96,768]{2,1,0:T(8,128)(2,1)}, u32[]{:S(2)}, u32[]{:S(2)}) collective-permute-start(bf16[4,96,768]{2,1,0:T(8,128)(2,1)} %pad_maximum_fusion.2.refs_8_), channel_id=1, source_target_pairs={{0,16},{1,9},{2,18},{3,11},{4,20},{5,13},{6,22},{7,15},{8,24},{9,1... | collective-permute-start | bytes 1769480 | tf_op jit(solution)/shard_map/ppermute | solution.py:574
  92.7 16.6 %collective-permute-start.22 = (bf16[4,96,768]{2,1,0:T(8,128)(2,1)}, bf16[4,96,768]{2,1,0:T(8,128)(2,1)}, u32[]{:S(2)}, u32[]{:S(2)}) collective-permute-start(bf16[4,96,768]{2,1,0:T(8,128)(2,1)} %pad_maximum_fusion.2.refs_8_), channel_id=1, source_target_pairs={{0,8},{1,17},{2,10},{3,19},{4,12},{5,21},{6,14},{7,23},{8,0},{9,25... | collective-permute-start | bytes 1769480 | tf_op jit(solution)/shard_map/ppermute | solution.py:574
  93.0 26.7 %collective-permute-start.18 = (bf16[4,96,768]{2,1,0:T(8,128)(2,1)}, bf16[4,96,768]{2,1,0:T(8,128)(2,1)}, u32[]{:S(2)}, u32[]{:S(2)}) collective-permute-start(bf16[4,96,768]{2,1,0:T(8,128)(2,1)} %copy-done.17), channel_id=1, source_target_pairs={{0,16},{1,9},{2,18},{3,11},{4,20},{5,13},{6,22},{7,15},{8,24},{9,1... | collective-permute-start | bytes 1769480 | tf_op jit(solution)/shard_map/ppermute | solution.py:574
  109.2 16.7 %collective-permute-start.25 = (bf16[4,96,768]{2,1,0:T(8,128)(2,1)}, bf16[4,96,768]{2,1,0:T(8,128)(2,1)S(1)}, u32[]{:S(2)}, u32[]{:S(2)}) collective-permute-start(bf16[4,96,768]{2,1,0:T(8,128)(2,1)} %collective-permute-done.22.refs_9_), channel_id=1, source_target_pairs={{0,16},{1,9},{2,18},{3,11},{4,20},{5,13},{6,22},{7,15},{8,24},{9,1... | collective-permute-start | bytes 1769480 | tf_op jit(solution)/shard_map/ppermute | solution.py:574
  119.7 6.7 %collective-permute-start.28 = (bf16[4,96,768]{2,1,0:T(8,128)(2,1)}, bf16[4,96,768]{2,1,0:T(8,128)(2,1)S(1)}, u32[]{:S(2)}, u32[]{:S(2)}) collective-permute-start(bf16[4,96,768]{2,1,0:T(8,128)(2,1)} %collective-permute-done.24.refs_10_), channel_id=1, source_target_pairs={{0,1},{1,0},{2,3},{3,2},{4,5},{5,4},{6,7},{7,6},{8,9},{9,8},{10,11... | collective-permute-start | bytes 1769480 | tf_op jit(solution)/shard_map/ppermute | solution.py:574
  119.7 6.8 %collective-permute-start.27 = (bf16[4,96,768]{2,1,0:T(8,128)(2,1)}, bf16[4,96,768]{2,1,0:T(8,128)(2,1)S(1)}, u32[]{:S(2)}, u32[]{:S(2)}) collective-permute-start(bf16[4,96,768]{2,1,0:T(8,128)(2,1)} %collective-permute-done.22.refs_9_), channel_id=1, source_target_pairs={{0,1},{1,0},{2,3},{3,2},{4,5},{5,4},{6,7},{7,6},{8,9},{9,8},{10,11... | collective-permute-start | bytes 1769480 | tf_op jit(solution)/shard_map/ppermute | solution.py:574
  120.2 6.7 %collective-permute-start.26 = (bf16[4,96,768]{2,1,0:T(8,128)(2,1)}, bf16[4,96,768]{2,1,0:T(8,128)(2,1)S(1)}, u32[]{:S(2)}, u32[]{:S(2)}) collective-permute-start(bf16[4,96,768]{2,1,0:T(8,128)(2,1)} %pad_maximum_fusion.2.refs_8_), channel_id=1, source_target_pairs={{0,1},{1,0},{2,3},{3,2},{4,5},{5,4},{6,7},{7,6},{8,9},{9,8},{10,11... | collective-permute-start | bytes 1769480 | tf_op jit(solution)/shard_map/ppermute | solution.py:574
  125.9 2.2 collective-permute-start.23
  125.9 4.7 %collective-permute-start.21 = (bf16[4,96,768]{2,1,0:T(8,128)(2,1)}, bf16[4,96,768]{2,1,0:T(8,128)(2,1)S(1)}, u32[]{:S(2)}, u32[]{:S(2)}) collective-permute-start(bf16[4,96,768]{2,1,0:T(8,128)(2,1)} %collective-permute-done.17.refs_2_), channel_id=1, source_target_pairs={{0,1},{1,0},{2,3},{3,2},{4,5},{5,4},{6,7},{7,6},{8,9},{9,8},{10,11... | collective-permute-start | bytes 1769480 | tf_op jit(solution)/shard_map/ppermute | solution.py:574
  126.4 4.4 %collective-permute-start.20 = (bf16[4,96,768]{2,1,0:T(8,128)(2,1)}, bf16[4,96,768]{2,1,0:T(8,128)(2,1)}, u32[]{:S(2)}, u32[]{:S(2)}) collective-permute-start(bf16[4,96,768]{2,1,0:T(8,128)(2,1)} %copy-done.17), channel_id=1, source_target_pairs={{0,1},{1,0},{2,3},{3,2},{4,5},{5,4},{6,7},{7,6},{8,9},{9,8},{10,11... | collective-permute-start | bytes 1769480 | tf_op jit(solution)/shard_map/ppermute | solution.py:574
  126.5 4.3 %collective-permute-start.29 = (bf16[4,96,768]{2,1,0:T(8,128)(2,1)S(1)}, bf16[4,96,768]{2,1,0:T(8,128)(2,1)}, u32[]{:S(2)}, u32[]{:S(2)}) collective-permute-start(bf16[4,96,768]{2,1,0:T(8,128)(2,1)S(1)} %collective-permute-done.25.refs_11_), channel_id=1, source_target_pairs={{0,1},{1,0},{2,3},{3,2},{4,5},{5,4},{6,7},{7,6},{8,9},{9,8},{10,11... | collective-permute-start | bytes 1769480 | tf_op jit(solution)/shard_map/ppermute | solution.py:574
  161.6 12.9 %collective-permute-start.33 = (bf16[16,64,1792]{2,1,0:T(8,128)(2,1)}, bf16[16,64,1792]{2,1,0:T(8,128)(2,1)}, u32[]{:S(2)}, u32[]{:S(2)}) collective-permute-start(bf16[16,64,1792]{2,1,0:T(8,128)(2,1)} %get-tuple-element.140), channel_id=1, source_target_pairs={{0,1},{1,0},{2,3},{3,2},{4,5},{5,4},{6,7},{7,6},{8,9},{9,8},{10,11... | collective-permute-start | bytes 11010056 | tf_op jit(solution)/shard_map/ppermute | solution.py:574
  161.8 17.2 %collective-permute-start.32 = (bf16[64,4800]{1,0:T(8,128)(2,1)}, bf16[64,4800]{1,0:T(8,128)(2,1)}, u32[]{:S(2)}, u32[]{:S(2)}) collective-permute-start(bf16[64,4800]{1,0:T(8,128)(2,1)} %get-tuple-element.139), channel_id=1, source_target_pairs={{0,8},{8,0},{16,24},{24,16},{1,9},{9,1},{17,25},{25,17},{2,10},{10... | collective-permute-start | bytes 1843208 | tf_op jit(solution)/shard_map/ppermute | solution.py:767
  162.1 29.7 %collective-permute-start.31 = (bf16[64,4800]{1,0:T(8,128)(2,1)}, bf16[64,4800]{1,0:T(8,128)(2,1)}, u32[]{:S(2)}, u32[]{:S(2)}) collective-permute-start(bf16[64,4800]{1,0:T(8,128)(2,1)} %get-tuple-element.138), channel_id=1, source_target_pairs={{0,16},{8,24},{16,0},{24,8},{1,17},{9,25},{17,1},{25,9},{2,18},{10... | collective-permute-start | bytes 1843208 | tf_op jit(solution)/shard_map/ppermute | solution.py:767
  163.2 28.6 %collective-permute-start.30 = (bf16[64,4800]{1,0:T(8,128)(2,1)}, bf16[64,4800]{1,0:T(8,128)(2,1)}, u32[]{:S(2)}, u32[]{:S(2)}) collective-permute-start(bf16[64,4800]{1,0:T(8,128)(2,1)} %get-tuple-element.137), channel_id=1, source_target_pairs={{0,24},{8,16},{16,8},{24,0},{1,25},{9,17},{17,9},{25,1},{2,26},{10... | collective-permute-start | bytes 1843208 | tf_op jit(solution)/shard_map/ppermute | solution.py:767
  165.3 30.3 %copy-start = (bf16[16,64,1792]{2,1,0:T(8,128)(2,1)S(1)}, bf16[16,64,1792]{2,1,0:T(8,128)(2,1)}, u32[]{:S(2)}) copy-start(bf16[16,64,1792]{2,1,0:T(8,128)(2,1)} %get-tuple-element.159) | copy-start | bytes 11010052
  195.5 4.9 %collective-permute-start.35 = (bf16[4,96,1536]{2,1,0:T(8,128)(2,1)}, bf16[4,96,1536]{2,1,0:T(8,128)(2,1)S(1)}, u32[]{:S(2)}, u32[]{:S(2)}) collective-permute-start(bf16[4,96,1536]{2,1,0:T(8,128)(2,1)} %get-tuple-element.149), channel_id=1, source_target_pairs={{0,1},{1,0},{2,3},{3,2},{4,5},{5,4},{6,7},{7,6},{8,9},{9,8},{10,11... | collective-permute-start | bytes 3538952 | tf_op jit(solution)/shard_map/ppermute | solution.py:574
  195.6 8.2 %copy-start.26 = (bf16[64,2304]{1,0:T(8,128)(2,1)S(1)}, bf16[64,2304]{1,0:T(8,128)(2,1)}, u32[]{:S(2)}) copy-start(bf16[64,2304]{1,0:T(8,128)(2,1)} %get-tuple-element.147) | copy-start | bytes 884740
  195.6 9.9 %copy-start.25 = (bf16[64,2304]{1,0:T(8,128)(2,1)S(1)}, bf16[64,2304]{1,0:T(8,128)(2,1)}, u32[]{:S(2)}) copy-start(bf16[64,2304]{1,0:T(8,128)(2,1)} %get-tuple-element.152) | copy-start | bytes 884740
  195.6 10.5 %copy-start.24 = (bf16[64,2304]{1,0:T(8,128)(2,1)S(1)}, bf16[64,2304]{1,0:T(8,128)(2,1)}, u32[]{:S(2)}) copy-start(bf16[64,2304]{1,0:T(8,128)(2,1)} %get-tuple-element.155) | copy-start | bytes 884740
  199.0 8.3 %copy-start.14 = (f32[1,49,768]{2,1,0:T(8,128)S(1)}, f32[1,49,768]{2,1,0:T(8,128)}, u32[]{:S(2)}) copy-start(f32[1,49,768]{2,1,0:T(8,128)} %get-tuple-element.172) | copy-start | bytes 451588
  199.0 9.1 %copy-start.12 = (f32[1,196,512]{2,1,0:T(8,128)S(1)}, f32[1,196,512]{2,1,0:T(8,128)}, u32[]{:S(2)}) copy-start(f32[1,196,512]{2,1,0:T(8,128)} %get-tuple-element.171) | copy-start | bytes 1204228
  199.0 41.8 %collective-permute-start.39 = (bf16[8,64,1792]{2,1,0:T(8,128)(2,1)}, bf16[8,64,1792]{2,1,0:T(8,128)(2,1)}, u32[]{:S(2)}, u32[]{:S(2)}) collective-permute-start(bf16[8,64,1792]{2,1,0:T(8,128)(2,1)} %add_convert_fusion), channel_id=1, source_target_pairs={{0,16},{1,9},{2,18},{3,11},{4,20},{5,13},{6,22},{7,15},{8,24},{9,1... | collective-permute-start | bytes 5505032 | tf_op jit(solution)/shard_map/ppermute | solution.py:574
  201.7 36.9 %collective-permute-start.40 = (bf16[2,96,1536]{2,1,0:T(8,128)(2,1)}, bf16[2,96,1536]{2,1,0:T(8,128)(2,1)}, u32[]{:S(2)}, u32[]{:S(2)}) collective-permute-start(bf16[2,96,1536]{2,1,0:T(8,128)(2,1)} %add_convert_fusion.3), channel_id=1, source_target_pairs={{0,2},{1,3},{6,4},{7,5},{8,10},{9,11},{14,12},{15,13},{16,18},{17,... | collective-permute-start | bytes 1769480 | tf_op jit(solution)/shard_map/ppermute | solution.py:626
  203.8 9.9 %collective-permute-start.34 = (bf16[64,2304]{1,0:T(8,128)(2,1)S(1)}, bf16[64,2304]{1,0:T(8,128)(2,1)S(1)}, u32[]{:S(2)}, u32[]{:S(2)}) collective-permute-start(bf16[64,2304]{1,0:T(8,128)(2,1)S(1)} %copy-done.26), channel_id=1, source_target_pairs={{0,8},{8,0},{16,24},{24,16},{1,9},{9,1},{17,25},{25,17},{2,10},{10... | collective-permute-start | bytes 884744 | tf_op jit(solution)/shard_map/ppermute | solution.py:767
  205.6 28.5 %collective-permute-start.36 = (bf16[64,2304]{1,0:T(8,128)(2,1)S(1)}, bf16[64,2304]{1,0:T(8,128)(2,1)}, u32[]{:S(2)}, u32[]{:S(2)}) collective-permute-start(bf16[64,2304]{1,0:T(8,128)(2,1)S(1)} %copy-done.25), channel_id=1, source_target_pairs={{0,16},{8,24},{16,0},{24,8},{1,17},{9,25},{17,1},{25,9},{2,18},{10... | collective-permute-start | bytes 884744 | tf_op jit(solution)/shard_map/ppermute | solution.py:767
  206.1 28.0 %collective-permute-start.37 = (bf16[64,2304]{1,0:T(8,128)(2,1)S(1)}, bf16[64,2304]{1,0:T(8,128)(2,1)}, u32[]{:S(2)}, u32[]{:S(2)}) collective-permute-start(bf16[64,2304]{1,0:T(8,128)(2,1)S(1)} %copy-done.24), channel_id=1, source_target_pairs={{0,24},{8,16},{16,8},{24,0},{1,25},{9,17},{17,9},{25,1},{2,26},{10... | collective-permute-start | bytes 884744 | tf_op jit(solution)/shard_map/ppermute | solution.py:767
  213.8 20.3 %copy-start.13 = (bf16[64,2304]{1,0:T(8,128)(2,1)}, bf16[64,2304]{1,0:T(8,128)(2,1)S(1)}, u32[]{:S(2)}) copy-start(bf16[64,2304]{1,0:T(8,128)(2,1)S(1)} %collective-permute-done.34.refs_0_) | copy-start | bytes 884740
  237.2 7.1 %collective-permute-start.38 = (bf16[4,112,768]{2,1,0:T(8,128)(2,1)}, bf16[4,112,768]{2,1,0:T(8,128)(2,1)S(1)}, u32[]{:S(2)}, u32[]{:S(2)}) collective-permute-start(bf16[4,112,768]{2,1,0:T(8,128)(2,1)} %get-tuple-element.158), channel_id=1, source_target_pairs={{0,1},{1,0},{2,3},{3,2},{4,5},{5,4},{6,7},{7,6},{8,9},{9,8},{10,11... | collective-permute-start | bytes 2064392 | tf_op jit(solution)/shard_map/ppermute | solution.py:574
  240.0 7.7 %collective-permute-start.42 = (bf16[2,96,1536]{2,1,0:T(8,128)(2,1)S(1)}, bf16[2,96,1536]{2,1,0:T(8,128)(2,1)S(1)}, u32[]{:S(2)}, u32[]{:S(2)}) collective-permute-start(bf16[2,96,1536]{2,1,0:T(8,128)(2,1)S(1)} %add_convert_fusion.2), channel_id=1, source_target_pairs={{2,4},{3,5},{4,2},{5,3},{10,12},{11,13},{12,10},{13,11},{18,20},{1... | collective-permute-start | bytes 1769480 | tf_op jit(solution)/shard_map/ppermute | solution.py:626
  242.7 16.4 %collective-permute-start.44 = (bf16[4,64,1792]{2,1,0:T(8,128)(2,1)S(1)}, bf16[4,64,1792]{2,1,0:T(8,128)(2,1)S(1)}, u32[]{:S(2)}, u32[]{:S(2)}) collective-permute-start(bf16[4,64,1792]{2,1,0:T(8,128)(2,1)S(1)} %add_convert_fusion.1), channel_id=1, source_target_pairs={{0,8},{1,17},{2,10},{3,19},{4,12},{5,21},{6,14},{7,23},{8,0},{9,25... | collective-permute-start | bytes 2752520 | tf_op jit(solution)/shard_map/ppermute | solution.py:574
  244.4 13.9 %collective-permute-start.41 = (bf16[2,112,768]{2,1,0:T(8,128)(2,1)S(1)}, bf16[2,112,768]{2,1,0:T(8,128)(2,1)S(1)}, u32[]{:S(2)}, u32[]{:S(2)}) collective-permute-start(bf16[2,112,768]{2,1,0:T(8,128)(2,1)S(1)} %add_convert_fusion.7), channel_id=1, source_target_pairs={{0,2},{1,3},{6,4},{7,5},{8,10},{9,11},{14,12},{15,13},{16,18},{17,... | collective-permute-start | bytes 1032200 | tf_op jit(solution)/shard_map/ppermute | solution.py:626
  248.0 17.3 %collective-permute-start.47 = (bf16[96,1536]{1,0:T(8,128)(2,1)S(1)}, bf16[96,1536]{1,0:T(8,128)(2,1)S(1)}, u32[]{:S(2)}, u32[]{:S(2)}) collective-permute-start(bf16[96,1536]{1,0:T(8,128)(2,1)S(1)} %fusion.3), channel_id=1, source_target_pairs={{0,2},{1,3},{2,0},{3,1},{4,6},{5,7},{6,4},{7,5},{8,10},{9,11},{10,... | collective-permute-start | bytes 884744 | tf_op jit(solution)/shard_map/ppermute | solution.py:574
  258.4 2.1 collective-permute-start.43
  265.3 17.4 %collective-permute-start.46 = (bf16[2,64,1792]{2,1,0:T(8,128)(2,1)S(1)}, bf16[2,64,1792]{2,1,0:T(8,128)(2,1)S(1)}, u32[]{:S(2)}, u32[]{:S(2)}) collective-permute-start(bf16[2,64,1792]{2,1,0:T(8,128)(2,1)S(1)} %add_convert_fusion.5), channel_id=1, source_target_pairs={{0,2},{1,3},{6,4},{7,5},{8,10},{9,11},{14,12},{15,13},{16,18},{17,... | collective-permute-start | bytes 1376264 | tf_op jit(solution)/shard_map/ppermute | solution.py:626
  272.2 12.4 %collective-permute-start.45 = (bf16[112,768]{1,0:T(8,128)(2,1)S(1)}, bf16[112,768]{1,0:T(8,128)(2,1)S(1)}, u32[]{:S(2)}, u32[]{:S(2)}) collective-permute-start(bf16[112,768]{1,0:T(8,128)(2,1)S(1)} %fusion.5), channel_id=1, source_target_pairs={{0,2},{1,3},{2,0},{3,1},{4,6},{5,7},{6,4},{7,5},{8,10},{9,11},{10,... | collective-permute-start | bytes 516104 | tf_op jit(solution)/shard_map/ppermute | solution.py:574
  285.7 1.8 collective-permute-start.48
  289.0 17.0 %collective-permute-start.49 = (bf16[64,1792]{1,0:T(8,128)(2,1)S(1)}, bf16[64,1792]{1,0:T(8,128)(2,1)S(1)}, u32[]{:S(2)}, u32[]{:S(2)}) collective-permute-start(bf16[64,1792]{1,0:T(8,128)(2,1)S(1)} %fusion.4), channel_id=1, source_target_pairs={{0,2},{1,3},{2,0},{3,1},{4,6},{5,7},{6,4},{7,5},{8,10},{9,11},{10,... | collective-permute-start | bytes 688136 | tf_op jit(solution)/shard_map/ppermute | solution.py:574
  (14 other events, 56.3 us)
Sparse Core Ops, SparseCore 0:
  11.5 88.5 all-gather.2
